TPU v7x, 128 devices: a whole 4x4x4 slice. The times are simulated.
128 devices in a mesh: layer: 16 (over x, z), tile: 8 (over y, core).
Axes of the slice: x: 4, y: 4, z: 4, core: 2. Of those that a mesh axis runs over, the one named last changes fastest.
Arguments:
- source_modes: bfloat16 [16, 8, 2, 64, 512], P('layer', None, None, 'tile'), may hold values from -6 to 6
- port_cells: int32 [8], replicated, may hold values from 0 to 511
- frequencies: float32 [2], replicated, may hold values from 0.3 to 1.5, as said below
- layer_inverse: bfloat16 [16, 2, 64, 512, 512], P('layer', None, 'tile'), may hold values from -0.092807765 to 1.6928078
- coupling_self: float32 [16, 2, 64, 512], P('layer', None, 'tile'), may hold values from 0.4 to 1
- coupling_curl: float32 [16, 2, 64, 512], P('layer', None, 'tile'), may hold values from -4 to 4
Outputs:
- snapshot_basis: float32 [16, 32, 2, 64, 512], P('layer', None, None, 'tile')
- triangle: float32 [32, 32], replicated
Inputs may be any that keep to these rules, and one draw needn't show every extreme that they name: `port_cells`: each port's profile is centred on this plane column. `frequencies`: the second frequency is 1.5 to 2.5 times the first.
All inputs are finite; a program needn't handle non-finite values.
Results may differ from a plain program's by a relative error of at most 0.04.
Values may be sent and summed in bfloat16 or wider, within the bound.
No kernel may reach another device: no remote copies, remote signals or barrier semaphores. Data moves between devices by JAX's collectives and lax.ppermute only.
A program may use at most 64 MiB of HBM per device.

v0:
```python
import jax
import jax.numpy as jnp
from jax import lax
from jax.sharding import PartitionSpec as P


def with_halo(cells, sides, width):
    for axis, dim in sides:
        count = lax.axis_size(axis)
        ends = count - 1
        head = lax.slice_in_dim(cells, 0, width, axis=dim)
        tail = lax.slice_in_dim(cells, cells.shape[dim] - width, cells.shape[dim], axis=dim)
        cells = jnp.concatenate(
            [
                lax.ppermute(tail, axis, [(i, (i + 1) % count) for i in range(ends)]),
                cells,
                lax.ppermute(head, axis, [((i + 1) % count, i) for i in range(ends)]),
            ],
            axis=dim,
        )
    return cells


def shifted(array, axis, by):
    size = lax.axis_size(axis)
    pairs = [(i, i + by) for i in range(size) if 0 <= i + by < size]
    return lax.ppermute(array, axis, pairs)


def lower_factor(gram):
    order = gram.shape[0]
    index_row = jnp.arange(order)

    def column_step(col_no, lower):
        unit = (index_row == col_no).astype(gram.dtype)
        column = jnp.dot(gram, unit, precision=lax.Precision.HIGHEST)
        lower_row = jnp.dot(unit, lower, precision=lax.Precision.HIGHEST)
        column = column - jnp.dot(lower, lower_row, precision=lax.Precision.HIGHEST)
        pivot = jnp.sqrt(jnp.sum(column * unit))
        scaled = jnp.where(index_row >= col_no, column / pivot, 0.0)
        return lower + scaled[:, None] * unit[None, :]

    return lax.fori_loop(0, order, column_step, jnp.zeros_like(gram))


def lower_inverse(lower):
    order = lower.shape[0]
    index_row = jnp.arange(order)

    def row_step(row_no, inverse):
        unit = (index_row == row_no).astype(lower.dtype)
        lower_row = jnp.dot(unit, lower, precision=lax.Precision.HIGHEST)
        pivot = jnp.sum(lower_row * unit)
        new_row = (unit - jnp.dot(lower_row, inverse, precision=lax.Precision.HIGHEST)) / pivot
        return inverse + unit[:, None] * new_row[None, :]

    return lax.fori_loop(0, order, row_step, jnp.zeros_like(lower))


def per_device(source_modes, port_cells, frequencies, layer_inverse, coupling_self, coupling_curl):
    layers_total = lax.axis_size("layer")
    tile_count = lax.axis_size("tile")
    layer_pos = lax.axis_index("layer")
    inverse_block = layer_inverse[0]
    self_w = coupling_self[0]
    curl_w = coupling_curl[0]
    rows_dev = source_modes.shape[3]
    plane_width = source_modes.shape[4]
    columns = jnp.arange(plane_width, dtype=jnp.float32)
    offsets = (columns[None, :] - port_cells.astype(jnp.float32)[:, None]) / (plane_width // 8)
    port_taper = 1.0 / (1.0 + offsets * offsets)
    phase_angle = frequencies * (layer_pos + 1).astype(jnp.float32)
    phase_pair = jnp.stack([jnp.cos(phase_angle), jnp.sin(phase_angle)], axis=1)
    source_layer = source_modes[0].astype(jnp.float32)
    forcing = (
        source_layer[:, None, None]
        * port_taper[:, None, None, None, None, :]
        * phase_pair[None, :, :, None, None, None]
    )
    forcing = forcing.reshape((-1, 2, rows_dev, plane_width))
    column_total = forcing.shape[0]
    group_count = 1
    group_width = column_total // group_count
    forcing_groups = forcing.reshape(group_count, group_width, 2, rows_dev, plane_width)
    step_count = layers_total + group_count - 1

    def couple(field):
        x_part = field[:, 0].astype(jnp.float32)
        y_part = field[:, 1].astype(jnp.float32)
        rim_rows = with_halo(y_part, (("tile", 1),), 1)
        row_diff = rim_rows[:, 2:] - rim_rows[:, :-2]
        cols_pad = jnp.pad(x_part, ((0, 0), (0, 0), (1, 1)))
        col_diff = cols_pad[:, :, 2:] - cols_pad[:, :, :-2]
        part_one = self_w[0] * x_part + curl_w[0] * row_diff
        part_two = self_w[1] * y_part + curl_w[1] * col_diff
        return jnp.stack([part_one, part_two], axis=1)

    def apply_inverse(vectors):
        return jnp.einsum(
            "crik,jcrk->jcri", inverse_block, vectors, preferred_element_type=jnp.float32
        )

    store_shape = (group_count, group_width, 2, rows_dev, plane_width)
    group_shape = (group_width, 2, rows_dev, plane_width)

    def down_step(step_no, state_pair):
        stored, incoming = state_pair
        group_no = jnp.clip(step_no - layer_pos, 0, group_count - 1)
        forcing_now = lax.dynamic_index_in_dim(forcing_groups, group_no, 0, keepdims=False)
        residue = (forcing_now - couple(incoming)).astype(jnp.bfloat16)
        current = apply_inverse(residue).astype(jnp.bfloat16)
        stored = lax.dynamic_update_index_in_dim(stored, current, group_no, 0)
        incoming = shifted(current, "layer", 1)
        return (stored, incoming)

    down_store, _ = lax.fori_loop(
        0,
        step_count,
        down_step,
        (jnp.zeros(store_shape, jnp.bfloat16), jnp.zeros(group_shape, jnp.bfloat16)),
    )
    reverse_pos = layers_total - 1 - layer_pos

    def up_step(step_no, state_pair):
        stored, incoming = state_pair
        group_no = jnp.clip(step_no - reverse_pos, 0, group_count - 1)
        earlier = lax.dynamic_index_in_dim(down_store, group_no, 0, keepdims=False)
        up_image = couple(incoming).astype(jnp.bfloat16)
        current = earlier.astype(jnp.float32) - apply_inverse(up_image)
        stored = lax.dynamic_update_index_in_dim(stored, current, group_no, 0)
        incoming = shifted(current, "layer", -1)
        return (stored, incoming)

    up_store, _ = lax.fori_loop(
        0,
        step_count,
        up_step,
        (jnp.zeros(store_shape, jnp.float32), jnp.zeros(group_shape, jnp.float32)),
    )
    columns_mat = up_store.reshape(column_total, -1)
    gram_local = jnp.dot(columns_mat, columns_mat.T, precision=lax.Precision.HIGHEST)
    total_rows = layers_total * tile_count * columns_mat.shape[1]
    gram_whole = lax.psum(gram_local, ("layer", "tile"))
    triangle = lower_factor(gram_whole / total_rows).T
    solved = jnp.dot(lower_inverse(triangle.T), columns_mat, precision=lax.Precision.HIGHEST)
    basis_out = solved.reshape(1, column_total, 2, rows_dev, plane_width)
    return (basis_out, triangle)


def solution(mesh):
    in_specs = (
        P("layer", None, None, "tile", None),
        P(),
        P(),
        P("layer", None, "tile", None, None),
        P("layer", None, "tile", None),
        P("layer", None, "tile", None),
    )
    out_specs = (P("layer", None, None, "tile", None), P())
    return jax.shard_map(
        per_device, mesh=mesh, in_specs=in_specs, out_specs=out_specs, check_vma=False
    )
```

profile of v0, /device:TPU:0, one launch (start us, length us, event | category | flops | bytes accessed | tf_op | source)
XLA Modules:
  0.0 1397.8 jit_solution(80407090975050226)
XLA Ops:
  3.3 532.2 %while.65 = (s32[]{:T(128)}, bf16[1,32,2,8,512]{4,1,3,2,0:T(8,128)(2,1)}, bf16[32,2,8,512]{3,0,2,1:T(8,128)(2,1)S(1)}, f32[2,8,512]{2,1,0:T(8,128)}, f32[2,8,512...) while((s32[]{:T(128)}, ...), condition=%wide.region_1.2_spmd.clone, body=%wide.region_0.1_spmd.clone.sunk | while | flops 271581184 | bytes 23921008 | solution.py:116
  23.1 10.3 collective-permute-done.5
  56.0 10.3 collective-permute-done.5
  88.5 10.3 collective-permute-done.5
  120.6 10.3 collective-permute-done.5
  152.6 10.3 collective-permute-done.5
  185.4 10.3 collective-permute-done.5
  220.0 10.3 collective-permute-done.5
  249.1 6.1 collective-permute-start.5
  255.3 10.3 collective-permute-done.5
  283.7 6.0 collective-permute-start.5
  289.7 10.3 collective-permute-done.5
  317.7 6.4 collective-permute-start.5
  324.1 10.3 collective-permute-done.5
  351.0 6.3 collective-permute-start.5
  357.3 10.4 collective-permute-done.5
  384.2 6.5 collective-permute-start.5
  390.8 10.7 collective-permute-done.5
  417.7 6.5 collective-permute-start.5
  424.3 10.7 collective-permute-done.5
  451.2 6.4 collective-permute-start.5
  457.7 10.3 collective-permute-done.5
  484.9 6.5 collective-permute-start.5
  491.5 10.3 collective-permute-done.5
  518.7 6.5 collective-permute-start.5
  525.3 10.3 collective-permute-done.5
  535.6 668.1 %while.64 = (s32[]{:T(128)}, f32[1,32,2,8,512]{4,1,3,2,0:T(8,128)}, f32[32,2,8,512]{3,0,2,1:T(8,128)S(1)}, bf16[1,32,2,8,512]{4,1,3,2,0:T(8,128)(2,1)}, f32[2,8,...) while((s32[]{:T(128)}, f32[1,32,2,8,512]{4,1,3,2,0:T(8,128)}, ...), condition=%wide.region_3.4_spmd, body=%wide.region_2.3_spmd.sunk | while | flops 270794752 | bytes 24707304 | solution.py:134
  551.0 26.9 %collective-permute-done.2 = f32[32,2,8,512]{3,0,2,1:T(8,128)S(1)} collective-permute-done((f32[32,2,8,512]{3,0,2,1:T(8,128)S(1)}, f32[32,2,8,512]{3,0,2,1:T(8,128)S(1)}, u32[]{:S(2)}, u32[]{:S(2)}) %collective-permute-start.2) | collective-permute-done | bytes 1048608 | tf_op jit(solution)/shard_map/while/body/eval_jaxpr/ppermute | solution.py:27
  586.6 6.0 fusion.97
  593.9 26.9 %collective-permute-done.2 = f32[32,2,8,512]{3,0,2,1:T(8,128)S(1)} collective-permute-done((f32[32,2,8,512]{3,0,2,1:T(8,128)S(1)}, f32[32,2,8,512]{3,0,2,1:T(8,128)S(1)}, u32[]{:S(2)}, u32[]{:S(2)}) %collective-permute-start.2) | collective-permute-done | bytes 1048608 | tf_op jit(solution)/shard_map/while/body/eval_jaxpr/ppermute | solution.py:27
  629.5 6.0 fusion.97
  636.8 26.9 %collective-permute-done.2 = f32[32,2,8,512]{3,0,2,1:T(8,128)S(1)} collective-permute-done((f32[32,2,8,512]{3,0,2,1:T(8,128)S(1)}, f32[32,2,8,512]{3,0,2,1:T(8,128)S(1)}, u32[]{:S(2)}, u32[]{:S(2)}) %collective-permute-start.2) | collective-permute-done | bytes 1048608 | tf_op jit(solution)/shard_map/while/body/eval_jaxpr/ppermute | solution.py:27
  679.1 26.9 %collective-permute-done.2 = f32[32,2,8,512]{3,0,2,1:T(8,128)S(1)} collective-permute-done((f32[32,2,8,512]{3,0,2,1:T(8,128)S(1)}, f32[32,2,8,512]{3,0,2,1:T(8,128)S(1)}, u32[]{:S(2)}, u32[]{:S(2)}) %collective-permute-start.2) | collective-permute-done | bytes 1048608 | tf_op jit(solution)/shard_map/while/body/eval_jaxpr/ppermute | solution.py:27
  721.2 26.1 %collective-permute-done.2 = f32[32,2,8,512]{3,0,2,1:T(8,128)S(1)} collective-permute-done((f32[32,2,8,512]{3,0,2,1:T(8,128)S(1)}, f32[32,2,8,512]{3,0,2,1:T(8,128)S(1)}, u32[]{:S(2)}, u32[]{:S(2)}) %collective-permute-start.2) | collective-permute-done | bytes 1048608 | tf_op jit(solution)/shard_map/while/body/eval_jaxpr/ppermute | solution.py:27
  762.3 26.4 %collective-permute-done.2 = f32[32,2,8,512]{3,0,2,1:T(8,128)S(1)} collective-permute-done((f32[32,2,8,512]{3,0,2,1:T(8,128)S(1)}, f32[32,2,8,512]{3,0,2,1:T(8,128)S(1)}, u32[]{:S(2)}, u32[]{:S(2)}) %collective-permute-start.2) | collective-permute-done | bytes 1048608 | tf_op jit(solution)/shard_map/while/body/eval_jaxpr/ppermute | solution.py:27
  803.5 26.9 %collective-permute-done.2 = f32[32,2,8,512]{3,0,2,1:T(8,128)S(1)} collective-permute-done((f32[32,2,8,512]{3,0,2,1:T(8,128)S(1)}, f32[32,2,8,512]{3,0,2,1:T(8,128)S(1)}, u32[]{:S(2)}, u32[]{:S(2)}) %collective-permute-start.2) | collective-permute-done | bytes 1048608 | tf_op jit(solution)/shard_map/while/body/eval_jaxpr/ppermute | solution.py:27
  845.0 26.9 %collective-permute-done.2 = f32[32,2,8,512]{3,0,2,1:T(8,128)S(1)} collective-permute-done((f32[32,2,8,512]{3,0,2,1:T(8,128)S(1)}, f32[32,2,8,512]{3,0,2,1:T(8,128)S(1)}, u32[]{:S(2)}, u32[]{:S(2)}) %collective-permute-start.2) | collective-permute-done | bytes 1048608 | tf_op jit(solution)/shard_map/while/body/eval_jaxpr/ppermute | solution.py:27
  886.4 26.9 %collective-permute-done.2 = f32[32,2,8,512]{3,0,2,1:T(8,128)S(1)} collective-permute-done((f32[32,2,8,512]{3,0,2,1:T(8,128)S(1)}, f32[32,2,8,512]{3,0,2,1:T(8,128)S(1)}, u32[]{:S(2)}, u32[]{:S(2)}) %collective-permute-start.2) | collective-permute-done | bytes 1048608 | tf_op jit(solution)/shard_map/while/body/eval_jaxpr/ppermute | solution.py:27
  927.9 26.9 %collective-permute-done.2 = f32[32,2,8,512]{3,0,2,1:T(8,128)S(1)} collective-permute-done((f32[32,2,8,512]{3,0,2,1:T(8,128)S(1)}, f32[32,2,8,512]{3,0,2,1:T(8,128)S(1)}, u32[]{:S(2)}, u32[]{:S(2)}) %collective-permute-start.2) | collective-permute-done | bytes 1048608 | tf_op jit(solution)/shard_map/while/body/eval_jaxpr/ppermute | solution.py:27
  969.4 26.9 %collective-permute-done.2 = f32[32,2,8,512]{3,0,2,1:T(8,128)S(1)} collective-permute-done((f32[32,2,8,512]{3,0,2,1:T(8,128)S(1)}, f32[32,2,8,512]{3,0,2,1:T(8,128)S(1)}, u32[]{:S(2)}, u32[]{:S(2)}) %collective-permute-start.2) | collective-permute-done | bytes 1048608 | tf_op jit(solution)/shard_map/while/body/eval_jaxpr/ppermute | solution.py:27
  1010.9 26.9 %collective-permute-done.2 = f32[32,2,8,512]{3,0,2,1:T(8,128)S(1)} collective-permute-done((f32[32,2,8,512]{3,0,2,1:T(8,128)S(1)}, f32[32,2,8,512]{3,0,2,1:T(8,128)S(1)}, u32[]{:S(2)}, u32[]{:S(2)}) %collective-permute-start.2) | collective-permute-done | bytes 1048608 | tf_op jit(solution)/shard_map/while/body/eval_jaxpr/ppermute | solution.py:27
  1052.4 26.9 %collective-permute-done.2 = f32[32,2,8,512]{3,0,2,1:T(8,128)S(1)} collective-permute-done((f32[32,2,8,512]{3,0,2,1:T(8,128)S(1)}, f32[32,2,8,512]{3,0,2,1:T(8,128)S(1)}, u32[]{:S(2)}, u32[]{:S(2)}) %collective-permute-start.2) | collective-permute-done | bytes 1048608 | tf_op jit(solution)/shard_map/while/body/eval_jaxpr/ppermute | solution.py:27
  1093.9 26.9 %collective-permute-done.2 = f32[32,2,8,512]{3,0,2,1:T(8,128)S(1)} collective-permute-done((f32[32,2,8,512]{3,0,2,1:T(8,128)S(1)}, f32[32,2,8,512]{3,0,2,1:T(8,128)S(1)}, u32[]{:S(2)}, u32[]{:S(2)}) %collective-permute-start.2) | collective-permute-done | bytes 1048608 | tf_op jit(solution)/shard_map/while/body/eval_jaxpr/ppermute | solution.py:27
  1135.4 26.9 %collective-permute-done.2 = f32[32,2,8,512]{3,0,2,1:T(8,128)S(1)} collective-permute-done((f32[32,2,8,512]{3,0,2,1:T(8,128)S(1)}, f32[32,2,8,512]{3,0,2,1:T(8,128)S(1)}, u32[]{:S(2)}, u32[]{:S(2)}) %collective-permute-start.2) | collective-permute-done | bytes 1048608 | tf_op jit(solution)/shard_map/while/body/eval_jaxpr/ppermute | solution.py:27
  1176.9 26.9 %collective-permute-done.2 = f32[32,2,8,512]{3,0,2,1:T(8,128)S(1)} collective-permute-done((f32[32,2,8,512]{3,0,2,1:T(8,128)S(1)}, f32[32,2,8,512]{3,0,2,1:T(8,128)S(1)}, u32[]{:S(2)}, u32[]{:S(2)}) %collective-permute-start.2) | collective-permute-done | bytes 1048608 | tf_op jit(solution)/shard_map/while/body/eval_jaxpr/ppermute | solution.py:27
  1206.4 74.7 %psum.7 = f32[32,32]{1,0:T(8,128)S(1)} all-reduce(f32[32,32]{1,0:T(8,128)S(1)} %convolution_bitcast_fusion.6), channel_id=1, replica_groups=mesh['layer'=16,'tile'=8] {'layer','tile'}, use_global_device_ids=true, to_apply=%region_4.5 | all-reduce | flops 1024 | bytes 8192 | tf_op jit(solution)/shard_map/psum | solution.py:143
  1281.0 58.8 %while.67 = (s32[]{:T(128)}, f32[32,32]{1,0:T(8,128)S(1)}, f32[32,32]{1,0:T(8,128)S(1)}, s32[]{:T(128)}, s32[]{:T(128)}) while((s32[]{:T(128)}, f32[32,32]{1,0:T(8,128)S(1)}, f32[32,32]{1,0:T(8,128)S(1)}, s32[]{:T(128)}, s32[]{:T(128)}) %tuple.174), condition=%wide.region_7.8_spmd.clone.clone, body=%wide.region_5.7_spmd.clone.clone.sunk | while | flops 42338 | bytes 21869 | solution.py:43
  1339.8 51.5 %while.66 = (s32[]{:T(128)}, f32[32,32]{1,0:T(8,128)S(1)}, f32[32,32]{1,0:T(8,128)S(1)}, s32[]{:T(128)}, s32[]{:T(128)}) while((s32[]{:T(128)}, f32[32,32]{1,0:T(8,128)S(1)}, f32[32,32]{1,0:T(8,128)S(1)}, s32[]{:T(128)}, s32[]{:T(128)}) %tuple.177), condition=%wide.region_10.11_spmd.clone, body=%wide.region_8.10_spmd.clone.sunk | while | flops 28994 | bytes 17244 | solution.py:57
  (747 shorter events, 634.3 us)
Async XLA Ops:
  19.2 14.1 %collective-permute-start.5 = (bf16[32,2,8,512]{3,0,2,1:T(8,128)(2,1)S(1)}, bf16[32,2,8,512]{3,0,2,1:T(8,128)(2,1)S(1)}, u32[]{:S(2)}, u32[]{:S(2)}) collective-permute-start(bf16[32,2,8,512]{3,0,2,1:T(8,128)(2,1)S(1)} %bitcast.184), channel_id=1, source_target_pairs={{0,8},{8,16},{16,24},{24,32},{32,40},{40,48},{48,56},{56,64},{64,7... | collective-permute-start | bytes 1572872 | tf_op jit(solution)/shard_map/while/body/eval_jaxpr/ppermute | solution.py:27
  34.9 7.2 collective-permute-start.3
  51.5 14.7 %collective-permute-start.5 = (bf16[32,2,8,512]{3,0,2,1:T(8,128)(2,1)S(1)}, bf16[32,2,8,512]{3,0,2,1:T(8,128)(2,1)S(1)}, u32[]{:S(2)}, u32[]{:S(2)}) collective-permute-start(bf16[32,2,8,512]{3,0,2,1:T(8,128)(2,1)S(1)} %bitcast.184), channel_id=1, source_target_pairs={{0,8},{8,16},{16,24},{24,32},{32,40},{40,48},{48,56},{56,64},{64,7... | collective-permute-start | bytes 1572872 | tf_op jit(solution)/shard_map/while/body/eval_jaxpr/ppermute | solution.py:27
  67.8 7.2 collective-permute-start.3
  84.1 14.7 %collective-permute-start.5 = (bf16[32,2,8,512]{3,0,2,1:T(8,128)(2,1)S(1)}, bf16[32,2,8,512]{3,0,2,1:T(8,128)(2,1)S(1)}, u32[]{:S(2)}, u32[]{:S(2)}) collective-permute-start(bf16[32,2,8,512]{3,0,2,1:T(8,128)(2,1)S(1)} %bitcast.184), channel_id=1, source_target_pairs={{0,8},{8,16},{16,24},{24,32},{32,40},{40,48},{48,56},{56,64},{64,7... | collective-permute-start | bytes 1572872 | tf_op jit(solution)/shard_map/while/body/eval_jaxpr/ppermute | solution.py:27
  100.3 7.2 collective-permute-start.3
  116.2 14.7 %collective-permute-start.5 = (bf16[32,2,8,512]{3,0,2,1:T(8,128)(2,1)S(1)}, bf16[32,2,8,512]{3,0,2,1:T(8,128)(2,1)S(1)}, u32[]{:S(2)}, u32[]{:S(2)}) collective-permute-start(bf16[32,2,8,512]{3,0,2,1:T(8,128)(2,1)S(1)} %bitcast.184), channel_id=1, source_target_pairs={{0,8},{8,16},{16,24},{24,32},{32,40},{40,48},{48,56},{56,64},{64,7... | collective-permute-start | bytes 1572872 | tf_op jit(solution)/shard_map/while/body/eval_jaxpr/ppermute | solution.py:27
  132.4 7.1 collective-permute-start.3
  148.1 14.7 %collective-permute-start.5 = (bf16[32,2,8,512]{3,0,2,1:T(8,128)(2,1)S(1)}, bf16[32,2,8,512]{3,0,2,1:T(8,128)(2,1)S(1)}, u32[]{:S(2)}, u32[]{:S(2)}) collective-permute-start(bf16[32,2,8,512]{3,0,2,1:T(8,128)(2,1)S(1)} %bitcast.184), channel_id=1, source_target_pairs={{0,8},{8,16},{16,24},{24,32},{32,40},{40,48},{48,56},{56,64},{64,7... | collective-permute-start | bytes 1572872 | tf_op jit(solution)/shard_map/while/body/eval_jaxpr/ppermute | solution.py:27
  164.4 7.2 collective-permute-start.3
  180.9 14.7 %collective-permute-start.5 = (bf16[32,2,8,512]{3,0,2,1:T(8,128)(2,1)S(1)}, bf16[32,2,8,512]{3,0,2,1:T(8,128)(2,1)S(1)}, u32[]{:S(2)}, u32[]{:S(2)}) collective-permute-start(bf16[32,2,8,512]{3,0,2,1:T(8,128)(2,1)S(1)} %bitcast.184), channel_id=1, source_target_pairs={{0,8},{8,16},{16,24},{24,32},{32,40},{40,48},{48,56},{56,64},{64,7... | collective-permute-start | bytes 1572872 | tf_op jit(solution)/shard_map/while/body/eval_jaxpr/ppermute | solution.py:27
  197.2 7.1 collective-permute-start.3
  214.3 16.0 %collective-permute-start.5 = (bf16[32,2,8,512]{3,0,2,1:T(8,128)(2,1)S(1)}, bf16[32,2,8,512]{3,0,2,1:T(8,128)(2,1)S(1)}, u32[]{:S(2)}, u32[]{:S(2)}) collective-permute-start(bf16[32,2,8,512]{3,0,2,1:T(8,128)(2,1)S(1)} %bitcast.184), channel_id=1, source_target_pairs={{0,8},{8,16},{16,24},{24,32},{32,40},{40,48},{48,56},{56,64},{64,7... | collective-permute-start | bytes 1572872 | tf_op jit(solution)/shard_map/while/body/eval_jaxpr/ppermute | solution.py:27
  231.9 7.2 collective-permute-start.3
  249.1 16.4 %collective-permute-start.5 = (bf16[32,2,8,512]{3,0,2,1:T(8,128)(2,1)S(1)}, bf16[32,2,8,512]{3,0,2,1:T(8,128)(2,1)S(1)}, u32[]{:S(2)}, u32[]{:S(2)}) collective-permute-start(bf16[32,2,8,512]{3,0,2,1:T(8,128)(2,1)S(1)} %bitcast.184), channel_id=1, source_target_pairs={{0,8},{8,16},{16,24},{24,32},{32,40},{40,48},{48,56},{56,64},{64,7... | collective-permute-start | bytes 1572872 | tf_op jit(solution)/shard_map/while/body/eval_jaxpr/ppermute | solution.py:27
  267.1 7.1 collective-permute-start.3
  283.7 16.3 %collective-permute-start.5 = (bf16[32,2,8,512]{3,0,2,1:T(8,128)(2,1)S(1)}, bf16[32,2,8,512]{3,0,2,1:T(8,128)(2,1)S(1)}, u32[]{:S(2)}, u32[]{:S(2)}) collective-permute-start(bf16[32,2,8,512]{3,0,2,1:T(8,128)(2,1)S(1)} %bitcast.184), channel_id=1, source_target_pairs={{0,8},{8,16},{16,24},{24,32},{32,40},{40,48},{48,56},{56,64},{64,7... | collective-permute-start | bytes 1572872 | tf_op jit(solution)/shard_map/while/body/eval_jaxpr/ppermute | solution.py:27
  301.6 7.2 collective-permute-start.3
  317.7 16.7 %collective-permute-start.5 = (bf16[32,2,8,512]{3,0,2,1:T(8,128)(2,1)S(1)}, bf16[32,2,8,512]{3,0,2,1:T(8,128)(2,1)S(1)}, u32[]{:S(2)}, u32[]{:S(2)}) collective-permute-start(bf16[32,2,8,512]{3,0,2,1:T(8,128)(2,1)S(1)} %bitcast.184), channel_id=1, source_target_pairs={{0,8},{8,16},{16,24},{24,32},{32,40},{40,48},{48,56},{56,64},{64,7... | collective-permute-start | bytes 1572872 | tf_op jit(solution)/shard_map/while/body/eval_jaxpr/ppermute | solution.py:27
  335.9 7.2 collective-permute-start.3
  351.0 16.7 %collective-permute-start.5 = (bf16[32,2,8,512]{3,0,2,1:T(8,128)(2,1)S(1)}, bf16[32,2,8,512]{3,0,2,1:T(8,128)(2,1)S(1)}, u32[]{:S(2)}, u32[]{:S(2)}) collective-permute-start(bf16[32,2,8,512]{3,0,2,1:T(8,128)(2,1)S(1)} %bitcast.184), channel_id=1, source_target_pairs={{0,8},{8,16},{16,24},{24,32},{32,40},{40,48},{48,56},{56,64},{64,7... | collective-permute-start | bytes 1572872 | tf_op jit(solution)/shard_map/while/body/eval_jaxpr/ppermute | solution.py:27
  369.3 7.0 collective-permute-start.3
  384.2 17.3 %collective-permute-start.5 = (bf16[32,2,8,512]{3,0,2,1:T(8,128)(2,1)S(1)}, bf16[32,2,8,512]{3,0,2,1:T(8,128)(2,1)S(1)}, u32[]{:S(2)}, u32[]{:S(2)}) collective-permute-start(bf16[32,2,8,512]{3,0,2,1:T(8,128)(2,1)S(1)} %bitcast.184), channel_id=1, source_target_pairs={{0,8},{8,16},{16,24},{24,32},{32,40},{40,48},{48,56},{56,64},{64,7... | collective-permute-start | bytes 1572872 | tf_op jit(solution)/shard_map/while/body/eval_jaxpr/ppermute | solution.py:27
  403.1 6.7 collective-permute-start.3
  417.7 17.2 %collective-permute-start.5 = (bf16[32,2,8,512]{3,0,2,1:T(8,128)(2,1)S(1)}, bf16[32,2,8,512]{3,0,2,1:T(8,128)(2,1)S(1)}, u32[]{:S(2)}, u32[]{:S(2)}) collective-permute-start(bf16[32,2,8,512]{3,0,2,1:T(8,128)(2,1)S(1)} %bitcast.184), channel_id=1, source_target_pairs={{0,8},{8,16},{16,24},{24,32},{32,40},{40,48},{48,56},{56,64},{64,7... | collective-permute-start | bytes 1572872 | tf_op jit(solution)/shard_map/while/body/eval_jaxpr/ppermute | solution.py:27
  436.5 6.7 collective-permute-start.3
  451.2 16.7 %collective-permute-start.5 = (bf16[32,2,8,512]{3,0,2,1:T(8,128)(2,1)S(1)}, bf16[32,2,8,512]{3,0,2,1:T(8,128)(2,1)S(1)}, u32[]{:S(2)}, u32[]{:S(2)}) collective-permute-start(bf16[32,2,8,512]{3,0,2,1:T(8,128)(2,1)S(1)} %bitcast.184), channel_id=1, source_target_pairs={{0,8},{8,16},{16,24},{24,32},{32,40},{40,48},{48,56},{56,64},{64,7... | collective-permute-start | bytes 1572872 | tf_op jit(solution)/shard_map/while/body/eval_jaxpr/ppermute | solution.py:27
  469.5 7.2 collective-permute-start.3
  484.9 16.8 %collective-permute-start.5 = (bf16[32,2,8,512]{3,0,2,1:T(8,128)(2,1)S(1)}, bf16[32,2,8,512]{3,0,2,1:T(8,128)(2,1)S(1)}, u32[]{:S(2)}, u32[]{:S(2)}) collective-permute-start(bf16[32,2,8,512]{3,0,2,1:T(8,128)(2,1)S(1)} %bitcast.184), channel_id=1, source_target_pairs={{0,8},{8,16},{16,24},{24,32},{32,40},{40,48},{48,56},{56,64},{64,7... | collective-permute-start | bytes 1572872 | tf_op jit(solution)/shard_map/while/body/eval_jaxpr/ppermute | solution.py:27
  503.3 7.2 collective-permute-start.3
  518.7 16.8 %collective-permute-start.5 = (bf16[32,2,8,512]{3,0,2,1:T(8,128)(2,1)S(1)}, bf16[32,2,8,512]{3,0,2,1:T(8,128)(2,1)S(1)}, u32[]{:S(2)}, u32[]{:S(2)}) collective-permute-start(bf16[32,2,8,512]{3,0,2,1:T(8,128)(2,1)S(1)} %bitcast.184), channel_id=1, source_target_pairs={{0,8},{8,16},{16,24},{24,32},{32,40},{40,48},{48,56},{56,64},{64,7... | collective-permute-start | bytes 1572872 | tf_op jit(solution)/shard_map/while/body/eval_jaxpr/ppermute | solution.py:27
  549.7 28.2 %collective-permute-start.2 = (f32[32,2,8,512]{3,0,2,1:T(8,128)S(1)}, f32[32,2,8,512]{3,0,2,1:T(8,128)S(1)}, u32[]{:S(2)}, u32[]{:S(2)}) collective-permute-start(f32[32,2,8,512]{3,0,2,1:T(8,128)S(1)} %fusion.97), channel_id=1, source_target_pairs={{8,0},{16,8},{24,16},{32,24},{40,32},{48,40},{56,48},{64,56},{72,6... | collective-permute-start | bytes 3145736 | tf_op jit(solution)/shard_map/while/body/eval_jaxpr/ppermute | solution.py:27
  578.0 6.1 collective-permute-start
  592.6 28.2 %collective-permute-start.2 = (f32[32,2,8,512]{3,0,2,1:T(8,128)S(1)}, f32[32,2,8,512]{3,0,2,1:T(8,128)S(1)}, u32[]{:S(2)}, u32[]{:S(2)}) collective-permute-start(f32[32,2,8,512]{3,0,2,1:T(8,128)S(1)} %fusion.97), channel_id=1, source_target_pairs={{8,0},{16,8},{24,16},{32,24},{40,32},{48,40},{56,48},{64,56},{72,6... | collective-permute-start | bytes 3145736 | tf_op jit(solution)/shard_map/while/body/eval_jaxpr/ppermute | solution.py:27
  635.5 28.2 %collective-permute-start.2 = (f32[32,2,8,512]{3,0,2,1:T(8,128)S(1)}, f32[32,2,8,512]{3,0,2,1:T(8,128)S(1)}, u32[]{:S(2)}, u32[]{:S(2)}) collective-permute-start(f32[32,2,8,512]{3,0,2,1:T(8,128)S(1)} %fusion.97), channel_id=1, source_target_pairs={{8,0},{16,8},{24,16},{32,24},{40,32},{48,40},{56,48},{64,56},{72,6... | collective-permute-start | bytes 3145736 | tf_op jit(solution)/shard_map/while/body/eval_jaxpr/ppermute | solution.py:27
  677.8 28.2 %collective-permute-start.2 = (f32[32,2,8,512]{3,0,2,1:T(8,128)S(1)}, f32[32,2,8,512]{3,0,2,1:T(8,128)S(1)}, u32[]{:S(2)}, u32[]{:S(2)}) collective-permute-start(f32[32,2,8,512]{3,0,2,1:T(8,128)S(1)} %fusion.97), channel_id=1, source_target_pairs={{8,0},{16,8},{24,16},{32,24},{40,32},{48,40},{56,48},{64,56},{72,6... | collective-permute-start | bytes 3145736 | tf_op jit(solution)/shard_map/while/body/eval_jaxpr/ppermute | solution.py:27
  719.9 27.4 %collective-permute-start.2 = (f32[32,2,8,512]{3,0,2,1:T(8,128)S(1)}, f32[32,2,8,512]{3,0,2,1:T(8,128)S(1)}, u32[]{:S(2)}, u32[]{:S(2)}) collective-permute-start(f32[32,2,8,512]{3,0,2,1:T(8,128)S(1)} %fusion.97), channel_id=1, source_target_pairs={{8,0},{16,8},{24,16},{32,24},{40,32},{48,40},{56,48},{64,56},{72,6... | collective-permute-start | bytes 3145736 | tf_op jit(solution)/shard_map/while/body/eval_jaxpr/ppermute | solution.py:27
  761.0 27.7 %collective-permute-start.2 = (f32[32,2,8,512]{3,0,2,1:T(8,128)S(1)}, f32[32,2,8,512]{3,0,2,1:T(8,128)S(1)}, u32[]{:S(2)}, u32[]{:S(2)}) collective-permute-start(f32[32,2,8,512]{3,0,2,1:T(8,128)S(1)} %fusion.97), channel_id=1, source_target_pairs={{8,0},{16,8},{24,16},{32,24},{40,32},{48,40},{56,48},{64,56},{72,6... | collective-permute-start | bytes 3145736 | tf_op jit(solution)/shard_map/while/body/eval_jaxpr/ppermute | solution.py:27
  802.2 28.2 %collective-permute-start.2 = (f32[32,2,8,512]{3,0,2,1:T(8,128)S(1)}, f32[32,2,8,512]{3,0,2,1:T(8,128)S(1)}, u32[]{:S(2)}, u32[]{:S(2)}) collective-permute-start(f32[32,2,8,512]{3,0,2,1:T(8,128)S(1)} %fusion.97), channel_id=1, source_target_pairs={{8,0},{16,8},{24,16},{32,24},{40,32},{48,40},{56,48},{64,56},{72,6... | collective-permute-start | bytes 3145736 | tf_op jit(solution)/shard_map/while/body/eval_jaxpr/ppermute | solution.py:27
  843.7 28.2 %collective-permute-start.2 = (f32[32,2,8,512]{3,0,2,1:T(8,128)S(1)}, f32[32,2,8,512]{3,0,2,1:T(8,128)S(1)}, u32[]{:S(2)}, u32[]{:S(2)}) collective-permute-start(f32[32,2,8,512]{3,0,2,1:T(8,128)S(1)} %fusion.97), channel_id=1, source_target_pairs={{8,0},{16,8},{24,16},{32,24},{40,32},{48,40},{56,48},{64,56},{72,6... | collective-permute-start | bytes 3145736 | tf_op jit(solution)/shard_map/while/body/eval_jaxpr/ppermute | solution.py:27
  885.1 28.2 %collective-permute-start.2 = (f32[32,2,8,512]{3,0,2,1:T(8,128)S(1)}, f32[32,2,8,512]{3,0,2,1:T(8,128)S(1)}, u32[]{:S(2)}, u32[]{:S(2)}) collective-permute-start(f32[32,2,8,512]{3,0,2,1:T(8,128)S(1)} %fusion.97), channel_id=1, source_target_pairs={{8,0},{16,8},{24,16},{32,24},{40,32},{48,40},{56,48},{64,56},{72,6... | collective-permute-start | bytes 3145736 | tf_op jit(solution)/shard_map/while/body/eval_jaxpr/ppermute | solution.py:27
  926.6 28.2 %collective-permute-start.2 = (f32[32,2,8,512]{3,0,2,1:T(8,128)S(1)}, f32[32,2,8,512]{3,0,2,1:T(8,128)S(1)}, u32[]{:S(2)}, u32[]{:S(2)}) collective-permute-start(f32[32,2,8,512]{3,0,2,1:T(8,128)S(1)} %fusion.97), channel_id=1, source_target_pairs={{8,0},{16,8},{24,16},{32,24},{40,32},{48,40},{56,48},{64,56},{72,6... | collective-permute-start | bytes 3145736 | tf_op jit(solution)/shard_map/while/body/eval_jaxpr/ppermute | solution.py:27
  968.1 28.2 %collective-permute-start.2 = (f32[32,2,8,512]{3,0,2,1:T(8,128)S(1)}, f32[32,2,8,512]{3,0,2,1:T(8,128)S(1)}, u32[]{:S(2)}, u32[]{:S(2)}) collective-permute-start(f32[32,2,8,512]{3,0,2,1:T(8,128)S(1)} %fusion.97), channel_id=1, source_target_pairs={{8,0},{16,8},{24,16},{32,24},{40,32},{48,40},{56,48},{64,56},{72,6... | collective-permute-start | bytes 3145736 | tf_op jit(solution)/shard_map/while/body/eval_jaxpr/ppermute | solution.py:27
  1009.6 28.2 %collective-permute-start.2 = (f32[32,2,8,512]{3,0,2,1:T(8,128)S(1)}, f32[32,2,8,512]{3,0,2,1:T(8,128)S(1)}, u32[]{:S(2)}, u32[]{:S(2)}) collective-permute-start(f32[32,2,8,512]{3,0,2,1:T(8,128)S(1)} %fusion.97), channel_id=1, source_target_pairs={{8,0},{16,8},{24,16},{32,24},{40,32},{48,40},{56,48},{64,56},{72,6... | collective-permute-start | bytes 3145736 | tf_op jit(solution)/shard_map/while/body/eval_jaxpr/ppermute | solution.py:27
  1051.1 28.2 %collective-permute-start.2 = (f32[32,2,8,512]{3,0,2,1:T(8,128)S(1)}, f32[32,2,8,512]{3,0,2,1:T(8,128)S(1)}, u32[]{:S(2)}, u32[]{:S(2)}) collective-permute-start(f32[32,2,8,512]{3,0,2,1:T(8,128)S(1)} %fusion.97), channel_id=1, source_target_pairs={{8,0},{16,8},{24,16},{32,24},{40,32},{48,40},{56,48},{64,56},{72,6... | collective-permute-start | bytes 3145736 | tf_op jit(solution)/shard_map/while/body/eval_jaxpr/ppermute | solution.py:27
  1092.6 28.2 %collective-permute-start.2 = (f32[32,2,8,512]{3,0,2,1:T(8,128)S(1)}, f32[32,2,8,512]{3,0,2,1:T(8,128)S(1)}, u32[]{:S(2)}, u32[]{:S(2)}) collective-permute-start(f32[32,2,8,512]{3,0,2,1:T(8,128)S(1)} %fusion.97), channel_id=1, source_target_pairs={{8,0},{16,8},{24,16},{32,24},{40,32},{48,40},{56,48},{64,56},{72,6... | collective-permute-start | bytes 3145736 | tf_op jit(solution)/shard_map/while/body/eval_jaxpr/ppermute | solution.py:27
  1134.1 28.2 %collective-permute-start.2 = (f32[32,2,8,512]{3,0,2,1:T(8,128)S(1)}, f32[32,2,8,512]{3,0,2,1:T(8,128)S(1)}, u32[]{:S(2)}, u32[]{:S(2)}) collective-permute-start(f32[32,2,8,512]{3,0,2,1:T(8,128)S(1)} %fusion.97), channel_id=1, source_target_pairs={{8,0},{16,8},{24,16},{32,24},{40,32},{48,40},{56,48},{64,56},{72,6... | collective-permute-start | bytes 3145736 | tf_op jit(solution)/shard_map/while/body/eval_jaxpr/ppermute | solution.py:27
  1175.6 28.2 %collective-permute-start.2 = (f32[32,2,8,512]{3,0,2,1:T(8,128)S(1)}, f32[32,2,8,512]{3,0,2,1:T(8,128)S(1)}, u32[]{:S(2)}, u32[]{:S(2)}) collective-permute-start(f32[32,2,8,512]{3,0,2,1:T(8,128)S(1)} %fusion.97), channel_id=1, source_target_pairs={{8,0},{16,8},{24,16},{32,24},{40,32},{48,40},{56,48},{64,56},{72,6... | collective-permute-start | bytes 3145736 | tf_op jit(solution)/shard_map/while/body/eval_jaxpr/ppermute | solution.py:27
  (80 other events, 920.1 us)
where the time goes:
time: 1410 us; the launch traced here: 1400 us
  waiting for transfers between devices  634 us (45%)
  matrix products  277 us (20%)
  starting transfers between devices  272 us (19%)
  blocking collectives  74.7 us (5%)
  local copies, waits for them, and re-layouts  59.2 us (4%)
  other arithmetic  56 us (4%)
  loops' own time  24.6 us (2%)
    ppermute x32, waiting for transfers between devices, shifted(): return lax.ppermute(array, axis, pairs)  594 us
    dot_general x32, matrix products, apply_inverse(): jnp.einsum('crik,jcrk->jcri', inverse_block, vectors, preferred_element_t...  190 us
    ppermute x32, starting transfers between devices, with_halo(): lax.ppermute(tail, axis, [(i, (i + 1) % count) for i in range(ends)])  120 us
    ppermute x32, starting transfers between devices, shifted(): return lax.ppermute(array, axis, pairs)  110 us
    psum x1, blocking collectives, per_device(): gram_whole = lax.psum(gram_local, ('layer', 'tile'))  74.7 us
    ppermute x32, starting transfers between devices, with_halo(): lax.ppermute(head, axis, [((i + 1) % count, i) for i in range(ends)])  41.3 us
    ppermute x32, waiting for transfers between devices, with_halo(): lax.ppermute(head, axis, [((i + 1) % count, i) for i in range(ends)])  39.9 us
    another operation x32, other arithmetic, couple(): return jnp.stack([part_one, part_two], axis=1)  33.5 us
  transfers between devices with their start and end apart: 96, of which 64 were waited for; matrix products, arithmetic and copies ran while one was open for 3% of the time, Pallas kernels for 0%

commit v1 on v0

v1 whole, which is shorter than its diff:
```python
import functools

import jax
import jax.numpy as jnp
from jax import lax
from jax.experimental import pallas as pl
from jax.experimental.pallas import tpu as pltpu
from jax.sharding import PartitionSpec as P

AXES = ("layer", "tile")
BF16 = jnp.bfloat16
F32 = jnp.float32
NL = 16
NY = 4
W = 512
NJ = 32
EXTRA = 16
BLOCK = W + EXTRA
VMEM = pl.BlockSpec(memory_space=pltpu.VMEM)
SMEM = pl.BlockSpec(memory_space=pltpu.SMEM)
ANY = pl.BlockSpec(memory_space=pl.ANY)
PARAMS = pltpu.CompilerParams(vmem_limit_bytes=24 * 1024 * 1024)


def spot(row, y):
    rank = row + (y % 2) * (NL - 1 - 2 * row)
    x, z = rank // 4, rank % 4
    return 4 * x + z + (x % 2) * (3 - 2 * z)


def device_of(row, comp):
    y = row // NL
    return spot(row % NL, y) * 2 * NY + 2 * y + comp


ROWS = NL * NY
CORE = [(device_of(r, c), device_of(r, 1 - c)) for r in range(ROWS) for c in range(2)]
RAISE = [(device_of(r, c), device_of((r + 1) % ROWS, 1 - c)) for r in range(ROWS) for c in range(2)]
LOWER = [(device_of(r, c), device_of((r - 1) % ROWS, 1 - c)) for r in range(ROWS) for c in range(2)]


def swap(value, pairs):
    return lax.ppermute(value, AXES, pairs)


def exchanges():
    rounds = [[(d, d ^ 1) for d in range(128)]]
    for bit in (1, 3, 5):
        size = 1 << bit
        for odd in (0, 1):
            pairs = []
            for d in range(128):
                at = (d // size) % 4
                to = at ^ 1 if odd == 0 else (at + 1 if at % 2 else at - 1) % 4
                pairs.append((d, d + (to - at) * size))
            rounds.append(pairs)
    return rounds


def pack_send(place, blocks, extras, out):
    out[0, 0:W, :] = blocks[0, 0, 0]
    out[0, W:BLOCK, :] = extras[0, 0]


def pack_other(place, received, part, out):
    out[0] = received[0]


def half_specs(other):
    def comp(place):
        return 1 - place[0] if other else place[0]

    return [
        pl.BlockSpec((1, 1, 1, W, W), lambda i, place: (0, comp(place), i, 0, 0)),
        pl.BlockSpec((1, 1, EXTRA, W), lambda i, place: (comp(place), i, 0, 0)),
    ]


def spot_spec(other):
    def index(i, place):
        core = 1 - place[0] if other else place[0]
        return (spot(8 * core + i, place[1]), 0, 0)

    return pl.BlockSpec((1, BLOCK, W), index)


def eight(kernel, out_rows, in_specs, out_spec, place, *arrays, **options):
    return pl.pallas_call(
        kernel,
        out_shape=jax.ShapeDtypeStruct((out_rows, BLOCK, W), BF16),
        grid_spec=pltpu.PrefetchScalarGridSpec(
            num_scalar_prefetch=1, grid=(8,), in_specs=in_specs, out_specs=out_spec
        ),
        **options,
    )(place, *arrays)


def apply_block(vectors, blocks, layer):
    return lax.dot_general(
        vectors, blocks[layer], (((1,), (1,)), ((), ())), preferred_element_type=F32
    )


def couple(coef, layer, own, diff):
    return coef[layer, 0:1, :] * own + coef[layer, 1:2, :] * diff


def start_kernel(blocks, forcing, down, send):
    current = apply_block(forcing[0].astype(BF16), blocks, 0).astype(BF16)
    down[0] = current
    send[...] = current


def phase_kernel(comp, steps, place, blocks, forcing, coef, *refs):
    near = refs[0:1] if comp == 1 else refs[0:2]
    down_in, up_in, down, up, send = refs[len(near):]
    columns = lax.broadcasted_iota(jnp.int32, (NJ, W), 1)

    def differences(slot):
        if comp == 1:
            field = near[0][slot].astype(F32)
            after = jnp.where(columns == W - 1, 0.0, pltpu.roll(field, W - 1, 1))
            before = jnp.where(columns == 0, 0.0, pltpu.roll(field, 1, 1))
            return after - before
        below = jnp.where(place[2] == 0, 0.0, near[0][slot].astype(F32))
        above = jnp.where(place[2] == ROWS - 1, 0.0, near[1][slot].astype(F32))
        return above - below

    @pl.when(place[0] == comp)
    def _():
        for slot, (layer, is_up) in enumerate(steps):
            diff = differences(slot)
            if is_up:
                own = down[layer + 1].astype(F32) if layer == NL - 2 else up[layer + 1]
                image = couple(coef, layer, own, diff).astype(BF16)
                current = down[layer].astype(F32) - apply_block(image, blocks, layer)
                up[layer] = current
                send[slot] = current.astype(BF16)
            else:
                own = down[layer - 1].astype(F32)
                residue = (forcing[layer] - couple(coef, layer, own, diff)).astype(BF16)
                current = apply_block(residue, blocks, layer).astype(BF16)
                down[layer] = current
                send[slot] = current
                if layer == NL - 1:
                    up[layer] = current.astype(F32)

    @pl.when(place[0] != comp)
    def _():
        send[...] = jnp.zeros_like(send)


def phase(comp, steps, place, blocks, forcing, coef, near, down, up):
    first = 4 + len(near)
    return pl.pallas_call(
        functools.partial(phase_kernel, comp, steps),
        out_shape=(
            jax.ShapeDtypeStruct(down.shape, down.dtype),
            jax.ShapeDtypeStruct(up.shape, up.dtype),
            jax.ShapeDtypeStruct((len(steps), NJ, W), BF16),
        ),
        in_specs=[SMEM] + [VMEM] * (5 + len(near)),
        out_specs=(VMEM, VMEM, VMEM),
        input_output_aliases={first: 0, first + 1: 1},
        compiler_params=PARAMS,
    )(place, blocks, forcing, coef, *near, down, up)


def gram_kernel(up, gram):
    total = jnp.zeros((NJ, NJ), F32)
    for layer in range(NL):
        rows = up[layer]
        total += lax.dot_general(
            rows, rows, (((1,), (1,)), ((), ())),
            precision=lax.Precision.HIGHEST, preferred_element_type=F32,
        )
    gram[...] = total


def factor_kernel(gram, up, basis, triangle):
    lane = lax.broadcasted_iota(jnp.int32, (NJ, NJ), 1)
    row = lax.broadcasted_iota(jnp.int32, (NJ, NJ), 0)
    left = gram[...] * (1.0 / (NL * 2 * ROWS * W))
    right = jnp.where(lane == row, 1.0, 0.0)
    for k in range(NJ):
        scale = lax.rsqrt(left[k:k + 1, k:k + 1])
        row_left = left[k:k + 1, :] * scale
        row_right = right[k:k + 1, :] * scale
        factor = jnp.where(row > k, left[:, k:k + 1] * scale, 0.0)
        left = jnp.where(row == k, row_left, left - factor * row_left)
        right = jnp.where(row == k, row_right, right - factor * row_right)
    triangle[...] = jnp.where(lane >= row, left, 0.0)
    for layer in range(NL):
        basis[layer] = jnp.dot(
            right, up[layer], precision=lax.Precision.HIGHEST, preferred_element_type=F32
        ).astype(BF16)


def unpack_send(place, rows, send):
    core, y = place[0], place[1]
    for i in range(8):
        send[i] = rows[spot(8 * (1 - core) + i, y)]


def unpack_all(place, rows, received, out):
    core, y = place[0], place[1]
    for i in range(8):
        own = rows[spot(8 * core + i, y)].astype(F32)
        other = received[i].astype(F32)
        out[0, :, 0, i, :] = jnp.where(core == 0, own, other)
        out[0, :, 1, i, :] = jnp.where(core == 0, other, own)


def per_device(source_modes, port_cells, frequencies, layer_inverse, coupling_self, coupling_curl):
    layer_pos = lax.axis_index("layer")
    tile = lax.axis_index("tile")
    core, y = tile % 2, tile // 2
    x, z = layer_pos // 4, layer_pos % 4
    rank = 4 * x + jnp.where(x % 2 == 0, z, 3 - z)
    row = NL * y + jnp.where(y % 2 == 0, rank, NL - 1 - rank)
    place = jnp.stack([core, y, row, jnp.zeros_like(row)]).astype(jnp.int32)

    def pieces(values):
        out = []
        for _ in range(3):
            part = lax.reduce_precision(values, 8, 7)
            out.append(part.astype(BF16))
            values = values - part
        return out

    extras = jnp.concatenate(
        [jnp.moveaxis(source_modes[0], 0, 2)]
        + [p[:, :, None] for p in pieces(coupling_self[0]) + pieces(coupling_curl[0])]
        + [jnp.zeros((2, 8, EXTRA - 14, W), BF16)],
        axis=2,
    )
    in_turn = pl.BlockSpec((1, BLOCK, W), lambda i, place: (i, 0, 0))
    to_send = eight(pack_send, 8, half_specs(True), in_turn, place, layer_inverse, extras)
    received = swap(to_send, CORE)
    part = eight(pack_send, NL, half_specs(False), spot_spec(False), place, layer_inverse, extras)
    packed = eight(
        pack_other, NL, [in_turn, ANY], spot_spec(True), place, received, part,
        input_output_aliases={2: 0},
    )
    arrived = lax.all_to_all(packed, "layer", 0, 0, tiled=True)
    blocks = arrived[:, 0:W]

    columns = jnp.arange(W, dtype=F32)
    offsets = (columns[None, :] - port_cells.astype(F32)[:, None]) / (W // 8)
    port_taper = 1.0 / (1.0 + offsets * offsets)
    angle = frequencies[None, :] * (jnp.arange(NL, dtype=F32)[:, None] + 1.0)
    phases = jnp.stack([jnp.cos(angle), jnp.sin(angle)], axis=2)
    sources = arrived[:, W:W + 8].astype(F32)
    forcing = (
        sources[:, :, None, None]
        * port_taper[None, :, None, None, :]
        * phases[:, None, :, :, None]
    ).reshape(NL, NJ, W)
    coupling = arrived[:, W + 8:W + 14].astype(F32)
    coef = jnp.stack(
        [coupling[:, 0] + coupling[:, 1] + coupling[:, 2], coupling[:, 3] + coupling[:, 4] + coupling[:, 5]],
        axis=1,
    )

    down, first = pl.pallas_call(
        start_kernel,
        out_shape=(jax.ShapeDtypeStruct((NL, NJ, W), BF16), jax.ShapeDtypeStruct((NJ, W), BF16)),
        in_specs=[VMEM, VMEM],
        out_specs=(VMEM, VMEM),
        compiler_params=PARAMS,
    )(blocks, forcing)
    up = jnp.zeros((NL, NJ, W), F32)

    sequence = [(layer, False) for layer in range(NL)] + [(layer, True) for layer in range(NL - 2, -1, -1)]
    run = lambda comp, at, near, down, up: phase(
        comp, sequence[at[0]:at[1]], place, blocks, forcing, coef, near, down, up
    )
    x_sent = swap(first, CORE)[None]
    down, up, y_new = run(1, (1, 2), [x_sent], down, up)
    y_pair = jnp.concatenate([first[None], y_new])
    at = 1
    last = len(sequence)
    while at < last:
        stop = min(at + 2, last)
        near = [swap(y_pair, RAISE), swap(y_pair, LOWER)]
        down, up, x_pair = run(0, (at, stop), near, down, up)
        y_stop = min(at + 3, last)
        x_sent = swap(x_pair[:y_stop - at - 1], CORE)
        down, up, y_pair = run(1, (at + 1, y_stop), [x_sent], down, up)
        at = stop

    gram = pl.pallas_call(
        gram_kernel,
        out_shape=jax.ShapeDtypeStruct((NJ, NJ), F32),
        in_specs=[VMEM],
        out_specs=VMEM,
        compiler_params=PARAMS,
    )(up)
    for pairs in exchanges():
        gram = gram + swap(gram, pairs)
    basis, triangle = pl.pallas_call(
        factor_kernel,
        out_shape=(jax.ShapeDtypeStruct((NL, NJ, W), BF16), jax.ShapeDtypeStruct((NJ, NJ), F32)),
        in_specs=[VMEM, VMEM],
        out_specs=(VMEM, VMEM),
        compiler_params=PARAMS,
    )(gram, up)
    rows = lax.all_to_all(basis, "layer", 0, 0, tiled=True)
    back = pl.pallas_call(
        unpack_send,
        out_shape=jax.ShapeDtypeStruct((8, NJ, W), BF16),
        in_specs=[SMEM, VMEM],
        out_specs=VMEM,
        compiler_params=PARAMS,
    )(place, rows)
    out = pl.pallas_call(
        unpack_all,
        out_shape=jax.ShapeDtypeStruct((1, NJ, 2, 8, W), F32),
        in_specs=[SMEM, VMEM, VMEM],
        out_specs=VMEM,
        compiler_params=PARAMS,
    )(place, rows, swap(back, CORE))
    return (out, triangle)


def solution(mesh):
    in_specs = (
        P("layer", None, None, "tile", None),
        P(),
        P(),
        P("layer", None, "tile", None, None),
        P("layer", None, "tile", None),
        P("layer", None, "tile", None),
    )
    out_specs = (P("layer", None, None, "tile", None), P())
    return jax.shard_map(
        per_device, mesh=mesh, in_specs=in_specs, out_specs=out_specs, check_vma=False
    )
```

time: 1410 us -> 391 us (0.28)
  waiting for transfers between devices: 634 us -> 232 us
  matrix products: 277 us -> 0 us
  starting transfers between devices: 272 us -> 67.6 us
  blocking collectives: 74.7 us -> 12.7 us
  Pallas kernels: 0 us -> 53.8 us
  other arithmetic: 56 us -> 4.07 us
  local copies, waits for them, and re-layouts: 59.2 us -> 16.5 us
  loops' own time: 24.6 us -> 0 us
    ppermute x96 -> x55, waiting for transfers between devices: 634 us -> 82.3 us  [swap(): return lax.ppermute(value, AXES, pairs)]
    dot_general x194 -> x0, matrix products: 277 us -> none  [the longest x32 190 us: apply_inverse(): jnp.einsum('crik,jcrk->jcri', inverse_block, vectors, preferred_element_t...]
    ppermute x96 -> x55, starting transfers between devices: 272 us -> 59.5 us  [swap(): return lax.ppermute(value, AXES, pairs)]
    all_to_all x0 -> x1, waiting for transfers between devices: none -> 150 us  [per_device(): arrived = lax.all_to_all(packed, 'layer', 0, 0, tiled=True)]
    psum x1 -> x0, blocking collectives: 74.7 us -> none  [per_device(): gram_whole = lax.psum(gram_local, ('layer', 'tile'))]
    pallas_call x0 -> x39, Pallas kernels: none -> 53.8 us  [the longest x31 24.4 us: phase(): pl.pallas_call(functools.partial(phase_kernel, comp, steps), out_shape=(j...]
    mul x66 -> x4, local copies, waits for them, and re-layouts: 41.5 us -> 1.11 us  [per_device(): sources[:, :, None, None] * port_taper[None, :, None, None, :]]
    another operation x34 -> x3, other arithmetic: 34.2 us -> 0.64 us  [the longest x1 0.56 us: per_device(): place = jnp.stack([core, y, row, jnp.zeros_like(row)]).astype(jnp.int32)]
  transfers between devices with their start and end apart: 96 -> 56, of which waited for: 64 -> 49; matrix products, arithmetic and copies ran while one was open for 3% -> 0% of each run, Pallas kernels for 0% -> 2%
where the time goes in v1:
time: 391 us; the launch traced here: 389 us
  waiting for transfers between devices  232 us (59%)
  starting transfers between devices  67.6 us (17%)
  Pallas kernels  53.8 us (14%)
  local copies, waits for them, and re-layouts  16.5 us (4%)
  blocking collectives  12.7 us (3%)
  other arithmetic  4.07 us (1%)
    all_to_all x1, waiting for transfers between devices, per_device(): arrived = lax.all_to_all(packed, 'layer', 0, 0, tiled=True)  150 us
    ppermute x55, waiting for transfers between devices, swap(): return lax.ppermute(value, AXES, pairs)  82.3 us
    ppermute x55, starting transfers between devices, swap(): return lax.ppermute(value, AXES, pairs)  59.5 us
    pallas_call x31, Pallas kernels, phase(): pl.pallas_call(functools.partial(phase_kernel, comp, steps), out_shape=(j...  24.4 us
    pallas_call x3, Pallas kernels, eight(): pl.pallas_call(kernel, out_shape=jax.ShapeDtypeStruct((out_rows, BLOCK, W...  22.1 us
    all_to_all x1, blocking collectives, per_device(): rows = lax.all_to_all(basis, 'layer', 0, 0, tiled=True)  12.7 us
    all_to_all x1, starting transfers between devices, per_device(): arrived = lax.all_to_all(packed, 'layer', 0, 0, tiled=True)  8.14 us
  transfers between devices with their start and end apart: 56, of which 49 were waited for; matrix products, arithmetic and copies ran while one was open for 0% of the time, Pallas kernels for 2%

profile of v1, /device:TPU:0, one launch (start us, length us, event | category | flops | bytes accessed | tf_op | source)
XLA Modules:
  0.0 388.6 jit_solution(17399456190936447375)
XLA Ops:
  4.9 7.3 %shard_map.77 = bf16[8,528,512]{2,1,0:T(8,128)(2,1)} custom-call(s32[4]{0:T(128)} %pad_add_fusion.place, bf16[1,2,8,512,512]{4,3,2,1,0:T(8,128)(2,1)} %blocks.3, bf16[2,8,16,512]{3,2,1,0:T(8,128)(2,1)} %concatenate.6.extras), custom_call_target="tpu_custom_call" | custom-call | tf_op jit(solution)/shard_map/pallas_call | solution.py:88
  12.2 7.4 %shard_map.78.part = bf16[16,528,512]{2,1,0:T(8,128)(2,1)} custom-call(s32[4]{0:T(128)} %pad_add_fusion.place, bf16[1,2,8,512,512]{4,3,2,1,0:T(8,128)(2,1)} %blocks.3, bf16[2,8,16,512]{3,2,1,0:T(8,128)(2,1)} %concatenate.6.extras), custom_call_target="tpu_custom_call" | custom-call | tf_op jit(solution)/shard_map/pallas_call | solution.py:88
  19.9 7.4 %shard_map.79 = bf16[16,528,512]{2,1,0:T(8,128)(2,1)} custom-call(s32[4]{0:T(128)} %pad_add_fusion.place, bf16[8,528,512]{2,1,0:T(8,128)(2,1)} %collective-permute-done.received, bf16[16,528,512]{2,1,0:T(8,128)(2,1)} %shard_map.78.part), custom_call_target="tpu_custom_call", output_to_operand_aliasing={{}: (2, {})} | custom-call | tf_op jit(solution)/shard_map/pallas_call | solution.py:88
  27.3 8.1 %all-to-all-start = ((bf16[16,528,512]{2,1,0:T(8,128)(2,1)}), bf16[16,528,512]{2,1,0:T(8,128)(2,1)}, u32[]{:S(2)}, u32[]{:S(2)}) async-start(bf16[16,528,512]{2,1,0:T(8,128)(2,1)} %shard_map.79), calls=%async_computation | async-start | bytes 17301504 | tf_op jit(solution)/shard_map/all_to_all | solution.py:245
  35.8 150.2 %all-to-all-done = bf16[16,528,512]{2,1,0:T(8,128)(2,1)} async-done(((bf16[16,528,512]{2,1,0:T(8,128)(2,1)}), bf16[16,528,512]{2,1,0:T(8,128)(2,1)}, u32[]{:S(2)}, u32[]{:S(2)}) %all-to-all-start) | async-done | bytes 8650784 | tf_op jit(solution)/shard_map/all_to_all | solution.py:245
  188.1 7.5 %slice.40.blocks = bf16[16,512,512]{2,1,0:T(8,128)(2,1)} slice(bf16[16,528,512]{2,1,0:T(8,128)(2,1)} %all-to-all-done), slice={[0:16], [0:512], [0:512]} | slice | bytes 16777216 | tf_op jit(solution)/shard_map/slice | solution.py:246
  195.6 3.4 copy-done
  200.7 1.7 copy-done.1
  203.0 4.3 %collective-permute-start.2 = (bf16[2,32,512]{2,1,0:T(8,128)(2,1)S(1)}, bf16[2,32,512]{2,1,0:T(8,128)(2,1)S(1)}, u32[]{:S(2)}, u32[]{:S(2)}) collective-permute-start(bf16[2,32,512]{2,1,0:T(8,128)(2,1)S(1)} %pad_maximum_fusion.1), channel_id=1, source_target_pairs={{0,9},{1,8},{8,17},{9,16},{16,25},{17,24},{24,57},{25,56},{56,49},... | collective-permute-start | bytes 196616 | tf_op jit(solution)/shard_map/ppermute | solution.py:43
  207.3 1.9 collective-permute-done.2.refs_0_
  209.2 1.8 collective-permute-done.3.refs_1_
  215.7 2.0 collective-permute-start.6
  217.8 1.9 collective-permute-done.5.refs_0_
  223.1 4.0 %collective-permute-start.9 = (bf16[2,32,512]{2,1,0:T(8,128)(2,1)S(1)}, bf16[2,32,512]{2,1,0:T(8,128)(2,1)S(1)}, u32[]{:S(2)}, u32[]{:S(2)}) collective-permute-start(bf16[2,32,512]{2,1,0:T(8,128)(2,1)S(1)} %get-tuple-element.111), channel_id=1, source_target_pairs={{0,7},{1,6},{8,1},{9,0},{16,9},{17,8},{24,17},{25,16},{56,25},{57,... | collective-permute-start | bytes 196616 | tf_op jit(solution)/shard_map/ppermute | solution.py:43
  227.2 2.5 collective-permute-done.8.refs_0_
  232.6 2.9 collective-permute-start.12
  235.5 1.9 collective-permute-done.11.refs_0_
  240.9 3.8 collective-permute-start.15
  244.7 2.5 collective-permute-done.14.refs_0_
  250.4 2.9 collective-permute-start.18
  253.3 1.9 collective-permute-done.17.refs_0_
  258.7 3.8 collective-permute-start.21
  262.5 2.5 collective-permute-done.20.refs_0_
  267.9 2.9 collective-permute-start.24
  270.9 1.9 collective-permute-done.23.refs_0_
  277.2 3.0 collective-permute-start.27
  280.2 2.5 collective-permute-done.26.refs_0_
  285.6 2.0 collective-permute-start.29
  288.7 1.9 collective-permute-done.29.refs_0_
  294.9 3.1 collective-permute-start.33
  298.0 1.9 collective-permute-done.32.refs_0_
  303.3 3.8 collective-permute-start.36
  307.1 2.5 collective-permute-done.35.refs_0_
  312.6 2.9 collective-permute-start.39
  315.5 1.9 collective-permute-done.38.refs_0_
  320.9 3.9 %collective-permute-start.42 = (bf16[2,32,512]{2,1,0:T(8,128)(2,1)S(1)}, bf16[2,32,512]{2,1,0:T(8,128)(2,1)S(1)}, u32[]{:S(2)}, u32[]{:S(2)}) collective-permute-start(bf16[2,32,512]{2,1,0:T(8,128)(2,1)S(1)} %get-tuple-element.177), channel_id=1, source_target_pairs={{0,7},{1,6},{8,1},{9,0},{16,9},{17,8},{24,17},{25,16},{56,25},{57,... | collective-permute-start | bytes 196616 | tf_op jit(solution)/shard_map/ppermute | solution.py:43
  324.8 2.5 collective-permute-done.41.refs_0_
  330.5 2.9 collective-permute-start.45
  333.5 1.9 collective-permute-done.44.refs_0_
  341.7 3.7 collective-permute-done.48
  345.4 3.6 collective-permute-start.49
  350.8 3.7 collective-permute-done.50
  354.5 4.9 %collective-permute-done.51 = f32[32,32]{1,0:T(8,128)S(1)} collective-permute-done((f32[32,32]{1,0:T(8,128)S(1)}, f32[32,32]{1,0:T(8,128)S(1)}, u32[]{:S(2)}, u32[]{:S(2)}) %collective-permute-start.51) | collective-permute-done | bytes 4128 | tf_op jit(solution)/shard_map/ppermute | solution.py:43
  359.5 3.7 collective-permute-done.52
  363.2 4.9 %collective-permute-done.53 = f32[32,32]{1,0:T(8,128)S(1)} collective-permute-done((f32[32,32]{1,0:T(8,128)S(1)}, f32[32,32]{1,0:T(8,128)S(1)}, u32[]{:S(2)}, u32[]{:S(2)}) %collective-permute-start.53) | collective-permute-done | bytes 4128 | tf_op jit(solution)/shard_map/ppermute | solution.py:43
  368.2 3.6 shard_map.113
  371.7 12.7 %all_to_all.10.rows = bf16[16,32,512]{2,1,0:T(8,128)(2,1)S(1)} all-to-all(bf16[16,32,512]{2,1,0:T(8,128)(2,1)S(1)} %get-tuple-element.190), channel_id=1, replica_groups=mesh['layer'=16,'tile'=8] {'layer'}, dimensions={0} | all-to-all | bytes 1048576 | tf_op jit(solution)/shard_map/all_to_all | solution.py:308
  386.7 1.9 shard_map.115
  (144 shorter events, 68.8 us)
Async XLA Ops:
  12.2 7.7 %collective-permute-start = (bf16[8,528,512]{2,1,0:T(8,128)(2,1)}, bf16[8,528,512]{2,1,0:T(8,128)(2,1)}, u32[]{:S(2)}, u32[]{:S(2)}) collective-permute-start(bf16[8,528,512]{2,1,0:T(8,128)(2,1)} %shard_map.77), channel_id=1, source_target_pairs={{0,1},{1,0},{8,9},{9,8},{16,17},{17,16},{24,25},{25,24},{56,57},{5... | collective-permute-start | bytes 12976136 | tf_op jit(solution)/shard_map/ppermute | solution.py:43
  27.3 158.7 %all-to-all-start = ((bf16[16,528,512]{2,1,0:T(8,128)(2,1)}), bf16[16,528,512]{2,1,0:T(8,128)(2,1)}, u32[]{:S(2)}, u32[]{:S(2)}) async-start(bf16[16,528,512]{2,1,0:T(8,128)(2,1)} %shard_map.79), calls=%async_computation | async-start | bytes 17301504 | tf_op jit(solution)/shard_map/all_to_all | solution.py:245
  199.2 1.3 collective-permute-start.1
  203.0 6.2 %collective-permute-start.2 = (bf16[2,32,512]{2,1,0:T(8,128)(2,1)S(1)}, bf16[2,32,512]{2,1,0:T(8,128)(2,1)S(1)}, u32[]{:S(2)}, u32[]{:S(2)}) collective-permute-start(bf16[2,32,512]{2,1,0:T(8,128)(2,1)S(1)} %pad_maximum_fusion.1), channel_id=1, source_target_pairs={{0,9},{1,8},{8,17},{9,16},{16,25},{17,24},{24,57},{25,56},{56,49},... | collective-permute-start | bytes 196616 | tf_op jit(solution)/shard_map/ppermute | solution.py:43
  207.3 3.7 collective-permute-start.3
  212.0 2.2 collective-permute-start.4
  214.7 5.0 %collective-permute-start.5 = (bf16[2,32,512]{2,1,0:T(8,128)(2,1)S(1)}, bf16[2,32,512]{2,1,0:T(8,128)(2,1)S(1)}, u32[]{:S(2)}, u32[]{:S(2)}) collective-permute-start(bf16[2,32,512]{2,1,0:T(8,128)(2,1)S(1)} %get-tuple-element.105), channel_id=1, source_target_pairs={{0,9},{1,8},{8,17},{9,16},{16,25},{17,24},{24,57},{25,56},{56,49},... | collective-permute-start | bytes 196616 | tf_op jit(solution)/shard_map/ppermute | solution.py:43
  215.7 4.4 %collective-permute-start.6 = (bf16[2,32,512]{2,1,0:T(8,128)(2,1)S(1)}, bf16[2,32,512]{2,1,0:T(8,128)(2,1)S(1)}, u32[]{:S(2)}, u32[]{:S(2)}) collective-permute-start(bf16[2,32,512]{2,1,0:T(8,128)(2,1)S(1)} %get-tuple-element.105), channel_id=1, source_target_pairs={{0,7},{1,6},{8,1},{9,0},{16,9},{17,8},{24,17},{25,16},{56,25},{57,... | collective-permute-start | bytes 196616 | tf_op jit(solution)/shard_map/ppermute | solution.py:43
  221.1 1.3 collective-permute-start.7
  223.0 6.6 %collective-permute-start.8 = (bf16[2,32,512]{2,1,0:T(8,128)(2,1)S(1)}, bf16[2,32,512]{2,1,0:T(8,128)(2,1)S(1)}, u32[]{:S(2)}, u32[]{:S(2)}) collective-permute-start(bf16[2,32,512]{2,1,0:T(8,128)(2,1)S(1)} %get-tuple-element.111), channel_id=1, source_target_pairs={{0,9},{1,8},{8,17},{9,16},{16,25},{17,24},{24,57},{25,56},{56,49},... | collective-permute-start | bytes 196616 | tf_op jit(solution)/shard_map/ppermute | solution.py:43
  223.1 6.5 %collective-permute-start.9 = (bf16[2,32,512]{2,1,0:T(8,128)(2,1)S(1)}, bf16[2,32,512]{2,1,0:T(8,128)(2,1)S(1)}, u32[]{:S(2)}, u32[]{:S(2)}) collective-permute-start(bf16[2,32,512]{2,1,0:T(8,128)(2,1)S(1)} %get-tuple-element.111), channel_id=1, source_target_pairs={{0,7},{1,6},{8,1},{9,0},{16,9},{17,8},{24,17},{25,16},{56,25},{57,... | collective-permute-start | bytes 196616 | tf_op jit(solution)/shard_map/ppermute | solution.py:43
  230.6 1.3 collective-permute-start.10
  232.5 5.0 %collective-permute-start.11 = (bf16[2,32,512]{2,1,0:T(8,128)(2,1)S(1)}, bf16[2,32,512]{2,1,0:T(8,128)(2,1)S(1)}, u32[]{:S(2)}, u32[]{:S(2)}) collective-permute-start(bf16[2,32,512]{2,1,0:T(8,128)(2,1)S(1)} %get-tuple-element.117), channel_id=1, source_target_pairs={{0,9},{1,8},{8,17},{9,16},{16,25},{17,24},{24,57},{25,56},{56,49},... | collective-permute-start | bytes 196616 | tf_op jit(solution)/shard_map/ppermute | solution.py:43
  232.6 5.3 %collective-permute-start.12 = (bf16[2,32,512]{2,1,0:T(8,128)(2,1)S(1)}, bf16[2,32,512]{2,1,0:T(8,128)(2,1)S(1)}, u32[]{:S(2)}, u32[]{:S(2)}) collective-permute-start(bf16[2,32,512]{2,1,0:T(8,128)(2,1)S(1)} %get-tuple-element.117), channel_id=1, source_target_pairs={{0,7},{1,6},{8,1},{9,0},{16,9},{17,8},{24,17},{25,16},{56,25},{57,... | collective-permute-start | bytes 196616 | tf_op jit(solution)/shard_map/ppermute | solution.py:43
  238.9 1.3 collective-permute-start.13
  240.8 6.4 %collective-permute-start.14 = (bf16[2,32,512]{2,1,0:T(8,128)(2,1)S(1)}, bf16[2,32,512]{2,1,0:T(8,128)(2,1)S(1)}, u32[]{:S(2)}, u32[]{:S(2)}) collective-permute-start(bf16[2,32,512]{2,1,0:T(8,128)(2,1)S(1)} %get-tuple-element.123), channel_id=1, source_target_pairs={{0,9},{1,8},{8,17},{9,16},{16,25},{17,24},{24,57},{25,56},{56,49},... | collective-permute-start | bytes 196616 | tf_op jit(solution)/shard_map/ppermute | solution.py:43
  240.9 6.3 %collective-permute-start.15 = (bf16[2,32,512]{2,1,0:T(8,128)(2,1)S(1)}, bf16[2,32,512]{2,1,0:T(8,128)(2,1)S(1)}, u32[]{:S(2)}, u32[]{:S(2)}) collective-permute-start(bf16[2,32,512]{2,1,0:T(8,128)(2,1)S(1)} %get-tuple-element.123), channel_id=1, source_target_pairs={{0,7},{1,6},{8,1},{9,0},{16,9},{17,8},{24,17},{25,16},{56,25},{57,... | collective-permute-start | bytes 196616 | tf_op jit(solution)/shard_map/ppermute | solution.py:43
  248.2 1.3 collective-permute-start.16
  250.1 5.2 %collective-permute-start.17 = (bf16[2,32,512]{2,1,0:T(8,128)(2,1)S(1)}, bf16[2,32,512]{2,1,0:T(8,128)(2,1)S(1)}, u32[]{:S(2)}, u32[]{:S(2)}) collective-permute-start(bf16[2,32,512]{2,1,0:T(8,128)(2,1)S(1)} %get-tuple-element.129), channel_id=1, source_target_pairs={{0,9},{1,8},{8,17},{9,16},{16,25},{17,24},{24,57},{25,56},{56,49},... | collective-permute-start | bytes 196616 | tf_op jit(solution)/shard_map/ppermute | solution.py:43
  250.4 5.3 %collective-permute-start.18 = (bf16[2,32,512]{2,1,0:T(8,128)(2,1)S(1)}, bf16[2,32,512]{2,1,0:T(8,128)(2,1)S(1)}, u32[]{:S(2)}, u32[]{:S(2)}) collective-permute-start(bf16[2,32,512]{2,1,0:T(8,128)(2,1)S(1)} %get-tuple-element.129), channel_id=1, source_target_pairs={{0,7},{1,6},{8,1},{9,0},{16,9},{17,8},{24,17},{25,16},{56,25},{57,... | collective-permute-start | bytes 196616 | tf_op jit(solution)/shard_map/ppermute | solution.py:43
  256.7 1.3 collective-permute-start.19
  258.6 6.4 %collective-permute-start.20 = (bf16[2,32,512]{2,1,0:T(8,128)(2,1)S(1)}, bf16[2,32,512]{2,1,0:T(8,128)(2,1)S(1)}, u32[]{:S(2)}, u32[]{:S(2)}) collective-permute-start(bf16[2,32,512]{2,1,0:T(8,128)(2,1)S(1)} %get-tuple-element.135), channel_id=1, source_target_pairs={{0,9},{1,8},{8,17},{9,16},{16,25},{17,24},{24,57},{25,56},{56,49},... | collective-permute-start | bytes 196616 | tf_op jit(solution)/shard_map/ppermute | solution.py:43
  258.7 6.3 %collective-permute-start.21 = (bf16[2,32,512]{2,1,0:T(8,128)(2,1)S(1)}, bf16[2,32,512]{2,1,0:T(8,128)(2,1)S(1)}, u32[]{:S(2)}, u32[]{:S(2)}) collective-permute-start(bf16[2,32,512]{2,1,0:T(8,128)(2,1)S(1)} %get-tuple-element.135), channel_id=1, source_target_pairs={{0,7},{1,6},{8,1},{9,0},{16,9},{17,8},{24,17},{25,16},{56,25},{57,... | collective-permute-start | bytes 196616 | tf_op jit(solution)/shard_map/ppermute | solution.py:43
  266.0 1.3 collective-permute-start.22
  267.9 5.0 %collective-permute-start.23 = (bf16[2,32,512]{2,1,0:T(8,128)(2,1)S(1)}, bf16[2,32,512]{2,1,0:T(8,128)(2,1)S(1)}, u32[]{:S(2)}, u32[]{:S(2)}) collective-permute-start(bf16[2,32,512]{2,1,0:T(8,128)(2,1)S(1)} %get-tuple-element.141), channel_id=1, source_target_pairs={{0,9},{1,8},{8,17},{9,16},{16,25},{17,24},{24,57},{25,56},{56,49},... | collective-permute-start | bytes 196616 | tf_op jit(solution)/shard_map/ppermute | solution.py:43
  267.9 5.4 %collective-permute-start.24 = (bf16[2,32,512]{2,1,0:T(8,128)(2,1)S(1)}, bf16[2,32,512]{2,1,0:T(8,128)(2,1)S(1)}, u32[]{:S(2)}, u32[]{:S(2)}) collective-permute-start(bf16[2,32,512]{2,1,0:T(8,128)(2,1)S(1)} %get-tuple-element.141), channel_id=1, source_target_pairs={{0,7},{1,6},{8,1},{9,0},{16,9},{17,8},{24,17},{25,16},{56,25},{57,... | collective-permute-start | bytes 196616 | tf_op jit(solution)/shard_map/ppermute | solution.py:43
  276.2 6.5 %collective-permute-start.26 = (bf16[2,32,512]{2,1,0:T(8,128)(2,1)S(1)}, bf16[2,32,512]{2,1,0:T(8,128)(2,1)S(1)}, u32[]{:S(2)}, u32[]{:S(2)}) collective-permute-start(bf16[2,32,512]{2,1,0:T(8,128)(2,1)S(1)} %get-tuple-element.147), channel_id=1, source_target_pairs={{0,9},{1,8},{8,17},{9,16},{16,25},{17,24},{24,57},{25,56},{56,49},... | collective-permute-start | bytes 196616 | tf_op jit(solution)/shard_map/ppermute | solution.py:43
  277.2 5.5 %collective-permute-start.27 = (bf16[2,32,512]{2,1,0:T(8,128)(2,1)S(1)}, bf16[2,32,512]{2,1,0:T(8,128)(2,1)S(1)}, u32[]{:S(2)}, u32[]{:S(2)}) collective-permute-start(bf16[2,32,512]{2,1,0:T(8,128)(2,1)S(1)} %get-tuple-element.147), channel_id=1, source_target_pairs={{0,7},{1,6},{8,1},{9,0},{16,9},{17,8},{24,17},{25,16},{56,25},{57,... | collective-permute-start | bytes 196616 | tf_op jit(solution)/shard_map/ppermute | solution.py:43
  285.6 5.0 %collective-permute-start.29 = (bf16[2,32,512]{2,1,0:T(8,128)(2,1)S(1)}, bf16[2,32,512]{2,1,0:T(8,128)(2,1)S(1)}, u32[]{:S(2)}, u32[]{:S(2)}) collective-permute-start(bf16[2,32,512]{2,1,0:T(8,128)(2,1)S(1)} %get-tuple-element.153), channel_id=1, source_target_pairs={{0,9},{1,8},{8,17},{9,16},{16,25},{17,24},{24,57},{25,56},{56,49},... | collective-permute-start | bytes 196616 | tf_op jit(solution)/shard_map/ppermute | solution.py:43
  287.6 4.3 %collective-permute-start.30 = (bf16[2,32,512]{2,1,0:T(8,128)(2,1)S(1)}, bf16[2,32,512]{2,1,0:T(8,128)(2,1)S(1)}, u32[]{:S(2)}, u32[]{:S(2)}) collective-permute-start(bf16[2,32,512]{2,1,0:T(8,128)(2,1)S(1)} %get-tuple-element.153), channel_id=1, source_target_pairs={{0,7},{1,6},{8,1},{9,0},{16,9},{17,8},{24,17},{25,16},{56,25},{57,... | collective-permute-start | bytes 196616 | tf_op jit(solution)/shard_map/ppermute | solution.py:43
  294.8 5.0 %collective-permute-start.32 = (bf16[2,32,512]{2,1,0:T(8,128)(2,1)S(1)}, bf16[2,32,512]{2,1,0:T(8,128)(2,1)S(1)}, u32[]{:S(2)}, u32[]{:S(2)}) collective-permute-start(bf16[2,32,512]{2,1,0:T(8,128)(2,1)S(1)} %get-tuple-element.159), channel_id=1, source_target_pairs={{0,9},{1,8},{8,17},{9,16},{16,25},{17,24},{24,57},{25,56},{56,49},... | collective-permute-start | bytes 196616 | tf_op jit(solution)/shard_map/ppermute | solution.py:43
  294.9 5.4 %collective-permute-start.33 = (bf16[2,32,512]{2,1,0:T(8,128)(2,1)S(1)}, bf16[2,32,512]{2,1,0:T(8,128)(2,1)S(1)}, u32[]{:S(2)}, u32[]{:S(2)}) collective-permute-start(bf16[2,32,512]{2,1,0:T(8,128)(2,1)S(1)} %get-tuple-element.159), channel_id=1, source_target_pairs={{0,7},{1,6},{8,1},{9,0},{16,9},{17,8},{24,17},{25,16},{56,25},{57,... | collective-permute-start | bytes 196616 | tf_op jit(solution)/shard_map/ppermute | solution.py:43
  303.2 6.4 %collective-permute-start.35 = (bf16[2,32,512]{2,1,0:T(8,128)(2,1)S(1)}, bf16[2,32,512]{2,1,0:T(8,128)(2,1)S(1)}, u32[]{:S(2)}, u32[]{:S(2)}) collective-permute-start(bf16[2,32,512]{2,1,0:T(8,128)(2,1)S(1)} %get-tuple-element.165), channel_id=1, source_target_pairs={{0,9},{1,8},{8,17},{9,16},{16,25},{17,24},{24,57},{25,56},{56,49},... | collective-permute-start | bytes 196616 | tf_op jit(solution)/shard_map/ppermute | solution.py:43
  303.3 6.3 %collective-permute-start.36 = (bf16[2,32,512]{2,1,0:T(8,128)(2,1)S(1)}, bf16[2,32,512]{2,1,0:T(8,128)(2,1)S(1)}, u32[]{:S(2)}, u32[]{:S(2)}) collective-permute-start(bf16[2,32,512]{2,1,0:T(8,128)(2,1)S(1)} %get-tuple-element.165), channel_id=1, source_target_pairs={{0,7},{1,6},{8,1},{9,0},{16,9},{17,8},{24,17},{25,16},{56,25},{57,... | collective-permute-start | bytes 196616 | tf_op jit(solution)/shard_map/ppermute | solution.py:43
  312.5 5.0 %collective-permute-start.38 = (bf16[2,32,512]{2,1,0:T(8,128)(2,1)S(1)}, bf16[2,32,512]{2,1,0:T(8,128)(2,1)S(1)}, u32[]{:S(2)}, u32[]{:S(2)}) collective-permute-start(bf16[2,32,512]{2,1,0:T(8,128)(2,1)S(1)} %get-tuple-element.171), channel_id=1, source_target_pairs={{0,9},{1,8},{8,17},{9,16},{16,25},{17,24},{24,57},{25,56},{56,49},... | collective-permute-start | bytes 196616 | tf_op jit(solution)/shard_map/ppermute | solution.py:43
  312.6 5.4 %collective-permute-start.39 = (bf16[2,32,512]{2,1,0:T(8,128)(2,1)S(1)}, bf16[2,32,512]{2,1,0:T(8,128)(2,1)S(1)}, u32[]{:S(2)}, u32[]{:S(2)}) collective-permute-start(bf16[2,32,512]{2,1,0:T(8,128)(2,1)S(1)} %get-tuple-element.171), channel_id=1, source_target_pairs={{0,7},{1,6},{8,1},{9,0},{16,9},{17,8},{24,17},{25,16},{56,25},{57,... | collective-permute-start | bytes 196616 | tf_op jit(solution)/shard_map/ppermute | solution.py:43
  320.9 6.5 %collective-permute-start.41 = (bf16[2,32,512]{2,1,0:T(8,128)(2,1)S(1)}, bf16[2,32,512]{2,1,0:T(8,128)(2,1)S(1)}, u32[]{:S(2)}, u32[]{:S(2)}) collective-permute-start(bf16[2,32,512]{2,1,0:T(8,128)(2,1)S(1)} %get-tuple-element.177), channel_id=1, source_target_pairs={{0,9},{1,8},{8,17},{9,16},{16,25},{17,24},{24,57},{25,56},{56,49},... | collective-permute-start | bytes 196616 | tf_op jit(solution)/shard_map/ppermute | solution.py:43
  320.9 6.4 %collective-permute-start.42 = (bf16[2,32,512]{2,1,0:T(8,128)(2,1)S(1)}, bf16[2,32,512]{2,1,0:T(8,128)(2,1)S(1)}, u32[]{:S(2)}, u32[]{:S(2)}) collective-permute-start(bf16[2,32,512]{2,1,0:T(8,128)(2,1)S(1)} %get-tuple-element.177), channel_id=1, source_target_pairs={{0,7},{1,6},{8,1},{9,0},{16,9},{17,8},{24,17},{25,16},{56,25},{57,... | collective-permute-start | bytes 196616 | tf_op jit(solution)/shard_map/ppermute | solution.py:43
  328.3 1.6 collective-permute-start.43
  330.5 5.0 %collective-permute-start.44 = (bf16[2,32,512]{2,1,0:T(8,128)(2,1)S(1)}, bf16[2,32,512]{2,1,0:T(8,128)(2,1)S(1)}, u32[]{:S(2)}, u32[]{:S(2)}) collective-permute-start(bf16[2,32,512]{2,1,0:T(8,128)(2,1)S(1)} %get-tuple-element.183), channel_id=1, source_target_pairs={{0,9},{1,8},{8,17},{9,16},{16,25},{17,24},{24,57},{25,56},{56,49},... | collective-permute-start | bytes 196616 | tf_op jit(solution)/shard_map/ppermute | solution.py:43
  330.5 5.4 %collective-permute-start.45 = (bf16[2,32,512]{2,1,0:T(8,128)(2,1)S(1)}, bf16[2,32,512]{2,1,0:T(8,128)(2,1)S(1)}, u32[]{:S(2)}, u32[]{:S(2)}) collective-permute-start(bf16[2,32,512]{2,1,0:T(8,128)(2,1)S(1)} %get-tuple-element.183), channel_id=1, source_target_pairs={{0,7},{1,6},{8,1},{9,0},{16,9},{17,8},{24,17},{25,16},{56,25},{57,... | collective-permute-start | bytes 196616 | tf_op jit(solution)/shard_map/ppermute | solution.py:43
  341.7 3.7 collective-permute-start.48
  345.4 5.3 %collective-permute-start.49 = (f32[32,32]{1,0:T(8,128)S(1)}, f32[32,32]{1,0:T(8,128)S(1)}, u32[]{:S(2)}, u32[]{:S(2)}) collective-permute-start(f32[32,32]{1,0:T(8,128)S(1)} %add.86), channel_id=1, source_target_pairs={{0,6},{1,7},{2,4},{3,5},{4,2},{5,3},{6,0},{7,1},{8,14},{9,15},{10,... | collective-permute-start | bytes 12296 | tf_op jit(solution)/shard_map/ppermute | solution.py:43
  350.8 3.7 collective-permute-start.50
  354.5 4.9 %collective-permute-start.51 = (f32[32,32]{1,0:T(8,128)S(1)}, f32[32,32]{1,0:T(8,128)S(1)}, u32[]{:S(2)}, u32[]{:S(2)}) collective-permute-start(f32[32,32]{1,0:T(8,128)S(1)} %add.88), channel_id=1, source_target_pairs={{0,24},{1,25},{2,26},{3,27},{4,28},{5,29},{6,30},{7,31},{8,16},{9,... | collective-permute-start | bytes 12296 | tf_op jit(solution)/shard_map/ppermute | solution.py:43
  359.5 3.7 collective-permute-start.52
  363.2 4.9 %collective-permute-start.53 = (f32[32,32]{1,0:T(8,128)S(1)}, f32[32,32]{1,0:T(8,128)S(1)}, u32[]{:S(2)}, u32[]{:S(2)}) collective-permute-start(f32[32,32]{1,0:T(8,128)S(1)} %add.90), channel_id=1, source_target_pairs={{0,96},{1,97},{2,98},{3,99},{4,100},{5,101},{6,102},{7,103},{8,104... | collective-permute-start | bytes 12296 | tf_op jit(solution)/shard_map/ppermute | solution.py:43
  385.1 1.6 collective-permute-start.54
  (13 other events, 37.2 us)

commit v2 on v1

v2 whole, which is shorter than its diff:
```python
import functools

import jax
import jax.numpy as jnp
from jax import lax
from jax.experimental import pallas as pl
from jax.experimental.pallas import tpu as pltpu
from jax.sharding import PartitionSpec as P

AXES = ("layer", "tile")
BF16 = jnp.bfloat16
F32 = jnp.float32
NL = 16
NY = 4
W = 512
NJ = 32
EXTRA = 16
BLOCK = W + EXTRA
TAIL = 128
VMEM = pl.BlockSpec(memory_space=pltpu.VMEM)
SMEM = pl.BlockSpec(memory_space=pltpu.SMEM)
ANY = pl.BlockSpec(memory_space=pl.ANY)
ALONE = pltpu.CompilerParams(vmem_limit_bytes=57 * 1024 * 1024)
PARAMS = pltpu.CompilerParams(vmem_limit_bytes=24 * 1024 * 1024)


def spot(row, y):
    rank = row + (y % 2) * (NL - 1 - 2 * row)
    x, z = rank // 4, rank % 4
    return 4 * x + z + (x % 2) * (3 - 2 * z)


def device_of(row, comp):
    y = row // NL
    return spot(row % NL, y) * 2 * NY + 2 * y + comp


ROWS = NL * NY
CORE = [(device_of(r, c), device_of(r, 1 - c)) for r in range(ROWS) for c in range(2)]
RAISE = [(device_of(r, c), device_of((r + 1) % ROWS, 1 - c)) for r in range(ROWS) for c in range(2)]
LOWER = [(device_of(r, c), device_of((r - 1) % ROWS, 1 - c)) for r in range(ROWS) for c in range(2)]


def swap(value, pairs):
    return lax.ppermute(value, AXES, pairs)


def exchanges():
    devices = range(NL * 2 * NY)
    even = [(d, d ^ 2) for d in devices]
    odd = [(d, d - d % 8 + (d + (2 if d & 2 else 6)) % 8) for d in devices]
    return [[(d, d ^ 1) for d in devices], even, odd]


def start_all(copies):
    for copy in copies:
        copy.start()
    return copies


def wait_all(copies):
    for copy in copies:
        copy.wait()


def pack_send(place, blocks, send, held, sems):
    entering = start_all([
        pltpu.make_async_copy(blocks.at[0, 1 - place[0], i], held.at[i], sems.at[i]) for i in range(8)
    ])
    leaving = []
    for i in range(8):
        entering[i].wait()
        leaving += start_all([pltpu.make_async_copy(held.at[i], send.at[i], sems.at[8 + i])])
    wait_all(leaving)


def pack_all(place, blocks, extras, received, more, phases, taper, out, phases_out, taper_out, sems):
    core, y = place[0], place[1]
    copies = []
    for i in range(8):
        own, other = spot(8 * core + i, y), spot(8 * (1 - core) + i, y)
        copies += start_all([
            pltpu.make_async_copy(blocks.at[0, core, i], out.at[own, pl.ds(0, W)], sems.at[i]),
            pltpu.make_async_copy(received.at[i], out.at[other, pl.ds(0, W)], sems.at[8 + i]),
        ])
    for i in range(8):
        own, other = spot(8 * core + i, y), spot(8 * (1 - core) + i, y)
        out[own, W:BLOCK, :] = extras[core, i]
        out[other, W:BLOCK, :] = more[i]
    phases_out[...] = phases[...]
    taper_out[...] = taper[...]
    wait_all(copies)


def apply_block(vectors, blocks, layer):
    return lax.dot_general(
        vectors, blocks[layer], (((1,), (1,)), ((), ())), preferred_element_type=F32
    )


def couple(coef, layer, own, diff):
    return coef[layer, 0:1, :] * own + coef[layer, 1:2, :] * diff


def start_kernel(phases, taper, arrived, blocks, forcing, coef, down, up, send, extras, sems):
    edge = pltpu.make_async_copy(arrived.at[:, pl.ds(W, EXTRA)], extras, sems.at[NL])
    edge.start()
    copies = []
    for layer in range(NL):
        copies.append(pltpu.make_async_copy(arrived.at[layer, pl.ds(0, W)], blocks.at[layer], sems.at[layer]))
        copies[layer].start()
    edge.wait()
    for layer in range(NL):
        rows = extras[layer].astype(F32)
        shaped = rows[0:8] * taper[...]
        for m in range(4):
            forcing[layer, 8 * m:8 * m + 8, :] = shaped * phases[layer, m]
        coef[layer, 0:1, :] = rows[8:9] + rows[9:10] + rows[10:11]
        coef[layer, 1:2, :] = rows[11:12] + rows[12:13] + rows[13:14]
    copies[0].wait()
    current = apply_block(forcing[0].astype(BF16), blocks, 0).astype(BF16)
    down[0] = current
    send[0] = current
    for layer in range(1, NL):
        copies[layer].wait()


def phase_kernel(comp, steps, place, blocks, forcing, coef, *refs):
    near = refs[0:1] if comp == 1 else refs[0:2]
    down_in, up_in, down, up, send = refs[len(near):]
    columns = lax.broadcasted_iota(jnp.int32, (NJ, W), 1)

    def differences(slot):
        if comp == 1:
            field = near[0][slot].astype(F32)
            after = jnp.where(columns == W - 1, 0.0, pltpu.roll(field, W - 1, 1))
            before = jnp.where(columns == 0, 0.0, pltpu.roll(field, 1, 1))
            return after - before
        below = jnp.where(place[2] == 0, 0.0, near[0][slot].astype(F32))
        above = jnp.where(place[2] == ROWS - 1, 0.0, near[1][slot].astype(F32))
        return above - below

    @pl.when(place[0] == comp)
    def _():
        for slot, (layer, is_up) in enumerate(steps):
            diff = differences(slot)
            if is_up:
                own = down[layer + 1].astype(F32) if layer == NL - 2 else up[layer + 1]
                image = couple(coef, layer, own, diff).astype(BF16)
                current = down[layer].astype(F32) - apply_block(image, blocks, layer)
                up[layer] = current
                send[slot] = current.astype(BF16)
            else:
                own = down[layer - 1].astype(F32)
                residue = (forcing[layer] - couple(coef, layer, own, diff)).astype(BF16)
                current = apply_block(residue, blocks, layer).astype(BF16)
                down[layer] = current
                send[slot] = current
                if layer == NL - 1:
                    up[layer] = current.astype(F32)

    @pl.when(place[0] != comp)
    def _():
        send[...] = jnp.zeros_like(send)


def phase(comp, steps, place, blocks, forcing, coef, near, down, up):
    first = 4 + len(near)
    return pl.pallas_call(
        functools.partial(phase_kernel, comp, steps),
        out_shape=(
            jax.ShapeDtypeStruct(down.shape, down.dtype),
            jax.ShapeDtypeStruct(up.shape, up.dtype),
            jax.ShapeDtypeStruct((len(steps), NJ, W), BF16),
        ),
        in_specs=[SMEM] + [VMEM] * (5 + len(near)),
        out_specs=(VMEM, VMEM, VMEM),
        input_output_aliases={first: 0, first + 1: 1},
        compiler_params=PARAMS,
    )(place, blocks, forcing, coef, *near, down, up)


def pieces(values):
    out = []
    for _ in range(3):
        part = values.astype(BF16)
        out.append(part)
        values = values - part.astype(F32)
    return out


def gram_kernel(up, send):
    total = jnp.zeros((NJ, NJ), F32)
    for layer in range(NL):
        rows = up[layer]
        total += lax.dot_general(
            rows, rows, (((1,), (1,)), ((), ())),
            precision=lax.Precision.HIGHEST, preferred_element_type=F32,
        )
        send[layer, :, 0:W] = rows.astype(BF16)
    tail = jnp.concatenate(pieces(total) + [jnp.zeros((NJ, NJ), BF16)], axis=1)
    for layer in range(NL):
        send[layer, :, W:W + TAIL] = tail


def collect_kernel(place, rows, gram, send):
    total = jnp.zeros((NJ, TAIL), F32)
    for at in range(NL):
        total += rows[at, :, W:W + TAIL].astype(F32)
    gram[...] = total[:, 0:NJ] + total[:, NJ:2 * NJ] + total[:, 2 * NJ:3 * NJ]
    for i in range(8):
        send[i] = rows[spot(8 * (1 - place[0]) + i, place[1]), :, 0:W]


def final_kernel(place, gram, rows, received, out, triangle):
    lane = lax.broadcasted_iota(jnp.int32, (NJ, NJ), 1)
    row = lax.broadcasted_iota(jnp.int32, (NJ, NJ), 0)
    order = jnp.where(lane == (row % 4) * 8 + row // 4, 1.0, 0.0)
    back = jnp.where(row == (lane % 4) * 8 + lane // 4, 1.0, 0.0)
    exact = functools.partial(jnp.dot, precision=lax.Precision.HIGHEST, preferred_element_type=F32)
    left = exact(exact(order, gram[...] * (1.0 / (NL * 2 * ROWS * W))), back)
    right = order
    for k in range(NJ):
        scale = lax.rsqrt(left[k:k + 1, k:k + 1])
        row_left = left[k:k + 1, :] * scale
        row_right = right[k:k + 1, :] * scale
        factor = jnp.where(row > k, left[:, k:k + 1] * scale, 0.0)
        left = jnp.where(row == k, row_left, left - factor * row_left)
        right = jnp.where(row == k, row_right, right - factor * row_right)
    triangle[...] = jnp.where(lane >= row, left, 0.0)
    core, y = place[0], place[1]
    for i in range(8):
        own = exact(right, rows[spot(8 * core + i, y), :, 0:W].astype(F32))
        other = exact(right, received[i].astype(F32))
        out[0, :, 0, i, :] = jnp.where(core == 0, own, other)
        out[0, :, 1, i, :] = jnp.where(core == 0, other, own)


def per_device(source_modes, port_cells, frequencies, layer_inverse, coupling_self, coupling_curl):
    layer_pos = lax.axis_index("layer")
    tile = lax.axis_index("tile")
    core, y = tile % 2, tile // 2
    x, z = layer_pos // 4, layer_pos % 4
    rank = 4 * x + jnp.where(x % 2 == 0, z, 3 - z)
    row = NL * y + jnp.where(y % 2 == 0, rank, NL - 1 - rank)
    place = jnp.stack([core, y, row, jnp.zeros_like(row)]).astype(jnp.int32)

    def split(values):
        out = []
        for _ in range(3):
            part = lax.reduce_precision(values, 8, 7)
            out.append(part.astype(BF16))
            values = values - part
        return out

    extras = jnp.concatenate(
        [jnp.moveaxis(source_modes[0], 0, 2)]
        + [p[:, :, None] for p in split(coupling_self[0]) + split(coupling_curl[0])]
        + [jnp.zeros((2, 8, EXTRA - 14, W), BF16)],
        axis=2,
    )
    columns = jnp.arange(W, dtype=F32)
    offsets = (columns[None, :] - port_cells.astype(F32)[:, None]) / (W // 8)
    port_taper = 1.0 / (1.0 + offsets * offsets)
    angle = frequencies[None, :] * (jnp.arange(NL, dtype=F32)[:, None] + 1.0)
    phases = jnp.stack([jnp.cos(angle), jnp.sin(angle)], axis=2).reshape(NL, 4)
    to_send = pl.pallas_call(
        pack_send,
        out_shape=jax.ShapeDtypeStruct((8, W, W), BF16),
        in_specs=[SMEM, ANY],
        out_specs=ANY,
        scratch_shapes=[pltpu.VMEM((8, W, W), BF16), pltpu.SemaphoreType.DMA((16,))],
        compiler_params=ALONE,
    )(place, layer_inverse)
    received = swap(to_send, CORE)
    more = swap(lax.dynamic_index_in_dim(extras, 1 - core, 0, keepdims=False), CORE)
    packed, phases, port_taper = pl.pallas_call(
        pack_all,
        out_shape=(
            jax.ShapeDtypeStruct((NL, BLOCK, W), BF16),
            jax.ShapeDtypeStruct(phases.shape, F32),
            jax.ShapeDtypeStruct(port_taper.shape, F32),
        ),
        in_specs=[SMEM, ANY, VMEM, ANY, VMEM, VMEM, VMEM],
        out_specs=(VMEM, VMEM, VMEM),
        scratch_shapes=[pltpu.SemaphoreType.DMA((16,))],
        compiler_params=PARAMS,
    )(place, layer_inverse, extras, received, more, phases, port_taper)
    arrived = lax.all_to_all(packed, "layer", 0, 0, tiled=True)

    blocks, forcing, coef, down, up, first = pl.pallas_call(
        start_kernel,
        out_shape=(
            jax.ShapeDtypeStruct((NL, W, W), BF16),
            jax.ShapeDtypeStruct((NL, NJ, W), F32),
            jax.ShapeDtypeStruct((NL, 2, W), F32),
            jax.ShapeDtypeStruct((NL, NJ, W), BF16),
            jax.ShapeDtypeStruct((NL, NJ, W), F32),
            jax.ShapeDtypeStruct((1, NJ, W), BF16),
        ),
        in_specs=[SMEM, VMEM, ANY],
        out_specs=(VMEM,) * 6,
        scratch_shapes=[pltpu.VMEM((NL, EXTRA, W), BF16), pltpu.SemaphoreType.DMA((NL + 1,))],
        compiler_params=PARAMS,
    )(phases, port_taper, arrived)

    sequence = [(layer, False) for layer in range(NL)] + [(layer, True) for layer in range(NL - 2, -1, -1)]
    run = lambda comp, at, near, down, up: phase(
        comp, sequence[at[0]:at[1]], place, blocks, forcing, coef, near, down, up
    )
    x_sent = swap(first, CORE)
    down, up, y_new = run(1, (1, 2), [x_sent], down, up)
    y_pair = jnp.concatenate([first, y_new])
    at = 1
    last = len(sequence)
    while at < last:
        stop = min(at + 2, last)
        near = [swap(y_pair, RAISE), swap(y_pair, LOWER)]
        down, up, x_pair = run(0, (at, stop), near, down, up)
        y_stop = min(at + 3, last)
        x_sent = swap(x_pair[:y_stop - at - 1], CORE)
        down, up, y_pair = run(1, (at + 1, y_stop), [x_sent], down, up)
        at = stop

    basis = pl.pallas_call(
        gram_kernel,
        out_shape=jax.ShapeDtypeStruct((NL, NJ, W + TAIL), BF16),
        in_specs=[VMEM],
        out_specs=VMEM,
        compiler_params=PARAMS,
    )(up)
    rows = lax.all_to_all(basis, "layer", 0, 0, tiled=True)
    gram, back = pl.pallas_call(
        collect_kernel,
        out_shape=(jax.ShapeDtypeStruct((NJ, NJ), F32), jax.ShapeDtypeStruct((8, NJ, W), BF16)),
        in_specs=[SMEM, VMEM],
        out_specs=(VMEM, VMEM),
        compiler_params=PARAMS,
    )(place, rows)
    received = swap(back, CORE)
    for pairs in exchanges():
        gram = gram + swap(gram, pairs)
    out, triangle = pl.pallas_call(
        final_kernel,
        out_shape=(
            jax.ShapeDtypeStruct((1, NJ, 2, 8, W), F32),
            jax.ShapeDtypeStruct((NJ, NJ), F32),
        ),
        in_specs=[SMEM, VMEM, VMEM, VMEM],
        out_specs=(VMEM, VMEM),
        compiler_params=PARAMS,
    )(place, gram, rows, received)
    return (out, triangle)


def solution(mesh):
    in_specs = (
        P("layer", None, None, "tile", None),
        P(),
        P(),
        P("layer", None, "tile", None, None),
        P("layer", None, "tile", None),
        P("layer", None, "tile", None),
    )
    out_specs = (P("layer", None, None, "tile", None), P())
    return jax.shard_map(
        per_device, mesh=mesh, in_specs=in_specs, out_specs=out_specs, check_vma=False
    )
```

time: 391 us -> 300 us (0.77)
  waiting for transfers between devices: 232 us -> 96.4 us
  blocking collectives: 12.7 us -> 123 us
  starting transfers between devices: 67.6 us -> 33.4 us
  Pallas kernels: 53.8 us -> 41 us
  local copies, waits for them, and re-layouts: 16.5 us -> 3.96 us
    all_to_all x1 -> x0, waiting for transfers between devices: 150 us -> none  [per_device(): arrived = lax.all_to_all(packed, 'layer', 0, 0, tiled=True)]
    all_to_all x0 -> x1, blocking collectives: none -> 106 us  [per_device(): arrived = lax.all_to_all(packed, 'layer', 0, 0, tiled=True)]
    ppermute x55 -> x52, starting transfers between devices: 59.5 us -> 33.4 us  [swap(): return lax.ppermute(value, AXES, pairs)]
    ppermute x55 -> x52, waiting for transfers between devices: 82.3 us -> 96.4 us  [swap(): return lax.ppermute(value, AXES, pairs)]
    pallas_call x8 -> x6, Pallas kernels: 29.4 us -> 16.5 us  [the longest x1 5.63 us: per_device(): pl.pallas_call(final_kernel, out_shape=(jax.ShapeDtypeStruct((1, NJ, 2, 8...]
    all_to_all x1 -> x0, starting transfers between devices: 8.14 us -> none  [per_device(): arrived = lax.all_to_all(packed, 'layer', 0, 0, tiled=True)]
    slice x1 -> x0, local copies, waits for them, and re-layouts: 7.48 us -> none  [per_device(): blocks = arrived[:, 0:W]]
  transfers between devices with their start and end apart: 56 -> 52, of which waited for: 49 -> 51; matrix products, arithmetic and copies ran while one was open for 0% -> 0% of each run, Pallas kernels for 2% -> 0%
where the time goes in v2:
time: 300 us
  blocking collectives  123 us (41%)
  waiting for transfers between devices  96.4 us (32%)
  Pallas kernels  41 us (14%)
  starting transfers between devices  33.4 us (11%)
  local copies, waits for them, and re-layouts  3.96 us (1%)
    all_to_all x1, blocking collectives, per_device(): arrived = lax.all_to_all(packed, 'layer', 0, 0, tiled=True)  106 us
    ppermute x52, waiting for transfers between devices, swap(): return lax.ppermute(value, AXES, pairs)  96.4 us
    ppermute x52, starting transfers between devices, swap(): return lax.ppermute(value, AXES, pairs)  33.4 us
    pallas_call x31, Pallas kernels, phase(): pl.pallas_call(functools.partial(phase_kernel, comp, steps), out_shape=(j...  24.4 us
    all_to_all x1, blocking collectives, per_device(): rows = lax.all_to_all(basis, 'layer', 0, 0, tiled=True)  16.2 us
  transfers between devices with their start and end apart: 52, of which 51 were waited for; matrix products, arithmetic and copies ran while one was open for 0% of the time, Pallas kernels for 0%

profile of v2, /device:TPU:0, one launch (start us, length us, event | category | flops | bytes accessed | tf_op | source)
XLA Modules:
  0.0 299.8 jit_solution(5075672012283577321)
XLA Ops:
  1.4 4.4 %shard_map.77 = bf16[8,512,512]{2,1,0:T(8,128)(2,1)} custom-call(s32[4]{0:T(128)} %pad_add_fusion.place, bf16[1,2,8,512,512]{4,3,2,1,0:T(8,128)(2,1)} %blocks.3), custom_call_target="tpu_custom_call" | custom-call | tf_op jit(solution)/shard_map/pallas_call | solution.py:267
  7.4 5.7 %collective-permute-done.1.more = bf16[8,16,512]{2,1,0:T(8,128)(2,1)S(1)} collective-permute-done((bf16[8,16,512]{2,1,0:T(8,128)(2,1)S(1)}, bf16[8,16,512]{2,1,0:T(8,128)(2,1)S(1)}, u32[]{:S(2)}, u32[]{:S(2)}) %collective-permute-start.1) | collective-permute-done | bytes 131104 | tf_op jit(solution)/shard_map/ppermute | solution.py:45
  13.3 3.4 %copy-done = bf16[1,2,8,512,512]{4,3,2,1,0:T(8,128)(2,1)S(1)} copy-done((bf16[1,2,8,512,512]{4,3,2,1,0:T(8,128)(2,1)S(1)}, bf16[1,2,8,512,512]{4,3,2,1,0:T(8,128)(2,1)}, u32[]{:S(2)}) %copy-start) | copy-done | bytes 8388632
  16.7 3.0 shard_map.78
  19.7 106.5 %all_to_all.10.arrived = bf16[16,528,512]{2,1,0:T(8,128)(2,1)S(1)} all-to-all(bf16[16,528,512]{2,1,0:T(8,128)(2,1)S(1)} %get-tuple-element.106), channel_id=1, replica_groups=mesh['layer'=16,'tile'=8] {'layer'}, dimensions={0} | all-to-all | bytes 17301504 | tf_op jit(solution)/shard_map/all_to_all | solution.py:289
  126.2 1.8 shard_map.79
  129.9 3.1 %collective-permute-start.4 = (bf16[2,32,512]{2,1,0:T(8,128)(2,1)S(1)}, bf16[2,32,512]{2,1,0:T(8,128)(2,1)S(1)}, u32[]{:S(2)}, u32[]{:S(2)}) collective-permute-start(bf16[2,32,512]{2,1,0:T(8,128)(2,1)S(1)} %constant_dynamic-update-slice_fusion), channel_id=1, source_target_pairs={{0,7},{1,6},{8,1},{9,0},{16,9},{17,8},{24,17},{25,16},{56,25},{57,... | collective-permute-start | bytes 196616 | tf_op jit(solution)/shard_map/ppermute | solution.py:45
  133.0 1.9 collective-permute-done.4.refs_1_
  134.9 3.4 %collective-permute-done.3.refs_0_ = bf16[2,32,512]{2,1,0:T(8,128)(2,1)S(1)} collective-permute-done((bf16[2,32,512]{2,1,0:T(8,128)(2,1)S(1)}, bf16[2,32,512]{2,1,0:T(8,128)(2,1)S(1)}, u32[]{:S(2)}, u32[]{:S(2)}) %collective-permute-start.3) | collective-permute-done | bytes 65568 | tf_op jit(solution)/shard_map/ppermute | solution.py:45
  141.3 1.7 collective-permute-start.6
  143.0 1.9 collective-permute-done.7.refs_1_
  151.0 1.9 collective-permute-done.10.refs_1_
  152.9 3.0 %collective-permute-done.9.refs_0_ = bf16[2,32,512]{2,1,0:T(8,128)(2,1)S(1)} collective-permute-done((bf16[2,32,512]{2,1,0:T(8,128)(2,1)S(1)}, bf16[2,32,512]{2,1,0:T(8,128)(2,1)S(1)}, u32[]{:S(2)}, u32[]{:S(2)}) %collective-permute-start.9) | collective-permute-done | bytes 65568 | tf_op jit(solution)/shard_map/ppermute | solution.py:45
  158.9 1.7 collective-permute-start.12
  160.6 1.9 collective-permute-done.13.refs_1_
  162.6 1.3 collective-permute-done.12.refs_0_
  168.6 1.9 collective-permute-done.16.refs_1_
  170.5 3.0 %collective-permute-done.15.refs_0_ = bf16[2,32,512]{2,1,0:T(8,128)(2,1)S(1)} collective-permute-done((bf16[2,32,512]{2,1,0:T(8,128)(2,1)S(1)}, bf16[2,32,512]{2,1,0:T(8,128)(2,1)S(1)}, u32[]{:S(2)}, u32[]{:S(2)}) %collective-permute-start.15) | collective-permute-done | bytes 65568 | tf_op jit(solution)/shard_map/ppermute | solution.py:45
  176.5 1.7 collective-permute-start.18
  178.2 1.9 collective-permute-done.19.refs_1_
  184.3 1.4 collective-permute-start.22
  186.4 1.9 collective-permute-done.22.refs_1_
  188.3 3.0 %collective-permute-done.21.refs_0_ = bf16[2,32,512]{2,1,0:T(8,128)(2,1)S(1)} collective-permute-done((bf16[2,32,512]{2,1,0:T(8,128)(2,1)S(1)}, bf16[2,32,512]{2,1,0:T(8,128)(2,1)S(1)}, u32[]{:S(2)}, u32[]{:S(2)}) %collective-permute-start.21) | collective-permute-done | bytes 65568 | tf_op jit(solution)/shard_map/ppermute | solution.py:45
  194.2 1.7 collective-permute-start.24
  196.0 1.9 collective-permute-done.25.refs_1_
  197.9 1.3 collective-permute-done.24.refs_0_
  202.1 1.4 collective-permute-start.28
  204.1 1.9 collective-permute-done.28.refs_1_
  206.0 3.1 %collective-permute-done.27.refs_0_ = bf16[2,32,512]{2,1,0:T(8,128)(2,1)S(1)} collective-permute-done((bf16[2,32,512]{2,1,0:T(8,128)(2,1)S(1)}, bf16[2,32,512]{2,1,0:T(8,128)(2,1)S(1)}, u32[]{:S(2)}, u32[]{:S(2)}) %collective-permute-start.27) | collective-permute-done | bytes 65568 | tf_op jit(solution)/shard_map/ppermute | solution.py:45
  212.0 1.7 collective-permute-start.30
  213.8 1.9 collective-permute-done.31.refs_1_
  219.9 1.4 collective-permute-start.34
  221.9 1.9 collective-permute-done.34.refs_1_
  223.8 3.1 %collective-permute-done.33.refs_0_ = bf16[2,32,512]{2,1,0:T(8,128)(2,1)S(1)} collective-permute-done((bf16[2,32,512]{2,1,0:T(8,128)(2,1)S(1)}, bf16[2,32,512]{2,1,0:T(8,128)(2,1)S(1)}, u32[]{:S(2)}, u32[]{:S(2)}) %collective-permute-start.33) | collective-permute-done | bytes 65568 | tf_op jit(solution)/shard_map/ppermute | solution.py:45
  229.8 1.7 collective-permute-start.36
  231.5 1.9 collective-permute-done.37.refs_1_
  237.7 1.4 collective-permute-start.40
  239.7 1.9 collective-permute-done.40.refs_1_
  241.5 3.1 %collective-permute-done.39.refs_0_ = bf16[2,32,512]{2,1,0:T(8,128)(2,1)S(1)} collective-permute-done((bf16[2,32,512]{2,1,0:T(8,128)(2,1)S(1)}, bf16[2,32,512]{2,1,0:T(8,128)(2,1)S(1)}, u32[]{:S(2)}, u32[]{:S(2)}) %collective-permute-start.39) | collective-permute-done | bytes 65568 | tf_op jit(solution)/shard_map/ppermute | solution.py:45
  247.6 1.7 collective-permute-start.42
  249.3 1.9 collective-permute-done.43.refs_1_
  255.5 1.4 collective-permute-start.46
  257.6 1.6 collective-permute-done.46.refs_1_
  259.3 3.1 %collective-permute-done.45.refs_0_ = bf16[2,32,512]{2,1,0:T(8,128)(2,1)S(1)} collective-permute-done((bf16[2,32,512]{2,1,0:T(8,128)(2,1)S(1)}, bf16[2,32,512]{2,1,0:T(8,128)(2,1)S(1)}, u32[]{:S(2)}, u32[]{:S(2)}) %collective-permute-start.45) | collective-permute-done | bytes 65568 | tf_op jit(solution)/shard_map/ppermute | solution.py:45
  266.9 16.2 %all_to_all.11.rows = bf16[16,32,640]{2,1,0:T(8,128)(2,1)S(1)} all-to-all(bf16[16,32,640]{2,1,0:T(8,128)(2,1)S(1)} %shard_map.111), channel_id=1, replica_groups=mesh['layer'=16,'tile'=8] {'layer'}, dimensions={0} | all-to-all | bytes 1310720 | tf_op jit(solution)/shard_map/all_to_all | solution.py:332
  285.4 3.7 %collective-permute-done.49 = f32[32,32]{1,0:T(8,128)S(1)} collective-permute-done((f32[32,32]{1,0:T(8,128)S(1)}, f32[32,32]{1,0:T(8,128)S(1)}, u32[]{:S(2)}, u32[]{:S(2)}) %collective-permute-start.49) | collective-permute-done | bytes 4128 | tf_op jit(solution)/shard_map/ppermute | solution.py:45
  289.2 4.9 %collective-permute-done.50 = f32[32,32]{1,0:T(8,128)S(1)} collective-permute-done((f32[32,32]{1,0:T(8,128)S(1)}, f32[32,32]{1,0:T(8,128)S(1)}, u32[]{:S(2)}, u32[]{:S(2)}) %collective-permute-start.50) | collective-permute-done | bytes 4128 | tf_op jit(solution)/shard_map/ppermute | solution.py:45
  294.1 5.6 %shard_map.113 = (f32[1,32,2,8,512]{4,3,2,1,0:T(8,128)}, f32[32,32]{1,0:T(8,128)}) custom-call(s32[4]{0:T(128)S(1)} %copy-done.1, f32[32,32]{1,0:T(8,128)S(1)} %add.57.gram, bf16[16,32,640]{2,1,0:T(8,128)(2,1)S(1)} %all_to_all.11.rows, bf16[8,32,512]{2,1,0:T(8,128)(2,1)S(1)} %collective-permute-done.51.received), custom_call_target="tpu_custom_call" | custom-call | tf_op jit(solution)/shard_map/pallas_call | solution.py:343
  (127 shorter events, 65.4 us)
Async XLA Ops:
  5.8 7.6 %collective-permute-start = (bf16[8,512,512]{2,1,0:T(8,128)(2,1)}, bf16[8,512,512]{2,1,0:T(8,128)(2,1)}, u32[]{:S(2)}, u32[]{:S(2)}) collective-permute-start(bf16[8,512,512]{2,1,0:T(8,128)(2,1)} %shard_map.77), channel_id=1, source_target_pairs={{0,1},{1,0},{8,9},{9,8},{16,17},{17,16},{24,25},{25,24},{56,57},{5... | collective-permute-start | bytes 12582920 | tf_op jit(solution)/shard_map/ppermute | solution.py:45
  6.6 6.6 %collective-permute-start.1 = (bf16[8,16,512]{2,1,0:T(8,128)(2,1)S(1)}, bf16[8,16,512]{2,1,0:T(8,128)(2,1)S(1)}, u32[]{:S(2)}, u32[]{:S(2)}) collective-permute-start(bf16[8,16,512]{2,1,0:T(8,128)(2,1)S(1)} %dynamic-slice_bitcast_fusion), channel_id=1, source_target_pairs={{0,1},{1,0},{8,9},{9,8},{16,17},{17,16},{24,25},{25,24},{56,57},{5... | collective-permute-start | bytes 393224 | tf_op jit(solution)/shard_map/ppermute | solution.py:45
  129.9 5.0 %collective-permute-start.4 = (bf16[2,32,512]{2,1,0:T(8,128)(2,1)S(1)}, bf16[2,32,512]{2,1,0:T(8,128)(2,1)S(1)}, u32[]{:S(2)}, u32[]{:S(2)}) collective-permute-start(bf16[2,32,512]{2,1,0:T(8,128)(2,1)S(1)} %constant_dynamic-update-slice_fusion), channel_id=1, source_target_pairs={{0,7},{1,6},{8,1},{9,0},{16,9},{17,8},{24,17},{25,16},{56,25},{57,... | collective-permute-start | bytes 196616 | tf_op jit(solution)/shard_map/ppermute | solution.py:45
  133.0 5.3 %collective-permute-start.3 = (bf16[2,32,512]{2,1,0:T(8,128)(2,1)S(1)}, bf16[2,32,512]{2,1,0:T(8,128)(2,1)S(1)}, u32[]{:S(2)}, u32[]{:S(2)}) collective-permute-start(bf16[2,32,512]{2,1,0:T(8,128)(2,1)S(1)} %constant_dynamic-update-slice_fusion), channel_id=1, source_target_pairs={{0,9},{1,8},{8,17},{9,16},{16,25},{17,24},{24,57},{25,56},{56,49},... | collective-permute-start | bytes 196616 | tf_op jit(solution)/shard_map/ppermute | solution.py:45
  139.3 1.3 collective-permute-start.5
  141.2 3.8 %collective-permute-start.7 = (bf16[2,32,512]{2,1,0:T(8,128)(2,1)S(1)}, bf16[2,32,512]{2,1,0:T(8,128)(2,1)S(1)}, u32[]{:S(2)}, u32[]{:S(2)}) collective-permute-start(bf16[2,32,512]{2,1,0:T(8,128)(2,1)S(1)} %get-tuple-element.119), channel_id=1, source_target_pairs={{0,7},{1,6},{8,1},{9,0},{16,9},{17,8},{24,17},{25,16},{56,25},{57,... | collective-permute-start | bytes 196616 | tf_op jit(solution)/shard_map/ppermute | solution.py:45
  141.3 5.0 %collective-permute-start.6 = (bf16[2,32,512]{2,1,0:T(8,128)(2,1)S(1)}, bf16[2,32,512]{2,1,0:T(8,128)(2,1)S(1)}, u32[]{:S(2)}, u32[]{:S(2)}) collective-permute-start(bf16[2,32,512]{2,1,0:T(8,128)(2,1)S(1)} %get-tuple-element.119), channel_id=1, source_target_pairs={{0,9},{1,8},{8,17},{9,16},{16,25},{17,24},{24,57},{25,56},{56,49},... | collective-permute-start | bytes 196616 | tf_op jit(solution)/shard_map/ppermute | solution.py:45
  147.3 1.3 collective-permute-start.8
  149.2 3.8 %collective-permute-start.10 = (bf16[2,32,512]{2,1,0:T(8,128)(2,1)S(1)}, bf16[2,32,512]{2,1,0:T(8,128)(2,1)S(1)}, u32[]{:S(2)}, u32[]{:S(2)}) collective-permute-start(bf16[2,32,512]{2,1,0:T(8,128)(2,1)S(1)} %get-tuple-element.125), channel_id=1, source_target_pairs={{0,7},{1,6},{8,1},{9,0},{16,9},{17,8},{24,17},{25,16},{56,25},{57,... | collective-permute-start | bytes 196616 | tf_op jit(solution)/shard_map/ppermute | solution.py:45
  150.4 5.5 %collective-permute-start.9 = (bf16[2,32,512]{2,1,0:T(8,128)(2,1)S(1)}, bf16[2,32,512]{2,1,0:T(8,128)(2,1)S(1)}, u32[]{:S(2)}, u32[]{:S(2)}) collective-permute-start(bf16[2,32,512]{2,1,0:T(8,128)(2,1)S(1)} %get-tuple-element.125), channel_id=1, source_target_pairs={{0,9},{1,8},{8,17},{9,16},{16,25},{17,24},{24,57},{25,56},{56,49},... | collective-permute-start | bytes 196616 | tf_op jit(solution)/shard_map/ppermute | solution.py:45
  156.9 1.3 collective-permute-start.11
  158.8 3.8 %collective-permute-start.13 = (bf16[2,32,512]{2,1,0:T(8,128)(2,1)S(1)}, bf16[2,32,512]{2,1,0:T(8,128)(2,1)S(1)}, u32[]{:S(2)}, u32[]{:S(2)}) collective-permute-start(bf16[2,32,512]{2,1,0:T(8,128)(2,1)S(1)} %get-tuple-element.131), channel_id=1, source_target_pairs={{0,7},{1,6},{8,1},{9,0},{16,9},{17,8},{24,17},{25,16},{56,25},{57,... | collective-permute-start | bytes 196616 | tf_op jit(solution)/shard_map/ppermute | solution.py:45
  158.9 5.0 %collective-permute-start.12 = (bf16[2,32,512]{2,1,0:T(8,128)(2,1)S(1)}, bf16[2,32,512]{2,1,0:T(8,128)(2,1)S(1)}, u32[]{:S(2)}, u32[]{:S(2)}) collective-permute-start(bf16[2,32,512]{2,1,0:T(8,128)(2,1)S(1)} %get-tuple-element.131), channel_id=1, source_target_pairs={{0,9},{1,8},{8,17},{9,16},{16,25},{17,24},{24,57},{25,56},{56,49},... | collective-permute-start | bytes 196616 | tf_op jit(solution)/shard_map/ppermute | solution.py:45
  164.8 1.3 collective-permute-start.14
  166.8 3.8 %collective-permute-start.16 = (bf16[2,32,512]{2,1,0:T(8,128)(2,1)S(1)}, bf16[2,32,512]{2,1,0:T(8,128)(2,1)S(1)}, u32[]{:S(2)}, u32[]{:S(2)}) collective-permute-start(bf16[2,32,512]{2,1,0:T(8,128)(2,1)S(1)} %get-tuple-element.137), channel_id=1, source_target_pairs={{0,7},{1,6},{8,1},{9,0},{16,9},{17,8},{24,17},{25,16},{56,25},{57,... | collective-permute-start | bytes 196616 | tf_op jit(solution)/shard_map/ppermute | solution.py:45
  168.0 5.5 %collective-permute-start.15 = (bf16[2,32,512]{2,1,0:T(8,128)(2,1)S(1)}, bf16[2,32,512]{2,1,0:T(8,128)(2,1)S(1)}, u32[]{:S(2)}, u32[]{:S(2)}) collective-permute-start(bf16[2,32,512]{2,1,0:T(8,128)(2,1)S(1)} %get-tuple-element.137), channel_id=1, source_target_pairs={{0,9},{1,8},{8,17},{9,16},{16,25},{17,24},{24,57},{25,56},{56,49},... | collective-permute-start | bytes 196616 | tf_op jit(solution)/shard_map/ppermute | solution.py:45
  174.5 1.3 collective-permute-start.17
  176.4 3.8 %collective-permute-start.19 = (bf16[2,32,512]{2,1,0:T(8,128)(2,1)S(1)}, bf16[2,32,512]{2,1,0:T(8,128)(2,1)S(1)}, u32[]{:S(2)}, u32[]{:S(2)}) collective-permute-start(bf16[2,32,512]{2,1,0:T(8,128)(2,1)S(1)} %get-tuple-element.143), channel_id=1, source_target_pairs={{0,7},{1,6},{8,1},{9,0},{16,9},{17,8},{24,17},{25,16},{56,25},{57,... | collective-permute-start | bytes 196616 | tf_op jit(solution)/shard_map/ppermute | solution.py:45
  176.5 5.0 %collective-permute-start.18 = (bf16[2,32,512]{2,1,0:T(8,128)(2,1)S(1)}, bf16[2,32,512]{2,1,0:T(8,128)(2,1)S(1)}, u32[]{:S(2)}, u32[]{:S(2)}) collective-permute-start(bf16[2,32,512]{2,1,0:T(8,128)(2,1)S(1)} %get-tuple-element.143), channel_id=1, source_target_pairs={{0,9},{1,8},{8,17},{9,16},{16,25},{17,24},{24,57},{25,56},{56,49},... | collective-permute-start | bytes 196616 | tf_op jit(solution)/shard_map/ppermute | solution.py:45
  182.4 1.3 collective-permute-start.20
  184.3 3.9 %collective-permute-start.22 = (bf16[2,32,512]{2,1,0:T(8,128)(2,1)S(1)}, bf16[2,32,512]{2,1,0:T(8,128)(2,1)S(1)}, u32[]{:S(2)}, u32[]{:S(2)}) collective-permute-start(bf16[2,32,512]{2,1,0:T(8,128)(2,1)S(1)} %get-tuple-element.149), channel_id=1, source_target_pairs={{0,7},{1,6},{8,1},{9,0},{16,9},{17,8},{24,17},{25,16},{56,25},{57,... | collective-permute-start | bytes 196616 | tf_op jit(solution)/shard_map/ppermute | solution.py:45
  185.8 5.5 %collective-permute-start.21 = (bf16[2,32,512]{2,1,0:T(8,128)(2,1)S(1)}, bf16[2,32,512]{2,1,0:T(8,128)(2,1)S(1)}, u32[]{:S(2)}, u32[]{:S(2)}) collective-permute-start(bf16[2,32,512]{2,1,0:T(8,128)(2,1)S(1)} %get-tuple-element.149), channel_id=1, source_target_pairs={{0,9},{1,8},{8,17},{9,16},{16,25},{17,24},{24,57},{25,56},{56,49},... | collective-permute-start | bytes 196616 | tf_op jit(solution)/shard_map/ppermute | solution.py:45
  192.3 1.3 collective-permute-start.23
  194.2 3.8 %collective-permute-start.25 = (bf16[2,32,512]{2,1,0:T(8,128)(2,1)S(1)}, bf16[2,32,512]{2,1,0:T(8,128)(2,1)S(1)}, u32[]{:S(2)}, u32[]{:S(2)}) collective-permute-start(bf16[2,32,512]{2,1,0:T(8,128)(2,1)S(1)} %get-tuple-element.155), channel_id=1, source_target_pairs={{0,7},{1,6},{8,1},{9,0},{16,9},{17,8},{24,17},{25,16},{56,25},{57,... | collective-permute-start | bytes 196616 | tf_op jit(solution)/shard_map/ppermute | solution.py:45
  194.2 5.0 %collective-permute-start.24 = (bf16[2,32,512]{2,1,0:T(8,128)(2,1)S(1)}, bf16[2,32,512]{2,1,0:T(8,128)(2,1)S(1)}, u32[]{:S(2)}, u32[]{:S(2)}) collective-permute-start(bf16[2,32,512]{2,1,0:T(8,128)(2,1)S(1)} %get-tuple-element.155), channel_id=1, source_target_pairs={{0,9},{1,8},{8,17},{9,16},{16,25},{17,24},{24,57},{25,56},{56,49},... | collective-permute-start | bytes 196616 | tf_op jit(solution)/shard_map/ppermute | solution.py:45
  200.2 1.3 collective-permute-start.26
  202.1 3.9 %collective-permute-start.28 = (bf16[2,32,512]{2,1,0:T(8,128)(2,1)S(1)}, bf16[2,32,512]{2,1,0:T(8,128)(2,1)S(1)}, u32[]{:S(2)}, u32[]{:S(2)}) collective-permute-start(bf16[2,32,512]{2,1,0:T(8,128)(2,1)S(1)} %get-tuple-element.161), channel_id=1, source_target_pairs={{0,7},{1,6},{8,1},{9,0},{16,9},{17,8},{24,17},{25,16},{56,25},{57,... | collective-permute-start | bytes 196616 | tf_op jit(solution)/shard_map/ppermute | solution.py:45
  203.5 5.5 %collective-permute-start.27 = (bf16[2,32,512]{2,1,0:T(8,128)(2,1)S(1)}, bf16[2,32,512]{2,1,0:T(8,128)(2,1)S(1)}, u32[]{:S(2)}, u32[]{:S(2)}) collective-permute-start(bf16[2,32,512]{2,1,0:T(8,128)(2,1)S(1)} %get-tuple-element.161), channel_id=1, source_target_pairs={{0,9},{1,8},{8,17},{9,16},{16,25},{17,24},{24,57},{25,56},{56,49},... | collective-permute-start | bytes 196616 | tf_op jit(solution)/shard_map/ppermute | solution.py:45
  210.1 1.3 collective-permute-start.29
  212.0 3.8 %collective-permute-start.31 = (bf16[2,32,512]{2,1,0:T(8,128)(2,1)S(1)}, bf16[2,32,512]{2,1,0:T(8,128)(2,1)S(1)}, u32[]{:S(2)}, u32[]{:S(2)}) collective-permute-start(bf16[2,32,512]{2,1,0:T(8,128)(2,1)S(1)} %get-tuple-element.167), channel_id=1, source_target_pairs={{0,7},{1,6},{8,1},{9,0},{16,9},{17,8},{24,17},{25,16},{56,25},{57,... | collective-permute-start | bytes 196616 | tf_op jit(solution)/shard_map/ppermute | solution.py:45
  212.0 5.0 %collective-permute-start.30 = (bf16[2,32,512]{2,1,0:T(8,128)(2,1)S(1)}, bf16[2,32,512]{2,1,0:T(8,128)(2,1)S(1)}, u32[]{:S(2)}, u32[]{:S(2)}) collective-permute-start(bf16[2,32,512]{2,1,0:T(8,128)(2,1)S(1)} %get-tuple-element.167), channel_id=1, source_target_pairs={{0,9},{1,8},{8,17},{9,16},{16,25},{17,24},{24,57},{25,56},{56,49},... | collective-permute-start | bytes 196616 | tf_op jit(solution)/shard_map/ppermute | solution.py:45
  218.0 1.3 collective-permute-start.32
  219.9 3.8 %collective-permute-start.34 = (bf16[2,32,512]{2,1,0:T(8,128)(2,1)S(1)}, bf16[2,32,512]{2,1,0:T(8,128)(2,1)S(1)}, u32[]{:S(2)}, u32[]{:S(2)}) collective-permute-start(bf16[2,32,512]{2,1,0:T(8,128)(2,1)S(1)} %get-tuple-element.173), channel_id=1, source_target_pairs={{0,7},{1,6},{8,1},{9,0},{16,9},{17,8},{24,17},{25,16},{56,25},{57,... | collective-permute-start | bytes 196616 | tf_op jit(solution)/shard_map/ppermute | solution.py:45
  221.3 5.5 %collective-permute-start.33 = (bf16[2,32,512]{2,1,0:T(8,128)(2,1)S(1)}, bf16[2,32,512]{2,1,0:T(8,128)(2,1)S(1)}, u32[]{:S(2)}, u32[]{:S(2)}) collective-permute-start(bf16[2,32,512]{2,1,0:T(8,128)(2,1)S(1)} %get-tuple-element.173), channel_id=1, source_target_pairs={{0,9},{1,8},{8,17},{9,16},{16,25},{17,24},{24,57},{25,56},{56,49},... | collective-permute-start | bytes 196616 | tf_op jit(solution)/shard_map/ppermute | solution.py:45
  227.8 1.3 collective-permute-start.35
  229.7 3.8 %collective-permute-start.37 = (bf16[2,32,512]{2,1,0:T(8,128)(2,1)S(1)}, bf16[2,32,512]{2,1,0:T(8,128)(2,1)S(1)}, u32[]{:S(2)}, u32[]{:S(2)}) collective-permute-start(bf16[2,32,512]{2,1,0:T(8,128)(2,1)S(1)} %get-tuple-element.179), channel_id=1, source_target_pairs={{0,7},{1,6},{8,1},{9,0},{16,9},{17,8},{24,17},{25,16},{56,25},{57,... | collective-permute-start | bytes 196616 | tf_op jit(solution)/shard_map/ppermute | solution.py:45
  229.8 5.0 %collective-permute-start.36 = (bf16[2,32,512]{2,1,0:T(8,128)(2,1)S(1)}, bf16[2,32,512]{2,1,0:T(8,128)(2,1)S(1)}, u32[]{:S(2)}, u32[]{:S(2)}) collective-permute-start(bf16[2,32,512]{2,1,0:T(8,128)(2,1)S(1)} %get-tuple-element.179), channel_id=1, source_target_pairs={{0,9},{1,8},{8,17},{9,16},{16,25},{17,24},{24,57},{25,56},{56,49},... | collective-permute-start | bytes 196616 | tf_op jit(solution)/shard_map/ppermute | solution.py:45
  237.7 3.8 %collective-permute-start.40 = (bf16[2,32,512]{2,1,0:T(8,128)(2,1)S(1)}, bf16[2,32,512]{2,1,0:T(8,128)(2,1)S(1)}, u32[]{:S(2)}, u32[]{:S(2)}) collective-permute-start(bf16[2,32,512]{2,1,0:T(8,128)(2,1)S(1)} %get-tuple-element.185), channel_id=1, source_target_pairs={{0,7},{1,6},{8,1},{9,0},{16,9},{17,8},{24,17},{25,16},{56,25},{57,... | collective-permute-start | bytes 196616 | tf_op jit(solution)/shard_map/ppermute | solution.py:45
  239.0 5.5 %collective-permute-start.39 = (bf16[2,32,512]{2,1,0:T(8,128)(2,1)S(1)}, bf16[2,32,512]{2,1,0:T(8,128)(2,1)S(1)}, u32[]{:S(2)}, u32[]{:S(2)}) collective-permute-start(bf16[2,32,512]{2,1,0:T(8,128)(2,1)S(1)} %get-tuple-element.185), channel_id=1, source_target_pairs={{0,9},{1,8},{8,17},{9,16},{16,25},{17,24},{24,57},{25,56},{56,49},... | collective-permute-start | bytes 196616 | tf_op jit(solution)/shard_map/ppermute | solution.py:45
  245.6 1.3 collective-permute-start.41
  247.5 3.8 %collective-permute-start.43 = (bf16[2,32,512]{2,1,0:T(8,128)(2,1)S(1)}, bf16[2,32,512]{2,1,0:T(8,128)(2,1)S(1)}, u32[]{:S(2)}, u32[]{:S(2)}) collective-permute-start(bf16[2,32,512]{2,1,0:T(8,128)(2,1)S(1)} %get-tuple-element.191), channel_id=1, source_target_pairs={{0,7},{1,6},{8,1},{9,0},{16,9},{17,8},{24,17},{25,16},{56,25},{57,... | collective-permute-start | bytes 196616 | tf_op jit(solution)/shard_map/ppermute | solution.py:45
  247.6 5.0 %collective-permute-start.42 = (bf16[2,32,512]{2,1,0:T(8,128)(2,1)S(1)}, bf16[2,32,512]{2,1,0:T(8,128)(2,1)S(1)}, u32[]{:S(2)}, u32[]{:S(2)}) collective-permute-start(bf16[2,32,512]{2,1,0:T(8,128)(2,1)S(1)} %get-tuple-element.191), channel_id=1, source_target_pairs={{0,9},{1,8},{8,17},{9,16},{16,25},{17,24},{24,57},{25,56},{56,49},... | collective-permute-start | bytes 196616 | tf_op jit(solution)/shard_map/ppermute | solution.py:45
  255.5 3.8 %collective-permute-start.46 = (bf16[2,32,512]{2,1,0:T(8,128)(2,1)S(1)}, bf16[2,32,512]{2,1,0:T(8,128)(2,1)S(1)}, u32[]{:S(2)}, u32[]{:S(2)}) collective-permute-start(bf16[2,32,512]{2,1,0:T(8,128)(2,1)S(1)} %get-tuple-element.197), channel_id=1, source_target_pairs={{0,7},{1,6},{8,1},{9,0},{16,9},{17,8},{24,17},{25,16},{56,25},{57,... | collective-permute-start | bytes 196616 | tf_op jit(solution)/shard_map/ppermute | solution.py:45
  256.8 5.5 %collective-permute-start.45 = (bf16[2,32,512]{2,1,0:T(8,128)(2,1)S(1)}, bf16[2,32,512]{2,1,0:T(8,128)(2,1)S(1)}, u32[]{:S(2)}, u32[]{:S(2)}) collective-permute-start(bf16[2,32,512]{2,1,0:T(8,128)(2,1)S(1)} %get-tuple-element.197), channel_id=1, source_target_pairs={{0,9},{1,8},{8,17},{9,16},{16,25},{17,24},{24,57},{25,56},{56,49},... | collective-permute-start | bytes 196616 | tf_op jit(solution)/shard_map/ppermute | solution.py:45
  283.8 10.3 %collective-permute-start.51 = (bf16[8,32,512]{2,1,0:T(8,128)(2,1)S(1)}, bf16[8,32,512]{2,1,0:T(8,128)(2,1)S(1)}, u32[]{:S(2)}, u32[]{:S(2)}) collective-permute-start(bf16[8,32,512]{2,1,0:T(8,128)(2,1)S(1)} %get-tuple-element.205), channel_id=1, source_target_pairs={{0,1},{1,0},{8,9},{9,8},{16,17},{17,16},{24,25},{25,24},{56,57},{5... | collective-permute-start | bytes 786440 | tf_op jit(solution)/shard_map/ppermute | solution.py:45
  283.9 1.5 collective-permute-start.48
  285.4 3.7 %collective-permute-start.49 = (f32[32,32]{1,0:T(8,128)S(1)}, f32[32,32]{1,0:T(8,128)S(1)}, u32[]{:S(2)}, u32[]{:S(2)}) collective-permute-start(f32[32,32]{1,0:T(8,128)S(1)} %add.55), channel_id=1, source_target_pairs={{0,2},{1,3},{2,0},{3,1},{4,6},{5,7},{6,4},{7,5},{8,10},{9,11},{10,... | collective-permute-start | bytes 12296 | tf_op jit(solution)/shard_map/ppermute | solution.py:45
  289.2 4.9 %collective-permute-start.50 = (f32[32,32]{1,0:T(8,128)S(1)}, f32[32,32]{1,0:T(8,128)S(1)}, u32[]{:S(2)}, u32[]{:S(2)}) collective-permute-start(f32[32,32]{1,0:T(8,128)S(1)} %add.56), channel_id=1, source_target_pairs={{0,6},{1,7},{2,4},{3,5},{4,2},{5,3},{6,0},{7,1},{8,14},{9,15},{10,... | collective-permute-start | bytes 12296 | tf_op jit(solution)/shard_map/ppermute | solution.py:45
  (11 other events, 49.4 us)

commit v3 on v2

--- a/solution.py
+++ b/solution.py
@@ -14,6 +14,8 @@
 NY = 4
 W = 512
 NJ = 32
+HALF = NJ // 2
+PART = 4
 EXTRA = 16
 BLOCK = W + EXTRA
 TAIL = 128
@@ -37,8 +39,8 @@
 
 ROWS = NL * NY
 CORE = [(device_of(r, c), device_of(r, 1 - c)) for r in range(ROWS) for c in range(2)]
-RAISE = [(device_of(r, c), device_of((r + 1) % ROWS, 1 - c)) for r in range(ROWS) for c in range(2)]
-LOWER = [(device_of(r, c), device_of((r - 1) % ROWS, 1 - c)) for r in range(ROWS) for c in range(2)]
+RAISE = [(device_of(r, c), device_of((r + 1) % ROWS, c)) for r in range(ROWS) for c in range(2)]
+LOWER = [(device_of(r, c), device_of((r - 1) % ROWS, c)) for r in range(ROWS) for c in range(2)]
 
 
 def swap(value, pairs):
@@ -92,92 +94,97 @@
     wait_all(copies)
 
 
-def apply_block(vectors, blocks, layer):
-    return lax.dot_general(
-        vectors, blocks[layer], (((1,), (1,)), ((), ())), preferred_element_type=F32
-    )
-
-
-def couple(coef, layer, own, diff):
-    return coef[layer, 0:1, :] * own + coef[layer, 1:2, :] * diff
-
-
-def start_kernel(phases, taper, arrived, blocks, forcing, coef, down, up, send, extras, sems):
-    edge = pltpu.make_async_copy(arrived.at[:, pl.ds(W, EXTRA)], extras, sems.at[NL])
-    edge.start()
-    copies = []
-    for layer in range(NL):
-        copies.append(pltpu.make_async_copy(arrived.at[layer, pl.ds(0, W)], blocks.at[layer], sems.at[layer]))
-        copies[layer].start()
-    edge.wait()
-    for layer in range(NL):
-        rows = extras[layer].astype(F32)
-        shaped = rows[0:8] * taper[...]
-        for m in range(4):
-            forcing[layer, 8 * m:8 * m + 8, :] = shaped * phases[layer, m]
-        coef[layer, 0:1, :] = rows[8:9] + rows[9:10] + rows[10:11]
-        coef[layer, 1:2, :] = rows[11:12] + rows[12:13] + rows[13:14]
-    copies[0].wait()
-    current = apply_block(forcing[0].astype(BF16), blocks, 0).astype(BF16)
-    down[0] = current
-    send[0] = current
-    for layer in range(1, NL):
-        copies[layer].wait()
-
-
-def phase_kernel(comp, steps, place, blocks, forcing, coef, *refs):
-    near = refs[0:1] if comp == 1 else refs[0:2]
-    down_in, up_in, down, up, send = refs[len(near):]
-    columns = lax.broadcasted_iota(jnp.int32, (NJ, W), 1)
-
-    def differences(slot):
-        if comp == 1:
-            field = near[0][slot].astype(F32)
-            after = jnp.where(columns == W - 1, 0.0, pltpu.roll(field, W - 1, 1))
-            before = jnp.where(columns == 0, 0.0, pltpu.roll(field, 1, 1))
-            return after - before
-        below = jnp.where(place[2] == 0, 0.0, near[0][slot].astype(F32))
-        above = jnp.where(place[2] == ROWS - 1, 0.0, near[1][slot].astype(F32))
-        return above - below
-
-    @pl.when(place[0] == comp)
-    def _():
-        for slot, (layer, is_up) in enumerate(steps):
-            diff = differences(slot)
+def split_kernel(arrived, *refs):
+    parts, sems = refs[:-1], refs[-1]
+    wait_all(start_all([
+        pltpu.make_async_copy(arrived.at[pl.ds(PART * q, PART)], part, sems.at[q])
+        for q, part in enumerate(parts)
+    ]))
+
+
+STEPS = [(layer, False) for layer in range(NL)] + [(layer, True) for layer in range(NL - 2, -1, -1)]
+
+
+def sweep_kernel(x_steps, y_steps, chunks, place, phases, taper, *refs):
+    first = x_steps[0] == 0
+    near = () if first else refs[0:2]
+    refs = refs[len(near):]
+    own_parts, other_parts = refs[:len(chunks)], refs[len(chunks):2 * len(chunks)]
+    refs = refs[2 * len(chunks):]
+    down, up, send = refs if first else refs[2:]
+    columns = lax.broadcasted_iota(jnp.int32, (HALF, W), 1)
+
+    def sweep(core):
+        def advance(comp, step, diff):
+            layer, is_up = STEPS[step]
+            part = (own_parts if comp == core else other_parts)[chunks.index(layer // PART)]
+            rows = part[layer % PART, W:BLOCK, :].astype(F32)
+            self_coef = rows[8:9] + rows[9:10] + rows[10:11]
+            curl_coef = rows[11:12] + rows[12:13] + rows[13:14]
+
+            def solve(vectors):
+                return lax.dot_general(
+                    vectors.astype(BF16), part[layer % PART, 0:W, :],
+                    (((1,), (1,)), ((), ())), preferred_element_type=F32,
+                )
+
             if is_up:
-                own = down[layer + 1].astype(F32) if layer == NL - 2 else up[layer + 1]
-                image = couple(coef, layer, own, diff).astype(BF16)
-                current = down[layer].astype(F32) - apply_block(image, blocks, layer)
-                up[layer] = current
-                send[slot] = current.astype(BF16)
+                own = down[comp, layer + 1].astype(F32) if layer == NL - 2 else up[comp, layer + 1]
+                current = down[comp, layer].astype(F32) - solve(self_coef * own + curl_coef * diff)
+                up[comp, layer] = current
+                return current
+            shaped = rows[0:8] * taper[...]
+            forcing = jnp.concatenate([shaped * phases[layer, 2 * core + m] for m in range(2)], axis=0)
+            if layer == 0:
+                residue = forcing
             else:
-                own = down[layer - 1].astype(F32)
-                residue = (forcing[layer] - couple(coef, layer, own, diff)).astype(BF16)
-                current = apply_block(residue, blocks, layer).astype(BF16)
-                down[layer] = current
-                send[slot] = current
-                if layer == NL - 1:
-                    up[layer] = current.astype(F32)
-
-    @pl.when(place[0] != comp)
-    def _():
-        send[...] = jnp.zeros_like(send)
-
-
-def phase(comp, steps, place, blocks, forcing, coef, near, down, up):
-    first = 4 + len(near)
+                own = down[comp, layer - 1].astype(F32)
+                residue = forcing - (self_coef * own + curl_coef * diff)
+            current = solve(residue).astype(BF16)
+            down[comp, layer] = current
+            current = current.astype(F32)
+            if layer == NL - 1:
+                up[comp, layer] = current
+            return current
+
+        x_new = {}
+        for slot, step in enumerate(x_steps):
+            diff = None
+            if step > 0:
+                below = jnp.where(place[2] == 0, 0.0, near[0][slot].astype(F32))
+                above = jnp.where(place[2] == ROWS - 1, 0.0, near[1][slot].astype(F32))
+                diff = above - below
+            x_new[step] = advance(0, step, diff)
+        for slot, step in enumerate(y_steps):
+            diff = None
+            if step > 0:
+                field = x_new[step - 1]
+                after = jnp.where(columns == W - 1, 0.0, pltpu.roll(field, W - 1, 1))
+                before = jnp.where(columns == 0, 0.0, pltpu.roll(field, 1, 1))
+                diff = after - before
+            send[slot] = advance(1, step, diff).astype(BF16)
+
+    for core in range(2):
+        pl.when(place[0] == core)(functools.partial(sweep, core))
+
+
+def sweep(x_steps, y_steps, place, phases, taper, near, own_parts, other_parts, state):
+    x_steps, y_steps = list(x_steps), list(y_steps)
+    chunks = sorted({STEPS[step][0] // PART for step in x_steps + y_steps})
+    inputs = [taper, *near] + [own_parts[q] for q in chunks] + [other_parts[q] for q in chunks] + list(state)
+    aliases = {2 + len(inputs) - len(state) + i: i for i in range(len(state))}
     return pl.pallas_call(
-        functools.partial(phase_kernel, comp, steps),
+        functools.partial(sweep_kernel, x_steps, y_steps, chunks),
         out_shape=(
-            jax.ShapeDtypeStruct(down.shape, down.dtype),
-            jax.ShapeDtypeStruct(up.shape, up.dtype),
-            jax.ShapeDtypeStruct((len(steps), NJ, W), BF16),
+            jax.ShapeDtypeStruct((2, NL, HALF, W), BF16),
+            jax.ShapeDtypeStruct((2, NL, HALF, W), F32),
+            jax.ShapeDtypeStruct((len(y_steps), HALF, W), BF16),
         ),
-        in_specs=[SMEM] + [VMEM] * (5 + len(near)),
+        in_specs=[SMEM, SMEM] + [VMEM] * len(inputs),
         out_specs=(VMEM, VMEM, VMEM),
-        input_output_aliases={first: 0, first + 1: 1},
-        compiler_params=PARAMS,
-    )(place, blocks, forcing, coef, *near, down, up)
+        input_output_aliases=aliases,
+        compiler_params=PARAMS,
+    )(place, phases, *inputs)
 
 
 def pieces(values):
@@ -189,15 +196,22 @@
     return out
 
 
-def gram_kernel(up, send):
+def share_kernel(place, up, send):
+    for layer in range(NL):
+        send[layer] = up[1 - place[0], layer].astype(BF16)
+
+
+def gram_kernel(place, up, received, send):
+    core = place[0]
     total = jnp.zeros((NJ, NJ), F32)
     for layer in range(NL):
-        rows = up[layer]
+        own, other = up[core, layer], received[layer].astype(F32)
+        low, high = jnp.where(core == 0, own, other), jnp.where(core == 0, other, own)
+        rows = jnp.concatenate([low, high], axis=0).astype(BF16)
         total += lax.dot_general(
-            rows, rows, (((1,), (1,)), ((), ())),
-            precision=lax.Precision.HIGHEST, preferred_element_type=F32,
+            rows, rows, (((1,), (1,)), ((), ())), preferred_element_type=F32
         )
-        send[layer, :, 0:W] = rows.astype(BF16)
+        send[layer, :, 0:W] = rows
     tail = jnp.concatenate(pieces(total) + [jnp.zeros((NJ, NJ), BF16)], axis=1)
     for layer in range(NL):
         send[layer, :, W:W + TAIL] = tail
@@ -288,47 +302,41 @@
     )(place, layer_inverse, extras, received, more, phases, port_taper)
     arrived = lax.all_to_all(packed, "layer", 0, 0, tiled=True)
 
-    blocks, forcing, coef, down, up, first = pl.pallas_call(
-        start_kernel,
-        out_shape=(
-            jax.ShapeDtypeStruct((NL, W, W), BF16),
-            jax.ShapeDtypeStruct((NL, NJ, W), F32),
-            jax.ShapeDtypeStruct((NL, 2, W), F32),
-            jax.ShapeDtypeStruct((NL, NJ, W), BF16),
-            jax.ShapeDtypeStruct((NL, NJ, W), F32),
-            jax.ShapeDtypeStruct((1, NJ, W), BF16),
-        ),
-        in_specs=[SMEM, VMEM, ANY],
-        out_specs=(VMEM,) * 6,
-        scratch_shapes=[pltpu.VMEM((NL, EXTRA, W), BF16), pltpu.SemaphoreType.DMA((NL + 1,))],
-        compiler_params=PARAMS,
-    )(phases, port_taper, arrived)
-
-    sequence = [(layer, False) for layer in range(NL)] + [(layer, True) for layer in range(NL - 2, -1, -1)]
-    run = lambda comp, at, near, down, up: phase(
-        comp, sequence[at[0]:at[1]], place, blocks, forcing, coef, near, down, up
+    parts = pl.pallas_call(
+        split_kernel,
+        out_shape=(jax.ShapeDtypeStruct((PART, BLOCK, W), BF16),) * (NL // PART),
+        in_specs=[ANY],
+        out_specs=(VMEM,) * (NL // PART),
+        scratch_shapes=[pltpu.SemaphoreType.DMA((NL // PART,))],
+        compiler_params=PARAMS,
+    )(arrived)
+    others = [swap(part, CORE) for part in parts]
+
+    run = lambda x_steps, y_steps, near, state: sweep(
+        x_steps, y_steps, place, phases, port_taper, near, parts, others, state
     )
-    x_sent = swap(first, CORE)
-    down, up, y_new = run(1, (1, 2), [x_sent], down, up)
-    y_pair = jnp.concatenate([first, y_new])
-    at = 1
-    last = len(sequence)
-    while at < last:
-        stop = min(at + 2, last)
-        near = [swap(y_pair, RAISE), swap(y_pair, LOWER)]
-        down, up, x_pair = run(0, (at, stop), near, down, up)
-        y_stop = min(at + 3, last)
-        x_sent = swap(x_pair[:y_stop - at - 1], CORE)
-        down, up, y_pair = run(1, (at + 1, y_stop), [x_sent], down, up)
-        at = stop
-
+    down, up, pair = run(range(1), range(2), (), ())
+    last = len(STEPS)
+    for at in range(1, last, 2):
+        near = (swap(pair, RAISE), swap(pair, LOWER))
+        down, up, pair = run(
+            range(at, min(at + 2, last)), range(at + 1, min(at + 3, last)), near, (down, up)
+        )
+
+    shared = pl.pallas_call(
+        share_kernel,
+        out_shape=jax.ShapeDtypeStruct((NL, HALF, W), BF16),
+        in_specs=[SMEM, VMEM],
+        out_specs=VMEM,
+        compiler_params=PARAMS,
+    )(place, up)
     basis = pl.pallas_call(
         gram_kernel,
         out_shape=jax.ShapeDtypeStruct((NL, NJ, W + TAIL), BF16),
-        in_specs=[VMEM],
+        in_specs=[SMEM, VMEM, VMEM],
         out_specs=VMEM,
         compiler_params=PARAMS,
-    )(up)
+    )(place, up, swap(shared, CORE))
     rows = lax.all_to_all(basis, "layer", 0, 0, tiled=True)
     gram, back = pl.pallas_call(
         collect_kernel,

time: 300 us -> 272 us (0.907)
  waiting for transfers between devices: 96.4 us -> 70.1 us
    ppermute x52 -> x41, waiting for transfers between devices: 96.4 us -> 70.1 us  [swap(): return lax.ppermute(value, AXES, pairs)]
    pallas_call x32 -> x18, Pallas kernels: 26.2 us -> 24.4 us  [the longest x16 22.9 us: sweep(): pl.pallas_call(functools.partial(sweep_kernel, x_steps, y_steps, chunks),...]
    ppermute x52 -> x41, starting transfers between devices: 33.4 us -> 34.3 us  [swap(): return lax.ppermute(value, AXES, pairs)]
  transfers between devices with their start and end apart: 52 -> 41, of which waited for: 51 -> 37; matrix products, arithmetic and copies ran while one was open for 0% -> 0% of each run, Pallas kernels for 0% -> 3%
where the time goes in v3:
time: 272 us
  blocking collectives  122 us (45%)
  waiting for transfers between devices  70.1 us (26%)
  Pallas kernels  39 us (14%)
  starting transfers between devices  34.3 us (13%)
  local copies, waits for them, and re-layouts  3.95 us (1%)
    all_to_all x1, blocking collectives, per_device(): arrived = lax.all_to_all(packed, 'layer', 0, 0, tiled=True)  106 us
    ppermute x41, waiting for transfers between devices, swap(): return lax.ppermute(value, AXES, pairs)  70.1 us
    ppermute x41, starting transfers between devices, swap(): return lax.ppermute(value, AXES, pairs)  34.3 us
    pallas_call x16, Pallas kernels, sweep(): pl.pallas_call(functools.partial(sweep_kernel, x_steps, y_steps, chunks),...  22.9 us
    all_to_all x1, blocking collectives, per_device(): rows = lax.all_to_all(basis, 'layer', 0, 0, tiled=True)  15.9 us
    pallas_call x1, Pallas kernels, per_device(): pl.pallas_call(final_kernel, out_shape=(jax.ShapeDtypeStruct((1, NJ, 2, 8...  5.62 us
  transfers between devices with their start and end apart: 41, of which 37 were waited for; matrix products, arithmetic and copies ran while one was open for 0% of the time, Pallas kernels for 3%

profile of v3, /device:TPU:0, one launch (start us, length us, event | category | flops | bytes accessed | tf_op | source)
XLA Modules:
  0.0 271.8 jit_solution(5176704882241770388)
XLA Ops:
  1.3 4.4 %shard_map.77 = bf16[8,512,512]{2,1,0:T(8,128)(2,1)} custom-call(s32[4]{0:T(128)} %pad_add_fusion.place, bf16[1,2,8,512,512]{4,3,2,1,0:T(8,128)(2,1)} %blocks.3), custom_call_target="tpu_custom_call" | custom-call | tf_op jit(solution)/shard_map/pallas_call | solution.py:281
  7.4 5.7 %collective-permute-done.1.more = bf16[8,16,512]{2,1,0:T(8,128)(2,1)S(1)} collective-permute-done((bf16[8,16,512]{2,1,0:T(8,128)(2,1)S(1)}, bf16[8,16,512]{2,1,0:T(8,128)(2,1)S(1)}, u32[]{:S(2)}, u32[]{:S(2)}) %collective-permute-start.1) | collective-permute-done | bytes 131104 | tf_op jit(solution)/shard_map/ppermute | solution.py:47
  13.3 3.4 %copy-done = bf16[1,2,8,512,512]{4,3,2,1,0:T(8,128)(2,1)S(1)} copy-done((bf16[1,2,8,512,512]{4,3,2,1,0:T(8,128)(2,1)S(1)}, bf16[1,2,8,512,512]{4,3,2,1,0:T(8,128)(2,1)}, u32[]{:S(2)}) %copy-start) | copy-done | bytes 8388632
  16.7 3.0 %shard_map.78 = (bf16[16,528,512]{2,1,0:T(8,128)(2,1)S(1)}, f32[16,4]{1,0:T(8,128)S(1)}, f32[8,512]{1,0:T(8,128)S(1)}) custom-call(s32[4]{0:T(128)S(1)} %copy-done.1, bf16[1,2,8,512,512]{4,3,2,1,0:T(8,128)(2,1)S(1)} %copy-done, bf16[2,8,16,512]{3,2,1,0:T(8,128)(2,1)S(1)} %concatenate.3.extras, bf16[8,512,512]{2,1,0:T(8,128)(2,1)} %collective-permute-done.received, ...), custom_call_target="tpu_custom_call" | custom-call | tf_op jit(solution)/shard_map/pallas_call | solution.py:291
  19.7 106.5 %all_to_all.10.arrived = bf16[16,528,512]{2,1,0:T(8,128)(2,1)S(1)} all-to-all(bf16[16,528,512]{2,1,0:T(8,128)(2,1)S(1)} %get-tuple-element.59), channel_id=1, replica_groups=mesh['layer'=16,'tile'=8] {'layer'}, dimensions={0} | all-to-all | bytes 17301504 | tf_op jit(solution)/shard_map/all_to_all | solution.py:303
  128.2 3.2 %collective-permute-done.2.refs_1_.refs_3_.refs_4_ = bf16[4,528,512]{2,1,0:T(8,128)(2,1)S(1)} collective-permute-done((bf16[4,528,512]{2,1,0:T(8,128)(2,1)S(1)}, bf16[4,528,512]{2,1,0:T(8,128)(2,1)S(1)}, u32[]{:S(2)}, u32[]{:S(2)}) %collective-permute-start.2) | collective-permute-done | bytes 2162720 | tf_op jit(solution)/shard_map/ppermute | solution.py:47
  132.7 3.1 %collective-permute-start.4 = (bf16[2,16,512]{2,1,0:T(8,128)(2,1)S(1)}, bf16[2,16,512]{2,1,0:T(8,128)(2,1)S(1)}, u32[]{:S(2)}, u32[]{:S(2)}) collective-permute-start(bf16[2,16,512]{2,1,0:T(8,128)(2,1)S(1)} %get-tuple-element.61), channel_id=1, source_target_pairs={{0,6},{1,7},{8,0},{9,1},{16,8},{17,9},{24,16},{25,17},{56,24},{57,... | collective-permute-start | bytes 98312 | tf_op jit(solution)/shard_map/ppermute | solution.py:47
  135.7 1.6 collective-permute-done.4.refs_1_
  137.3 3.5 %collective-permute-done.3.refs_0_ = bf16[2,16,512]{2,1,0:T(8,128)(2,1)S(1)} collective-permute-done((bf16[2,16,512]{2,1,0:T(8,128)(2,1)S(1)}, bf16[2,16,512]{2,1,0:T(8,128)(2,1)S(1)}, u32[]{:S(2)}, u32[]{:S(2)}) %collective-permute-start.3) | collective-permute-done | bytes 32800 | tf_op jit(solution)/shard_map/ppermute | solution.py:47
  140.9 1.4 shard_map.81
  142.3 2.0 collective-permute-start.5
  144.3 1.9 collective-permute-done.6.refs_1_
  148.9 2.1 collective-permute-start.8
  150.9 1.9 collective-permute-done.9.refs_1_
  154.1 1.4 shard_map.83
  155.5 2.1 collective-permute-start.10
  157.6 1.9 collective-permute-done.11.refs_1_
  162.1 2.1 collective-permute-start.13
  164.2 2.0 collective-permute-done.14.refs_1_
  169.0 1.9 collective-permute-start.15
  170.9 1.9 collective-permute-done.16.refs_1_
  174.1 1.6 shard_map.86
  175.7 2.0 collective-permute-start.18
  177.8 1.9 collective-permute-done.19.refs_1_
  180.9 1.4 shard_map.87
  182.4 2.0 collective-permute-start.20
  184.4 1.9 collective-permute-done.21.refs_1_
  187.5 1.4 shard_map.88
  189.0 2.0 collective-permute-start.22
  191.0 1.9 collective-permute-done.23.refs_1_
  195.6 2.0 collective-permute-start.24
  197.6 2.1 collective-permute-done.25.refs_1_
  202.4 2.0 collective-permute-start.26
  204.5 1.9 collective-permute-done.27.refs_1_
  209.1 2.0 collective-permute-start.28
  211.1 1.9 collective-permute-done.29.refs_1_
  215.7 2.0 collective-permute-start.30
  217.7 1.9 collective-permute-done.31.refs_1_
  222.3 2.0 collective-permute-start.32
  224.3 1.9 collective-permute-done.33.refs_1_
  229.1 2.0 collective-permute-start.34
  231.1 1.9 collective-permute-done.35.refs_1_
  234.3 1.9 shard_map.95
  236.9 1.5 collective-permute-done.36.received
  239.3 15.9 %all_to_all.11.rows = bf16[16,32,640]{2,1,0:T(8,128)(2,1)S(1)} all-to-all(bf16[16,32,640]{2,1,0:T(8,128)(2,1)S(1)} %shard_map.97), channel_id=1, replica_groups=mesh['layer'=16,'tile'=8] {'layer'}, dimensions={0} | all-to-all | bytes 1310720 | tf_op jit(solution)/shard_map/all_to_all | solution.py:340
  257.5 3.7 %collective-permute-done.38 = f32[32,32]{1,0:T(8,128)S(1)} collective-permute-done((f32[32,32]{1,0:T(8,128)S(1)}, f32[32,32]{1,0:T(8,128)S(1)}, u32[]{:S(2)}, u32[]{:S(2)}) %collective-permute-start.38) | collective-permute-done | bytes 4128 | tf_op jit(solution)/shard_map/ppermute | solution.py:47
  261.2 4.9 %collective-permute-done.39 = f32[32,32]{1,0:T(8,128)S(1)} collective-permute-done((f32[32,32]{1,0:T(8,128)S(1)}, f32[32,32]{1,0:T(8,128)S(1)}, u32[]{:S(2)}, u32[]{:S(2)}) %collective-permute-start.39) | collective-permute-done | bytes 4128 | tf_op jit(solution)/shard_map/ppermute | solution.py:47
  266.2 5.6 %shard_map.99 = (f32[1,32,2,8,512]{4,3,2,1,0:T(8,128)}, f32[32,32]{1,0:T(8,128)}) custom-call(s32[4]{0:T(128)S(1)} %copy-done.1, f32[32,32]{1,0:T(8,128)S(1)} %add.57.gram, bf16[16,32,640]{2,1,0:T(8,128)(2,1)S(1)} %all_to_all.11.rows, bf16[8,32,512]{2,1,0:T(8,128)(2,1)S(1)} %collective-permute-done.40.received), custom_call_target="tpu_custom_call" | custom-call | tf_op jit(solution)/shard_map/pallas_call | solution.py:351
  (88 shorter events, 40.4 us)
Async XLA Ops:
  1.3 4.6 %copy-start.2 = (bf16[1,8,2,8,512]{4,3,2,1,0:T(8,128)(2,1)S(1)}, bf16[1,8,2,8,512]{4,3,2,1,0:T(8,128)(2,1)}, u32[]{:S(2)}) copy-start(bf16[1,8,2,8,512]{4,3,2,1,0:T(8,128)(2,1)} %param.6) | copy-start | bytes 393220
  1.3 4.7 %copy-start.3 = (f32[1,2,8,512]{3,2,1,0:T(8,128)S(1)}, f32[1,2,8,512]{3,2,1,0:T(8,128)}, u32[]{:S(2)}) copy-start(f32[1,2,8,512]{3,2,1,0:T(8,128)} %param.10) | copy-start | bytes 98308
  1.3 4.7 %copy-start.4 = (f32[1,2,8,512]{3,2,1,0:T(8,128)S(1)}, f32[1,2,8,512]{3,2,1,0:T(8,128)}, u32[]{:S(2)}) copy-start(f32[1,2,8,512]{3,2,1,0:T(8,128)} %param.11) | copy-start | bytes 98308
  1.3 5.8 %copy-start.6 = (s32[8]{0:T(128)S(1)}, s32[8]{0:T(128)}, u32[]{:S(2)}) copy-start(s32[8]{0:T(128)} %param.7) | copy-start | bytes 100
  1.3 5.8 %copy-start.5 = (f32[2]{0:T(128)S(1)}, f32[2]{0:T(128)}, u32[]{:S(2)}) copy-start(f32[2]{0:T(128)} %param.8) | copy-start | bytes 28
  1.3 12.0 %copy-start.1 = (s32[4]{0:T(128)S(1)}, s32[4]{0:T(128)}, u32[]{:S(2)}) copy-start(s32[4]{0:T(128)} %pad_add_fusion.place) | copy-start | bytes 52
  5.8 7.6 %collective-permute-start = (bf16[8,512,512]{2,1,0:T(8,128)(2,1)}, bf16[8,512,512]{2,1,0:T(8,128)(2,1)}, u32[]{:S(2)}, u32[]{:S(2)}) collective-permute-start(bf16[8,512,512]{2,1,0:T(8,128)(2,1)} %shard_map.77), channel_id=1, source_target_pairs={{0,1},{1,0},{8,9},{9,8},{16,17},{17,16},{24,25},{25,24},{56,57},{5... | collective-permute-start | bytes 12582920 | tf_op jit(solution)/shard_map/ppermute | solution.py:47
  6.6 6.6 %collective-permute-start.1 = (bf16[8,16,512]{2,1,0:T(8,128)(2,1)S(1)}, bf16[8,16,512]{2,1,0:T(8,128)(2,1)S(1)}, u32[]{:S(2)}, u32[]{:S(2)}) collective-permute-start(bf16[8,16,512]{2,1,0:T(8,128)(2,1)S(1)} %dynamic-slice_bitcast_fusion), channel_id=1, source_target_pairs={{0,1},{1,0},{8,9},{9,8},{16,17},{17,16},{24,25},{25,24},{56,57},{5... | collective-permute-start | bytes 393224 | tf_op jit(solution)/shard_map/ppermute | solution.py:47
  13.3 3.4 %copy-start = (bf16[1,2,8,512,512]{4,3,2,1,0:T(8,128)(2,1)S(1)}, bf16[1,2,8,512,512]{4,3,2,1,0:T(8,128)(2,1)}, u32[]{:S(2)}) copy-start(bf16[1,2,8,512,512]{4,3,2,1,0:T(8,128)(2,1)} %blocks.3) | copy-start | bytes 25165828
  127.1 4.3 %collective-permute-start.2 = (bf16[4,528,512]{2,1,0:T(8,128)(2,1)S(1)}, bf16[4,528,512]{2,1,0:T(8,128)(2,1)S(1)}, u32[]{:S(2)}, u32[]{:S(2)}) collective-permute-start(bf16[4,528,512]{2,1,0:T(8,128)(2,1)S(1)} %get-tuple-element.60.refs_0_.refs_2_), channel_id=1, source_target_pairs={{0,1},{1,0},{8,9},{9,8},{16,17},{17,16},{24,25},{25,24},{56,57},{5... | collective-permute-start | bytes 6488072 | tf_op jit(solution)/shard_map/ppermute | solution.py:47
  127.2 17.1 %collective-permute-start.7 = (bf16[4,528,512]{2,1,0:T(8,128)(2,1)S(1)}, bf16[4,528,512]{2,1,0:T(8,128)(2,1)S(1)}, u32[]{:S(2)}, u32[]{:S(2)}) collective-permute-start(bf16[4,528,512]{2,1,0:T(8,128)(2,1)S(1)} %get-tuple-element.65.refs_3_.refs_2_), channel_id=1, source_target_pairs={{0,1},{1,0},{8,9},{9,8},{16,17},{17,16},{24,25},{25,24},{56,57},{5... | collective-permute-start | bytes 6488072 | tf_op jit(solution)/shard_map/ppermute | solution.py:47
  127.7 29.8 %collective-permute-start.12 = (bf16[4,528,512]{2,1,0:T(8,128)(2,1)S(1)}, bf16[4,528,512]{2,1,0:T(8,128)(2,1)S(1)}, u32[]{:S(2)}, u32[]{:S(2)}) collective-permute-start(bf16[4,528,512]{2,1,0:T(8,128)(2,1)S(1)} %get-tuple-element.72.refs_3_.refs_2_), channel_id=1, source_target_pairs={{0,1},{1,0},{8,9},{9,8},{16,17},{17,16},{24,25},{25,24},{56,57},{5... | collective-permute-start | bytes 6488072 | tf_op jit(solution)/shard_map/ppermute | solution.py:47
  127.8 43.1 %collective-permute-start.17 = (bf16[4,528,512]{2,1,0:T(8,128)(2,1)S(1)}, bf16[4,528,512]{2,1,0:T(8,128)(2,1)S(1)}, u32[]{:S(2)}, u32[]{:S(2)}) collective-permute-start(bf16[4,528,512]{2,1,0:T(8,128)(2,1)S(1)} %get-tuple-element.79.refs_3_.refs_2_), channel_id=1, source_target_pairs={{0,1},{1,0},{8,9},{9,8},{16,17},{17,16},{24,25},{25,24},{56,57},{5... | collective-permute-start | bytes 6488072 | tf_op jit(solution)/shard_map/ppermute | solution.py:47
  132.7 4.7 %collective-permute-start.4 = (bf16[2,16,512]{2,1,0:T(8,128)(2,1)S(1)}, bf16[2,16,512]{2,1,0:T(8,128)(2,1)S(1)}, u32[]{:S(2)}, u32[]{:S(2)}) collective-permute-start(bf16[2,16,512]{2,1,0:T(8,128)(2,1)S(1)} %get-tuple-element.61), channel_id=1, source_target_pairs={{0,6},{1,7},{8,0},{9,1},{16,8},{17,9},{24,16},{25,17},{56,24},{57,... | collective-permute-start | bytes 98312 | tf_op jit(solution)/shard_map/ppermute | solution.py:47
  135.7 5.1 %collective-permute-start.3 = (bf16[2,16,512]{2,1,0:T(8,128)(2,1)S(1)}, bf16[2,16,512]{2,1,0:T(8,128)(2,1)S(1)}, u32[]{:S(2)}, u32[]{:S(2)}) collective-permute-start(bf16[2,16,512]{2,1,0:T(8,128)(2,1)S(1)} %get-tuple-element.61), channel_id=1, source_target_pairs={{0,8},{1,9},{8,16},{9,17},{16,24},{17,25},{24,56},{25,57},{56,48},... | collective-permute-start | bytes 98312 | tf_op jit(solution)/shard_map/ppermute | solution.py:47
  142.3 4.0 %collective-permute-start.6 = (bf16[2,16,512]{2,1,0:T(8,128)(2,1)S(1)}, bf16[2,16,512]{2,1,0:T(8,128)(2,1)S(1)}, u32[]{:S(2)}, u32[]{:S(2)}) collective-permute-start(bf16[2,16,512]{2,1,0:T(8,128)(2,1)S(1)} %get-tuple-element.64), channel_id=1, source_target_pairs={{0,6},{1,7},{8,0},{9,1},{16,8},{17,9},{24,16},{25,17},{56,24},{57,... | collective-permute-start | bytes 98312 | tf_op jit(solution)/shard_map/ppermute | solution.py:47
  142.3 5.2 %collective-permute-start.5 = (bf16[2,16,512]{2,1,0:T(8,128)(2,1)S(1)}, bf16[2,16,512]{2,1,0:T(8,128)(2,1)S(1)}, u32[]{:S(2)}, u32[]{:S(2)}) collective-permute-start(bf16[2,16,512]{2,1,0:T(8,128)(2,1)S(1)} %get-tuple-element.64), channel_id=1, source_target_pairs={{0,8},{1,9},{8,16},{9,17},{16,24},{17,25},{24,56},{25,57},{56,48},... | collective-permute-start | bytes 98312 | tf_op jit(solution)/shard_map/ppermute | solution.py:47
  148.9 4.0 %collective-permute-start.9 = (bf16[2,16,512]{2,1,0:T(8,128)(2,1)S(1)}, bf16[2,16,512]{2,1,0:T(8,128)(2,1)S(1)}, u32[]{:S(2)}, u32[]{:S(2)}) collective-permute-start(bf16[2,16,512]{2,1,0:T(8,128)(2,1)S(1)} %get-tuple-element.68), channel_id=1, source_target_pairs={{0,6},{1,7},{8,0},{9,1},{16,8},{17,9},{24,16},{25,17},{56,24},{57,... | collective-permute-start | bytes 98312 | tf_op jit(solution)/shard_map/ppermute | solution.py:47
  148.9 5.2 %collective-permute-start.8 = (bf16[2,16,512]{2,1,0:T(8,128)(2,1)S(1)}, bf16[2,16,512]{2,1,0:T(8,128)(2,1)S(1)}, u32[]{:S(2)}, u32[]{:S(2)}) collective-permute-start(bf16[2,16,512]{2,1,0:T(8,128)(2,1)S(1)} %get-tuple-element.68), channel_id=1, source_target_pairs={{0,8},{1,9},{8,16},{9,17},{16,24},{17,25},{24,56},{25,57},{56,48},... | collective-permute-start | bytes 98312 | tf_op jit(solution)/shard_map/ppermute | solution.py:47
  155.5 4.0 %collective-permute-start.11 = (bf16[2,16,512]{2,1,0:T(8,128)(2,1)S(1)}, bf16[2,16,512]{2,1,0:T(8,128)(2,1)S(1)}, u32[]{:S(2)}, u32[]{:S(2)}) collective-permute-start(bf16[2,16,512]{2,1,0:T(8,128)(2,1)S(1)} %get-tuple-element.71), channel_id=1, source_target_pairs={{0,6},{1,7},{8,0},{9,1},{16,8},{17,9},{24,16},{25,17},{56,24},{57,... | collective-permute-start | bytes 98312 | tf_op jit(solution)/shard_map/ppermute | solution.py:47
  155.5 5.2 %collective-permute-start.10 = (bf16[2,16,512]{2,1,0:T(8,128)(2,1)S(1)}, bf16[2,16,512]{2,1,0:T(8,128)(2,1)S(1)}, u32[]{:S(2)}, u32[]{:S(2)}) collective-permute-start(bf16[2,16,512]{2,1,0:T(8,128)(2,1)S(1)} %get-tuple-element.71), channel_id=1, source_target_pairs={{0,8},{1,9},{8,16},{9,17},{16,24},{17,25},{24,56},{25,57},{56,48},... | collective-permute-start | bytes 98312 | tf_op jit(solution)/shard_map/ppermute | solution.py:47
  162.1 4.1 %collective-permute-start.14 = (bf16[2,16,512]{2,1,0:T(8,128)(2,1)S(1)}, bf16[2,16,512]{2,1,0:T(8,128)(2,1)S(1)}, u32[]{:S(2)}, u32[]{:S(2)}) collective-permute-start(bf16[2,16,512]{2,1,0:T(8,128)(2,1)S(1)} %get-tuple-element.75), channel_id=1, source_target_pairs={{0,6},{1,7},{8,0},{9,1},{16,8},{17,9},{24,16},{25,17},{56,24},{57,... | collective-permute-start | bytes 98312 | tf_op jit(solution)/shard_map/ppermute | solution.py:47
  162.1 5.3 %collective-permute-start.13 = (bf16[2,16,512]{2,1,0:T(8,128)(2,1)S(1)}, bf16[2,16,512]{2,1,0:T(8,128)(2,1)S(1)}, u32[]{:S(2)}, u32[]{:S(2)}) collective-permute-start(bf16[2,16,512]{2,1,0:T(8,128)(2,1)S(1)} %get-tuple-element.75), channel_id=1, source_target_pairs={{0,8},{1,9},{8,16},{9,17},{16,24},{17,25},{24,56},{25,57},{56,48},... | collective-permute-start | bytes 98312 | tf_op jit(solution)/shard_map/ppermute | solution.py:47
  168.9 4.0 %collective-permute-start.16 = (bf16[2,16,512]{2,1,0:T(8,128)(2,1)S(1)}, bf16[2,16,512]{2,1,0:T(8,128)(2,1)S(1)}, u32[]{:S(2)}, u32[]{:S(2)}) collective-permute-start(bf16[2,16,512]{2,1,0:T(8,128)(2,1)S(1)} %get-tuple-element.78), channel_id=1, source_target_pairs={{0,6},{1,7},{8,0},{9,1},{16,8},{17,9},{24,16},{25,17},{56,24},{57,... | collective-permute-start | bytes 98312 | tf_op jit(solution)/shard_map/ppermute | solution.py:47
  169.0 5.1 %collective-permute-start.15 = (bf16[2,16,512]{2,1,0:T(8,128)(2,1)S(1)}, bf16[2,16,512]{2,1,0:T(8,128)(2,1)S(1)}, u32[]{:S(2)}, u32[]{:S(2)}) collective-permute-start(bf16[2,16,512]{2,1,0:T(8,128)(2,1)S(1)} %get-tuple-element.78), channel_id=1, source_target_pairs={{0,8},{1,9},{8,16},{9,17},{16,24},{17,25},{24,56},{25,57},{56,48},... | collective-permute-start | bytes 98312 | tf_op jit(solution)/shard_map/ppermute | solution.py:47
  175.7 4.0 %collective-permute-start.19 = (bf16[2,16,512]{2,1,0:T(8,128)(2,1)S(1)}, bf16[2,16,512]{2,1,0:T(8,128)(2,1)S(1)}, u32[]{:S(2)}, u32[]{:S(2)}) collective-permute-start(bf16[2,16,512]{2,1,0:T(8,128)(2,1)S(1)} %get-tuple-element.82), channel_id=1, source_target_pairs={{0,6},{1,7},{8,0},{9,1},{16,8},{17,9},{24,16},{25,17},{56,24},{57,... | collective-permute-start | bytes 98312 | tf_op jit(solution)/shard_map/ppermute | solution.py:47
  175.7 5.2 %collective-permute-start.18 = (bf16[2,16,512]{2,1,0:T(8,128)(2,1)S(1)}, bf16[2,16,512]{2,1,0:T(8,128)(2,1)S(1)}, u32[]{:S(2)}, u32[]{:S(2)}) collective-permute-start(bf16[2,16,512]{2,1,0:T(8,128)(2,1)S(1)} %get-tuple-element.82), channel_id=1, source_target_pairs={{0,8},{1,9},{8,16},{9,17},{16,24},{17,25},{24,56},{25,57},{56,48},... | collective-permute-start | bytes 98312 | tf_op jit(solution)/shard_map/ppermute | solution.py:47
  182.3 4.0 %collective-permute-start.21 = (bf16[2,16,512]{2,1,0:T(8,128)(2,1)S(1)}, bf16[2,16,512]{2,1,0:T(8,128)(2,1)S(1)}, u32[]{:S(2)}, u32[]{:S(2)}) collective-permute-start(bf16[2,16,512]{2,1,0:T(8,128)(2,1)S(1)} %get-tuple-element.85), channel_id=1, source_target_pairs={{0,6},{1,7},{8,0},{9,1},{16,8},{17,9},{24,16},{25,17},{56,24},{57,... | collective-permute-start | bytes 98312 | tf_op jit(solution)/shard_map/ppermute | solution.py:47
  182.4 5.2 %collective-permute-start.20 = (bf16[2,16,512]{2,1,0:T(8,128)(2,1)S(1)}, bf16[2,16,512]{2,1,0:T(8,128)(2,1)S(1)}, u32[]{:S(2)}, u32[]{:S(2)}) collective-permute-start(bf16[2,16,512]{2,1,0:T(8,128)(2,1)S(1)} %get-tuple-element.85), channel_id=1, source_target_pairs={{0,8},{1,9},{8,16},{9,17},{16,24},{17,25},{24,56},{25,57},{56,48},... | collective-permute-start | bytes 98312 | tf_op jit(solution)/shard_map/ppermute | solution.py:47
  189.0 4.0 %collective-permute-start.23 = (bf16[2,16,512]{2,1,0:T(8,128)(2,1)S(1)}, bf16[2,16,512]{2,1,0:T(8,128)(2,1)S(1)}, u32[]{:S(2)}, u32[]{:S(2)}) collective-permute-start(bf16[2,16,512]{2,1,0:T(8,128)(2,1)S(1)} %get-tuple-element.88), channel_id=1, source_target_pairs={{0,6},{1,7},{8,0},{9,1},{16,8},{17,9},{24,16},{25,17},{56,24},{57,... | collective-permute-start | bytes 98312 | tf_op jit(solution)/shard_map/ppermute | solution.py:47
  189.0 5.2 %collective-permute-start.22 = (bf16[2,16,512]{2,1,0:T(8,128)(2,1)S(1)}, bf16[2,16,512]{2,1,0:T(8,128)(2,1)S(1)}, u32[]{:S(2)}, u32[]{:S(2)}) collective-permute-start(bf16[2,16,512]{2,1,0:T(8,128)(2,1)S(1)} %get-tuple-element.88), channel_id=1, source_target_pairs={{0,8},{1,9},{8,16},{9,17},{16,24},{17,25},{24,56},{25,57},{56,48},... | collective-permute-start | bytes 98312 | tf_op jit(solution)/shard_map/ppermute | solution.py:47
  195.6 4.1 %collective-permute-start.25 = (bf16[2,16,512]{2,1,0:T(8,128)(2,1)S(1)}, bf16[2,16,512]{2,1,0:T(8,128)(2,1)S(1)}, u32[]{:S(2)}, u32[]{:S(2)}) collective-permute-start(bf16[2,16,512]{2,1,0:T(8,128)(2,1)S(1)} %get-tuple-element.91), channel_id=1, source_target_pairs={{0,6},{1,7},{8,0},{9,1},{16,8},{17,9},{24,16},{25,17},{56,24},{57,... | collective-permute-start | bytes 98312 | tf_op jit(solution)/shard_map/ppermute | solution.py:47
  195.6 5.4 %collective-permute-start.24 = (bf16[2,16,512]{2,1,0:T(8,128)(2,1)S(1)}, bf16[2,16,512]{2,1,0:T(8,128)(2,1)S(1)}, u32[]{:S(2)}, u32[]{:S(2)}) collective-permute-start(bf16[2,16,512]{2,1,0:T(8,128)(2,1)S(1)} %get-tuple-element.91), channel_id=1, source_target_pairs={{0,8},{1,9},{8,16},{9,17},{16,24},{17,25},{24,56},{25,57},{56,48},... | collective-permute-start | bytes 98312 | tf_op jit(solution)/shard_map/ppermute | solution.py:47
  202.4 4.0 %collective-permute-start.27 = (bf16[2,16,512]{2,1,0:T(8,128)(2,1)S(1)}, bf16[2,16,512]{2,1,0:T(8,128)(2,1)S(1)}, u32[]{:S(2)}, u32[]{:S(2)}) collective-permute-start(bf16[2,16,512]{2,1,0:T(8,128)(2,1)S(1)} %get-tuple-element.94), channel_id=1, source_target_pairs={{0,6},{1,7},{8,0},{9,1},{16,8},{17,9},{24,16},{25,17},{56,24},{57,... | collective-permute-start | bytes 98312 | tf_op jit(solution)/shard_map/ppermute | solution.py:47
  202.4 5.2 %collective-permute-start.26 = (bf16[2,16,512]{2,1,0:T(8,128)(2,1)S(1)}, bf16[2,16,512]{2,1,0:T(8,128)(2,1)S(1)}, u32[]{:S(2)}, u32[]{:S(2)}) collective-permute-start(bf16[2,16,512]{2,1,0:T(8,128)(2,1)S(1)} %get-tuple-element.94), channel_id=1, source_target_pairs={{0,8},{1,9},{8,16},{9,17},{16,24},{17,25},{24,56},{25,57},{56,48},... | collective-permute-start | bytes 98312 | tf_op jit(solution)/shard_map/ppermute | solution.py:47
  209.0 4.0 %collective-permute-start.29 = (bf16[2,16,512]{2,1,0:T(8,128)(2,1)S(1)}, bf16[2,16,512]{2,1,0:T(8,128)(2,1)S(1)}, u32[]{:S(2)}, u32[]{:S(2)}) collective-permute-start(bf16[2,16,512]{2,1,0:T(8,128)(2,1)S(1)} %get-tuple-element.97), channel_id=1, source_target_pairs={{0,6},{1,7},{8,0},{9,1},{16,8},{17,9},{24,16},{25,17},{56,24},{57,... | collective-permute-start | bytes 98312 | tf_op jit(solution)/shard_map/ppermute | solution.py:47
  209.1 5.2 %collective-permute-start.28 = (bf16[2,16,512]{2,1,0:T(8,128)(2,1)S(1)}, bf16[2,16,512]{2,1,0:T(8,128)(2,1)S(1)}, u32[]{:S(2)}, u32[]{:S(2)}) collective-permute-start(bf16[2,16,512]{2,1,0:T(8,128)(2,1)S(1)} %get-tuple-element.97), channel_id=1, source_target_pairs={{0,8},{1,9},{8,16},{9,17},{16,24},{17,25},{24,56},{25,57},{56,48},... | collective-permute-start | bytes 98312 | tf_op jit(solution)/shard_map/ppermute | solution.py:47
  215.7 4.0 %collective-permute-start.31 = (bf16[2,16,512]{2,1,0:T(8,128)(2,1)S(1)}, bf16[2,16,512]{2,1,0:T(8,128)(2,1)S(1)}, u32[]{:S(2)}, u32[]{:S(2)}) collective-permute-start(bf16[2,16,512]{2,1,0:T(8,128)(2,1)S(1)} %get-tuple-element.100), channel_id=1, source_target_pairs={{0,6},{1,7},{8,0},{9,1},{16,8},{17,9},{24,16},{25,17},{56,24},{57,... | collective-permute-start | bytes 98312 | tf_op jit(solution)/shard_map/ppermute | solution.py:47
  215.7 5.2 %collective-permute-start.30 = (bf16[2,16,512]{2,1,0:T(8,128)(2,1)S(1)}, bf16[2,16,512]{2,1,0:T(8,128)(2,1)S(1)}, u32[]{:S(2)}, u32[]{:S(2)}) collective-permute-start(bf16[2,16,512]{2,1,0:T(8,128)(2,1)S(1)} %get-tuple-element.100), channel_id=1, source_target_pairs={{0,8},{1,9},{8,16},{9,17},{16,24},{17,25},{24,56},{25,57},{56,48},... | collective-permute-start | bytes 98312 | tf_op jit(solution)/shard_map/ppermute | solution.py:47
  222.3 4.0 %collective-permute-start.33 = (bf16[2,16,512]{2,1,0:T(8,128)(2,1)S(1)}, bf16[2,16,512]{2,1,0:T(8,128)(2,1)S(1)}, u32[]{:S(2)}, u32[]{:S(2)}) collective-permute-start(bf16[2,16,512]{2,1,0:T(8,128)(2,1)S(1)} %get-tuple-element.103), channel_id=1, source_target_pairs={{0,6},{1,7},{8,0},{9,1},{16,8},{17,9},{24,16},{25,17},{56,24},{57,... | collective-permute-start | bytes 98312 | tf_op jit(solution)/shard_map/ppermute | solution.py:47
  222.3 5.2 %collective-permute-start.32 = (bf16[2,16,512]{2,1,0:T(8,128)(2,1)S(1)}, bf16[2,16,512]{2,1,0:T(8,128)(2,1)S(1)}, u32[]{:S(2)}, u32[]{:S(2)}) collective-permute-start(bf16[2,16,512]{2,1,0:T(8,128)(2,1)S(1)} %get-tuple-element.103), channel_id=1, source_target_pairs={{0,8},{1,9},{8,16},{9,17},{16,24},{17,25},{24,56},{25,57},{56,48},... | collective-permute-start | bytes 98312 | tf_op jit(solution)/shard_map/ppermute | solution.py:47
  228.9 4.1 %collective-permute-start.35 = (bf16[2,16,512]{2,1,0:T(8,128)(2,1)S(1)}, bf16[2,16,512]{2,1,0:T(8,128)(2,1)S(1)}, u32[]{:S(2)}, u32[]{:S(2)}) collective-permute-start(bf16[2,16,512]{2,1,0:T(8,128)(2,1)S(1)} %get-tuple-element.106), channel_id=1, source_target_pairs={{0,6},{1,7},{8,0},{9,1},{16,8},{17,9},{24,16},{25,17},{56,24},{57,... | collective-permute-start | bytes 98312 | tf_op jit(solution)/shard_map/ppermute | solution.py:47
  229.1 5.2 %collective-permute-start.34 = (bf16[2,16,512]{2,1,0:T(8,128)(2,1)S(1)}, bf16[2,16,512]{2,1,0:T(8,128)(2,1)S(1)}, u32[]{:S(2)}, u32[]{:S(2)}) collective-permute-start(bf16[2,16,512]{2,1,0:T(8,128)(2,1)S(1)} %get-tuple-element.106), channel_id=1, source_target_pairs={{0,8},{1,9},{8,16},{9,17},{16,24},{17,25},{24,56},{25,57},{56,48},... | collective-permute-start | bytes 98312 | tf_op jit(solution)/shard_map/ppermute | solution.py:47
  236.8 1.6 collective-permute-start.36
  255.9 10.3 %collective-permute-start.40 = (bf16[8,32,512]{2,1,0:T(8,128)(2,1)S(1)}, bf16[8,32,512]{2,1,0:T(8,128)(2,1)S(1)}, u32[]{:S(2)}, u32[]{:S(2)}) collective-permute-start(bf16[8,32,512]{2,1,0:T(8,128)(2,1)S(1)} %get-tuple-element.111), channel_id=1, source_target_pairs={{0,1},{1,0},{8,9},{9,8},{16,17},{17,16},{24,25},{25,24},{56,57},{5... | collective-permute-start | bytes 786440 | tf_op jit(solution)/shard_map/ppermute | solution.py:47
  255.9 1.5 collective-permute-start.37
  257.5 3.7 %collective-permute-start.38 = (f32[32,32]{1,0:T(8,128)S(1)}, f32[32,32]{1,0:T(8,128)S(1)}, u32[]{:S(2)}, u32[]{:S(2)}) collective-permute-start(f32[32,32]{1,0:T(8,128)S(1)} %add.55), channel_id=1, source_target_pairs={{0,2},{1,3},{2,0},{3,1},{4,6},{5,7},{6,4},{7,5},{8,10},{9,11},{10,... | collective-permute-start | bytes 12296 | tf_op jit(solution)/shard_map/ppermute | solution.py:47
  261.2 4.9 %collective-permute-start.39 = (f32[32,32]{1,0:T(8,128)S(1)}, f32[32,32]{1,0:T(8,128)S(1)}, u32[]{:S(2)}, u32[]{:S(2)}) collective-permute-start(f32[32,32]{1,0:T(8,128)S(1)} %add.56), channel_id=1, source_target_pairs={{0,6},{1,7},{2,4},{3,5},{4,2},{5,3},{6,0},{7,1},{8,14},{9,15},{10,... | collective-permute-start | bytes 12296 | tf_op jit(solution)/shard_map/ppermute | solution.py:47

commit v4 on v3

--- a/solution.py
+++ b/solution.py
@@ -15,7 +15,7 @@
 W = 512
 NJ = 32
 HALF = NJ // 2
-PART = 4
+BOUNDS = (0, 2, 4, 8, 16)
 EXTRA = 16
 BLOCK = W + EXTRA
 TAIL = 128
@@ -47,11 +47,9 @@
     return lax.ppermute(value, AXES, pairs)
 
 
-def exchanges():
-    devices = range(NL * 2 * NY)
-    even = [(d, d ^ 2) for d in devices]
-    odd = [(d, d - d % 8 + (d + (2 if d & 2 else 6)) % 8) for d in devices]
-    return [[(d, d ^ 1) for d in devices], even, odd]
+def beside_y(by):
+    tiles = 2 * NY
+    return [(d, d - d % tiles + (d + 2 * by) % tiles) for d in range(NL * tiles)]
 
 
 def start_all(copies):
@@ -65,9 +63,10 @@
         copy.wait()
 
 
-def pack_send(place, blocks, send, held, sems):
+def pack_send(blocks, send, held, sems):
+    other = 1 - lax.axis_index("tile") % 2
     entering = start_all([
-        pltpu.make_async_copy(blocks.at[0, 1 - place[0], i], held.at[i], sems.at[i]) for i in range(8)
+        pltpu.make_async_copy(blocks.at[0, other, i], held.at[i], sems.at[i]) for i in range(8)
     ])
     leaving = []
     for i in range(8):
@@ -76,30 +75,38 @@
     wait_all(leaving)
 
 
-def pack_all(place, blocks, extras, received, more, phases, taper, out, phases_out, taper_out, sems):
+def pack_own(place, blocks, extras, out, sems):
     core, y = place[0], place[1]
-    copies = []
+    to = [spot(8 * core + i, y) for i in range(8)]
+    copies = start_all([
+        pltpu.make_async_copy(blocks.at[0, core, i], out.at[to[i], pl.ds(0, W)], sems.at[i]) for i in range(8)
+    ])
     for i in range(8):
-        own, other = spot(8 * core + i, y), spot(8 * (1 - core) + i, y)
-        copies += start_all([
-            pltpu.make_async_copy(blocks.at[0, core, i], out.at[own, pl.ds(0, W)], sems.at[i]),
-            pltpu.make_async_copy(received.at[i], out.at[other, pl.ds(0, W)], sems.at[8 + i]),
-        ])
-    for i in range(8):
-        own, other = spot(8 * core + i, y), spot(8 * (1 - core) + i, y)
-        out[own, W:BLOCK, :] = extras[core, i]
-        out[other, W:BLOCK, :] = more[i]
+        out[to[i], W:BLOCK, :] = extras[core, i]
+    wait_all(copies)
+
+
+def pack_other(place, received, more, phases, taper, part, out, phases_out, taper_out, sems):
+    core, y = place[0], place[1]
+    to = [spot(8 * (1 - core) + i, y) for i in range(8)]
+    copies = start_all([
+        pltpu.make_async_copy(received.at[i], out.at[to[i], pl.ds(0, W)], sems.at[i]) for i in range(8)
+    ] + [
+        pltpu.make_async_copy(more.at[i], out.at[to[i], pl.ds(W, EXTRA)], sems.at[8 + i]) for i in range(8)
+    ])
     phases_out[...] = phases[...]
     taper_out[...] = taper[...]
     wait_all(copies)
 
 
-def split_kernel(arrived, *refs):
-    parts, sems = refs[:-1], refs[-1]
-    wait_all(start_all([
-        pltpu.make_async_copy(arrived.at[pl.ds(PART * q, PART)], part, sems.at[q])
-        for q, part in enumerate(parts)
-    ]))
+def part_of(layer):
+    return sum(layer >= bound for bound in BOUNDS[1:])
+
+
+def split_kernel(start, after, arrived, part, sem):
+    copy = pltpu.make_async_copy(arrived.at[pl.ds(start, part.shape[0])], part, sem)
+    copy.start()
+    copy.wait()
 
 
 STEPS = [(layer, False) for layer in range(NL)] + [(layer, True) for layer in range(NL - 2, -1, -1)]
@@ -117,14 +124,16 @@
     def sweep(core):
         def advance(comp, step, diff):
             layer, is_up = STEPS[step]
-            part = (own_parts if comp == core else other_parts)[chunks.index(layer // PART)]
-            rows = part[layer % PART, W:BLOCK, :].astype(F32)
+            chunk = part_of(layer)
+            part = (own_parts if comp == core else other_parts)[chunks.index(chunk)]
+            at = layer - BOUNDS[chunk]
+            rows = part[at, W:BLOCK, :].astype(F32)
             self_coef = rows[8:9] + rows[9:10] + rows[10:11]
             curl_coef = rows[11:12] + rows[12:13] + rows[13:14]
 
             def solve(vectors):
                 return lax.dot_general(
-                    vectors.astype(BF16), part[layer % PART, 0:W, :],
+                    vectors.astype(BF16), part[at, 0:W, :],
                     (((1,), (1,)), ((), ())), preferred_element_type=F32,
                 )
 
@@ -170,7 +179,7 @@
 
 def sweep(x_steps, y_steps, place, phases, taper, near, own_parts, other_parts, state):
     x_steps, y_steps = list(x_steps), list(y_steps)
-    chunks = sorted({STEPS[step][0] // PART for step in x_steps + y_steps})
+    chunks = sorted({part_of(STEPS[step][0]) for step in x_steps + y_steps})
     inputs = [taper, *near] + [own_parts[q] for q in chunks] + [other_parts[q] for q in chunks] + list(state)
     aliases = {2 + len(inputs) - len(state) + i: i for i in range(len(state))}
     return pl.pallas_call(
@@ -226,26 +235,33 @@
         send[i] = rows[spot(8 * (1 - place[0]) + i, place[1]), :, 0:W]
 
 
-def final_kernel(place, gram, rows, received, out, triangle):
+def final_kernel(place, gram_0, gram_2, gram_1, gram_3, rows, received, out, triangle):
     lane = lax.broadcasted_iota(jnp.int32, (NJ, NJ), 1)
     row = lax.broadcasted_iota(jnp.int32, (NJ, NJ), 0)
     order = jnp.where(lane == (row % 4) * 8 + row // 4, 1.0, 0.0)
     back = jnp.where(row == (lane % 4) * 8 + lane // 4, 1.0, 0.0)
     exact = functools.partial(jnp.dot, precision=lax.Precision.HIGHEST, preferred_element_type=F32)
-    left = exact(exact(order, gram[...] * (1.0 / (NL * 2 * ROWS * W))), back)
-    right = order
+    gram = (gram_0[...] + gram_2[...]) + (gram_1[...] + gram_3[...])
+    left = exact(exact(order, gram * (1.0 / (NL * 2 * ROWS * W))), back)
+    both = jnp.concatenate([left, order], axis=1)
+    wide_row = lax.broadcasted_iota(jnp.int32, both.shape, 0)
+    wide_lane = lax.broadcasted_iota(jnp.int32, both.shape, 1)
     for k in range(NJ):
-        scale = lax.rsqrt(left[k:k + 1, k:k + 1])
-        row_left = left[k:k + 1, :] * scale
-        row_right = right[k:k + 1, :] * scale
-        factor = jnp.where(row > k, left[:, k:k + 1] * scale, 0.0)
-        left = jnp.where(row == k, row_left, left - factor * row_left)
-        right = jnp.where(row == k, row_right, right - factor * row_right)
-    triangle[...] = jnp.where(lane >= row, left, 0.0)
+        factor = both[:, k:k + 1] * (1.0 / both[k:k + 1, k:k + 1])
+        both = both - jnp.where(wide_row > k, factor, 0.0) * both[k:k + 1, :]
+    pivots = jnp.sum(jnp.where(wide_lane == wide_row, both, 0.0), axis=1, keepdims=True)
+    both = both * lax.rsqrt(pivots)
+    triangle[...] = jnp.where(lane >= row, both[:, 0:NJ], 0.0)
+    inverse = jnp.concatenate(pieces(both[:, NJ:2 * NJ]), axis=0)
+
+    def product(values):
+        thirds = jnp.dot(inverse, values, preferred_element_type=F32)
+        return thirds[0:NJ] + thirds[NJ:2 * NJ] + thirds[2 * NJ:3 * NJ]
+
     core, y = place[0], place[1]
     for i in range(8):
-        own = exact(right, rows[spot(8 * core + i, y), :, 0:W].astype(F32))
-        other = exact(right, received[i].astype(F32))
+        own = product(rows[spot(8 * core + i, y), :, 0:W])
+        other = product(received[i])
         out[0, :, 0, i, :] = jnp.where(core == 0, own, other)
         out[0, :, 1, i, :] = jnp.where(core == 0, other, own)
 
@@ -281,44 +297,61 @@
     to_send = pl.pallas_call(
         pack_send,
         out_shape=jax.ShapeDtypeStruct((8, W, W), BF16),
-        in_specs=[SMEM, ANY],
+        in_specs=[ANY],
         out_specs=ANY,
         scratch_shapes=[pltpu.VMEM((8, W, W), BF16), pltpu.SemaphoreType.DMA((16,))],
         compiler_params=ALONE,
-    )(place, layer_inverse)
+    )(layer_inverse)
     received = swap(to_send, CORE)
     more = swap(lax.dynamic_index_in_dim(extras, 1 - core, 0, keepdims=False), CORE)
+    part = pl.pallas_call(
+        pack_own,
+        out_shape=jax.ShapeDtypeStruct((NL, BLOCK, W), BF16),
+        in_specs=[SMEM, ANY, VMEM],
+        out_specs=VMEM,
+        scratch_shapes=[pltpu.SemaphoreType.DMA((8,))],
+        compiler_params=PARAMS,
+    )(place, layer_inverse, extras)
     packed, phases, port_taper = pl.pallas_call(
-        pack_all,
+        pack_other,
         out_shape=(
             jax.ShapeDtypeStruct((NL, BLOCK, W), BF16),
             jax.ShapeDtypeStruct(phases.shape, F32),
             jax.ShapeDtypeStruct(port_taper.shape, F32),
         ),
-        in_specs=[SMEM, ANY, VMEM, ANY, VMEM, VMEM, VMEM],
-        out_specs=(VMEM, VMEM, VMEM),
+        in_specs=[SMEM, VMEM, VMEM, VMEM, VMEM, ANY],
+        out_specs=(ANY, VMEM, VMEM),
+        input_output_aliases={5: 0},
         scratch_shapes=[pltpu.SemaphoreType.DMA((16,))],
         compiler_params=PARAMS,
-    )(place, layer_inverse, extras, received, more, phases, port_taper)
+    )(place, received, more, phases, port_taper, part)
     arrived = lax.all_to_all(packed, "layer", 0, 0, tiled=True)
 
-    parts = pl.pallas_call(
-        split_kernel,
-        out_shape=(jax.ShapeDtypeStruct((PART, BLOCK, W), BF16),) * (NL // PART),
-        in_specs=[ANY],
-        out_specs=(VMEM,) * (NL // PART),
-        scratch_shapes=[pltpu.SemaphoreType.DMA((NL // PART,))],
-        compiler_params=PARAMS,
-    )(arrived)
-    others = [swap(part, CORE) for part in parts]
+    parts, others = [], []
+
+    def trade(after):
+        start, end = BOUNDS[len(parts):len(parts) + 2]
+        part = pl.pallas_call(
+            functools.partial(split_kernel, start),
+            out_shape=jax.ShapeDtypeStruct((end - start, BLOCK, W), BF16),
+            in_specs=[ANY, ANY],
+            out_specs=VMEM,
+            scratch_shapes=[pltpu.SemaphoreType.DMA],
+            compiler_params=PARAMS,
+        )(after, arrived)
+        parts.append(part)
+        others.append(swap(part, CORE))
 
     run = lambda x_steps, y_steps, near, state: sweep(
         x_steps, y_steps, place, phases, port_taper, near, parts, others, state
     )
+    trade(port_taper)
     down, up, pair = run(range(1), range(2), (), ())
     last = len(STEPS)
     for at in range(1, last, 2):
         near = (swap(pair, RAISE), swap(pair, LOWER))
+        if len(parts) < len(BOUNDS) - 1:
+            trade(pair)
         down, up, pair = run(
             range(at, min(at + 2, last)), range(at + 1, min(at + 3, last)), near, (down, up)
         )
@@ -346,18 +379,18 @@
         compiler_params=PARAMS,
     )(place, rows)
     received = swap(back, CORE)
-    for pairs in exchanges():
-        gram = gram + swap(gram, pairs)
+    gram = gram + swap(gram, CORE)
+    grams = [gram] + [swap(gram, beside_y(by)) for by in (2, 1, 3)]
     out, triangle = pl.pallas_call(
         final_kernel,
         out_shape=(
             jax.ShapeDtypeStruct((1, NJ, 2, 8, W), F32),
             jax.ShapeDtypeStruct((NJ, NJ), F32),
         ),
-        in_specs=[SMEM, VMEM, VMEM, VMEM],
+        in_specs=[SMEM] + [VMEM] * 6,
         out_specs=(VMEM, VMEM),
         compiler_params=PARAMS,
-    )(place, gram, rows, received)
+    )(place, *grams, rows, received)
     return (out, triangle)
 
 

time: 272 us -> 264 us (0.971)
  waiting for transfers between devices: 70.1 us -> 61.6 us
    ppermute x41 -> x42, waiting for transfers between devices: 70.1 us -> 61.6 us  [swap(): return lax.ppermute(value, AXES, pairs)]
    ppermute x41 -> x42, starting transfers between devices: 34.3 us -> 35.8 us  [swap(): return lax.ppermute(value, AXES, pairs)]
  transfers between devices with their start and end apart: 41 -> 42, of which waited for: 37 -> 38; matrix products, arithmetic and copies ran while one was open for 0% -> 0% of each run, Pallas kernels for 3% -> 1%
where the time goes in v4:
time: 264 us
  blocking collectives  122 us (46%)
  waiting for transfers between devices  61.6 us (23%)
  Pallas kernels  38.9 us (15%)
  starting transfers between devices  35.8 us (14%)
  local copies, waits for them, and re-layouts  3.95 us (1%)
    all_to_all x1, blocking collectives, per_device(): arrived = lax.all_to_all(packed, 'layer', 0, 0, tiled=True)  106 us
    ppermute x42, waiting for transfers between devices, swap(): return lax.ppermute(value, AXES, pairs)  61.6 us
    ppermute x42, starting transfers between devices, swap(): return lax.ppermute(value, AXES, pairs)  35.8 us
    pallas_call x16, Pallas kernels, sweep(): pl.pallas_call(functools.partial(sweep_kernel, x_steps, y_steps, chunks),...  22.9 us
    all_to_all x1, blocking collectives, per_device(): rows = lax.all_to_all(basis, 'layer', 0, 0, tiled=True)  15.9 us
  transfers between devices with their start and end apart: 42, of which 38 were waited for; matrix products, arithmetic and copies ran while one was open for 0% of the time, Pallas kernels for 1%

profile of v4, /device:TPU:0, one launch (start us, length us, event | category | flops | bytes accessed | tf_op | source)
XLA Modules:
  0.0 264.1 jit_solution(247043177462634285)
XLA Ops:
  0.7 3.7 %shard_map.77 = bf16[8,512,512]{2,1,0:T(8,128)(2,1)} custom-call(bf16[1,2,8,512,512]{4,3,2,1,0:T(8,128)(2,1)} %blocks.3), custom_call_target="tpu_custom_call" | custom-call | tf_op jit(solution)/shard_map/pallas_call | solution.py:297
  6.0 3.4 %copy-done = bf16[1,2,8,512,512]{4,3,2,1,0:T(8,128)(2,1)S(1)} copy-done((bf16[1,2,8,512,512]{4,3,2,1,0:T(8,128)(2,1)S(1)}, bf16[1,2,8,512,512]{4,3,2,1,0:T(8,128)(2,1)}, u32[]{:S(2)}) %copy-start) | copy-done | bytes 8388632
  11.9 2.9 %shard_map.79 = (bf16[16,528,512]{2,1,0:T(8,128)(2,1)S(1)}, f32[16,4]{1,0:T(8,128)S(1)}, f32[8,512]{1,0:T(8,128)S(1)}) custom-call(s32[4]{0:T(128)S(1)} %pad_add_fusion.place, bf16[8,512,512]{2,1,0:T(8,128)(2,1)} %collective-permute-done.received, bf16[8,16,512]{2,1,0:T(8,128)(2,1)S(1)} %collective-permute-done.1.more, ...), custom_call_target="tpu_custom_call", output_to_operand_aliasing={{0}: (5, {})} | custom-call | tf_op jit(solution)/shard_map/pallas_call | solution.py:315
  14.9 106.5 %all_to_all.10.arrived = bf16[16,528,512]{2,1,0:T(8,128)(2,1)S(1)} all-to-all(bf16[16,528,512]{2,1,0:T(8,128)(2,1)S(1)} %get-tuple-element.55), channel_id=1, replica_groups=mesh['layer'=16,'tile'=8] {'layer'}, dimensions={0} | all-to-all | bytes 17301504 | tf_op jit(solution)/shard_map/all_to_all | solution.py:328
  121.5 2.7 %collective-permute-done.2.refs_1_.refs_4_.refs_3_ = bf16[2,528,512]{2,1,0:T(8,128)(2,1)S(1)} collective-permute-done((bf16[2,528,512]{2,1,0:T(8,128)(2,1)S(1)}, bf16[2,528,512]{2,1,0:T(8,128)(2,1)S(1)}, u32[]{:S(2)}, u32[]{:S(2)}) %collective-permute-start.2) | collective-permute-done | bytes 1081376 | tf_op jit(solution)/shard_map/ppermute | solution.py:47
  125.8 3.0 %collective-permute-start.4 = (bf16[2,16,512]{2,1,0:T(8,128)(2,1)S(1)}, bf16[2,16,512]{2,1,0:T(8,128)(2,1)S(1)}, u32[]{:S(2)}, u32[]{:S(2)}) collective-permute-start(bf16[2,16,512]{2,1,0:T(8,128)(2,1)S(1)} %get-tuple-element.56.after), channel_id=1, source_target_pairs={{0,6},{1,7},{8,0},{9,1},{16,8},{17,9},{24,16},{25,17},{56,24},{57,... | collective-permute-start | bytes 98312 | tf_op jit(solution)/shard_map/ppermute | solution.py:47
  128.9 1.6 collective-permute-done.4.refs_1_
  130.5 3.5 %collective-permute-done.3.refs_0_ = bf16[2,16,512]{2,1,0:T(8,128)(2,1)S(1)} collective-permute-done((bf16[2,16,512]{2,1,0:T(8,128)(2,1)S(1)}, bf16[2,16,512]{2,1,0:T(8,128)(2,1)S(1)}, u32[]{:S(2)}, u32[]{:S(2)}) %collective-permute-start.3) | collective-permute-done | bytes 32800 | tf_op jit(solution)/shard_map/ppermute | solution.py:47
  134.0 1.4 shard_map.83
  135.9 2.0 collective-permute-start.6
  137.9 1.9 collective-permute-done.7.refs_1_
  141.1 1.4 shard_map.85
  143.1 2.0 collective-permute-start.9
  145.2 1.9 collective-permute-done.10.refs_1_
  149.8 2.0 collective-permute-start.11
  151.8 1.9 collective-permute-done.12.refs_1_
  156.4 2.1 collective-permute-start.14
  158.4 1.9 collective-permute-done.15.refs_1_
  163.0 2.1 collective-permute-start.16
  165.0 1.9 collective-permute-done.17.refs_1_
  168.2 1.6 shard_map.90
  169.8 2.1 collective-permute-start.18
  171.8 1.9 collective-permute-done.19.refs_1_
  175.0 1.4 shard_map.91
  176.4 2.0 collective-permute-start.20
  178.5 1.9 collective-permute-done.21.refs_1_
  183.1 2.0 collective-permute-start.22
  185.1 1.9 collective-permute-done.23.refs_1_
  189.7 2.0 collective-permute-start.24
  191.7 1.9 collective-permute-done.25.refs_1_
  196.3 2.0 collective-permute-start.26
  198.4 1.9 collective-permute-done.27.refs_1_
  203.0 2.0 collective-permute-start.28
  205.0 1.9 collective-permute-done.29.refs_1_
  209.6 2.0 collective-permute-start.30
  211.6 2.0 collective-permute-done.31.refs_1_
  216.5 1.8 collective-permute-start.32
  218.3 1.9 collective-permute-done.33.refs_1_
  220.2 1.4 collective-permute-done.32.refs_0_
  223.3 2.0 collective-permute-start.34
  225.3 1.9 collective-permute-done.35.refs_1_
  228.4 1.9 shard_map.99
  231.0 1.5 collective-permute-done.36.received
  233.4 15.9 %all_to_all.11.rows = bf16[16,32,640]{2,1,0:T(8,128)(2,1)S(1)} all-to-all(bf16[16,32,640]{2,1,0:T(8,128)(2,1)S(1)} %shard_map.101), channel_id=1, replica_groups=mesh['layer'=16,'tile'=8] {'layer'}, dimensions={0} | all-to-all | bytes 1310720 | tf_op jit(solution)/shard_map/all_to_all | solution.py:373
  251.6 2.0 collective-permute-start.39
  253.6 1.7 collective-permute-done.40.gram_3
  256.6 2.2 collective-permute-done.38.gram_2
  258.9 5.2 %shard_map.103 = (f32[1,32,2,8,512]{4,3,2,1,0:T(8,128)}, f32[32,32]{1,0:T(8,128)}) custom-call(s32[4]{0:T(128)S(1)} %pad_add_fusion.place, f32[32,32]{1,0:T(8,128)S(1)} %add.49.gram_0, f32[32,32]{1,0:T(8,128)S(1)} %collective-permute-done.38.gram_2, f32[32,32]{1,0:T(8,128)S(1)} %collective-permute-done.39.gram_1, ...), custom_call_target="tpu_custom_call" | custom-call | tf_op jit(solution)/shard_map/pallas_call | solution.py:384
  (90 shorter events, 43.4 us)
Async XLA Ops:
  0.6 3.8 %copy-start.1 = (bf16[1,8,2,8,512]{4,3,2,1,0:T(8,128)(2,1)S(1)}, bf16[1,8,2,8,512]{4,3,2,1,0:T(8,128)(2,1)}, u32[]{:S(2)}) copy-start(bf16[1,8,2,8,512]{4,3,2,1,0:T(8,128)(2,1)} %param.6) | copy-start | bytes 393220
  0.6 3.9 %copy-start.3 = (f32[1,2,8,512]{3,2,1,0:T(8,128)S(1)}, f32[1,2,8,512]{3,2,1,0:T(8,128)}, u32[]{:S(2)}) copy-start(f32[1,2,8,512]{3,2,1,0:T(8,128)} %param.11) | copy-start | bytes 98308
  0.7 3.9 %copy-start.2 = (f32[1,2,8,512]{3,2,1,0:T(8,128)S(1)}, f32[1,2,8,512]{3,2,1,0:T(8,128)}, u32[]{:S(2)}) copy-start(f32[1,2,8,512]{3,2,1,0:T(8,128)} %param.10) | copy-start | bytes 98308
  0.7 5.1 %copy-start.5 = (s32[8]{0:T(128)S(1)}, s32[8]{0:T(128)}, u32[]{:S(2)}) copy-start(s32[8]{0:T(128)} %param.7) | copy-start | bytes 100
  0.7 5.1 %copy-start.4 = (f32[2]{0:T(128)S(1)}, f32[2]{0:T(128)}, u32[]{:S(2)}) copy-start(f32[2]{0:T(128)} %param.8) | copy-start | bytes 28
  4.4 7.6 %collective-permute-start = (bf16[8,512,512]{2,1,0:T(8,128)(2,1)}, bf16[8,512,512]{2,1,0:T(8,128)(2,1)}, u32[]{:S(2)}, u32[]{:S(2)}) collective-permute-start(bf16[8,512,512]{2,1,0:T(8,128)(2,1)} %shard_map.77), channel_id=1, source_target_pairs={{0,1},{1,0},{8,9},{9,8},{16,17},{17,16},{24,25},{25,24},{56,57},{5... | collective-permute-start | bytes 12582920 | tf_op jit(solution)/shard_map/ppermute | solution.py:47
  5.2 6.6 %collective-permute-start.1 = (bf16[8,16,512]{2,1,0:T(8,128)(2,1)S(1)}, bf16[8,16,512]{2,1,0:T(8,128)(2,1)S(1)}, u32[]{:S(2)}, u32[]{:S(2)}) collective-permute-start(bf16[8,16,512]{2,1,0:T(8,128)(2,1)S(1)} %dynamic-slice_bitcast_fusion), channel_id=1, source_target_pairs={{0,1},{1,0},{8,9},{9,8},{16,17},{17,16},{24,25},{25,24},{56,57},{5... | collective-permute-start | bytes 393224 | tf_op jit(solution)/shard_map/ppermute | solution.py:47
  6.0 3.4 %copy-start = (bf16[1,2,8,512,512]{4,3,2,1,0:T(8,128)(2,1)S(1)}, bf16[1,2,8,512,512]{4,3,2,1,0:T(8,128)(2,1)}, u32[]{:S(2)}) copy-start(bf16[1,2,8,512,512]{4,3,2,1,0:T(8,128)(2,1)} %blocks.3) | copy-start | bytes 25165828
  121.5 2.8 %collective-permute-start.2 = (bf16[2,528,512]{2,1,0:T(8,128)(2,1)S(1)}, bf16[2,528,512]{2,1,0:T(8,128)(2,1)S(1)}, u32[]{:S(2)}, u32[]{:S(2)}) collective-permute-start(bf16[2,528,512]{2,1,0:T(8,128)(2,1)S(1)} %shard_map.80.refs_0_.refs_2_), channel_id=1, source_target_pairs={{0,1},{1,0},{8,9},{9,8},{16,17},{17,16},{24,25},{25,24},{56,57},{5... | collective-permute-start | bytes 3244040 | tf_op jit(solution)/shard_map/ppermute | solution.py:47
  125.6 8.4 %collective-permute-start.5 = (bf16[2,528,512]{2,1,0:T(8,128)(2,1)S(1)}, bf16[2,528,512]{2,1,0:T(8,128)(2,1)S(1)}, u32[]{:S(2)}, u32[]{:S(2)}) collective-permute-start(bf16[2,528,512]{2,1,0:T(8,128)(2,1)S(1)} %shard_map.82.refs_3_.refs_2_), channel_id=1, source_target_pairs={{0,1},{1,0},{8,9},{9,8},{16,17},{17,16},{24,25},{25,24},{56,57},{5... | collective-permute-start | bytes 3244040 | tf_op jit(solution)/shard_map/ppermute | solution.py:47
  125.8 4.6 %collective-permute-start.4 = (bf16[2,16,512]{2,1,0:T(8,128)(2,1)S(1)}, bf16[2,16,512]{2,1,0:T(8,128)(2,1)S(1)}, u32[]{:S(2)}, u32[]{:S(2)}) collective-permute-start(bf16[2,16,512]{2,1,0:T(8,128)(2,1)S(1)} %get-tuple-element.56.after), channel_id=1, source_target_pairs={{0,6},{1,7},{8,0},{9,1},{16,8},{17,9},{24,16},{25,17},{56,24},{57,... | collective-permute-start | bytes 98312 | tf_op jit(solution)/shard_map/ppermute | solution.py:47
  128.9 5.1 %collective-permute-start.3 = (bf16[2,16,512]{2,1,0:T(8,128)(2,1)S(1)}, bf16[2,16,512]{2,1,0:T(8,128)(2,1)S(1)}, u32[]{:S(2)}, u32[]{:S(2)}) collective-permute-start(bf16[2,16,512]{2,1,0:T(8,128)(2,1)S(1)} %get-tuple-element.56.after), channel_id=1, source_target_pairs={{0,8},{1,9},{8,16},{9,17},{16,24},{17,25},{24,56},{25,57},{56,48},... | collective-permute-start | bytes 98312 | tf_op jit(solution)/shard_map/ppermute | solution.py:47
  135.7 5.4 %collective-permute-start.8 = (bf16[4,528,512]{2,1,0:T(8,128)(2,1)S(1)}, bf16[4,528,512]{2,1,0:T(8,128)(2,1)S(1)}, u32[]{:S(2)}, u32[]{:S(2)}) collective-permute-start(bf16[4,528,512]{2,1,0:T(8,128)(2,1)S(1)} %shard_map.84.refs_3_.refs_2_), channel_id=1, source_target_pairs={{0,1},{1,0},{8,9},{9,8},{16,17},{17,16},{24,25},{25,24},{56,57},{5... | collective-permute-start | bytes 6488072 | tf_op jit(solution)/shard_map/ppermute | solution.py:47
  135.8 4.0 %collective-permute-start.7 = (bf16[2,16,512]{2,1,0:T(8,128)(2,1)S(1)}, bf16[2,16,512]{2,1,0:T(8,128)(2,1)S(1)}, u32[]{:S(2)}, u32[]{:S(2)}) collective-permute-start(bf16[2,16,512]{2,1,0:T(8,128)(2,1)S(1)} %get-tuple-element.59.after), channel_id=1, source_target_pairs={{0,6},{1,7},{8,0},{9,1},{16,8},{17,9},{24,16},{25,17},{56,24},{57,... | collective-permute-start | bytes 98312 | tf_op jit(solution)/shard_map/ppermute | solution.py:47
  135.9 5.2 %collective-permute-start.6 = (bf16[2,16,512]{2,1,0:T(8,128)(2,1)S(1)}, bf16[2,16,512]{2,1,0:T(8,128)(2,1)S(1)}, u32[]{:S(2)}, u32[]{:S(2)}) collective-permute-start(bf16[2,16,512]{2,1,0:T(8,128)(2,1)S(1)} %get-tuple-element.59.after), channel_id=1, source_target_pairs={{0,8},{1,9},{8,16},{9,17},{16,24},{17,25},{24,56},{25,57},{56,48},... | collective-permute-start | bytes 98312 | tf_op jit(solution)/shard_map/ppermute | solution.py:47
  143.0 12.0 %collective-permute-start.13 = (bf16[8,528,512]{2,1,0:T(8,128)(2,1)S(1)}, bf16[8,528,512]{2,1,0:T(8,128)(2,1)S(1)}, u32[]{:S(2)}, u32[]{:S(2)}) collective-permute-start(bf16[8,528,512]{2,1,0:T(8,128)(2,1)S(1)} %shard_map.87.refs_3_.refs_2_), channel_id=1, source_target_pairs={{0,1},{1,0},{8,9},{9,8},{16,17},{17,16},{24,25},{25,24},{56,57},{5... | collective-permute-start | bytes 12976136 | tf_op jit(solution)/shard_map/ppermute | solution.py:47
  143.1 4.0 %collective-permute-start.10 = (bf16[2,16,512]{2,1,0:T(8,128)(2,1)S(1)}, bf16[2,16,512]{2,1,0:T(8,128)(2,1)S(1)}, u32[]{:S(2)}, u32[]{:S(2)}) collective-permute-start(bf16[2,16,512]{2,1,0:T(8,128)(2,1)S(1)} %get-tuple-element.62.after), channel_id=1, source_target_pairs={{0,6},{1,7},{8,0},{9,1},{16,8},{17,9},{24,16},{25,17},{56,24},{57,... | collective-permute-start | bytes 98312 | tf_op jit(solution)/shard_map/ppermute | solution.py:47
  143.1 5.2 %collective-permute-start.9 = (bf16[2,16,512]{2,1,0:T(8,128)(2,1)S(1)}, bf16[2,16,512]{2,1,0:T(8,128)(2,1)S(1)}, u32[]{:S(2)}, u32[]{:S(2)}) collective-permute-start(bf16[2,16,512]{2,1,0:T(8,128)(2,1)S(1)} %get-tuple-element.62.after), channel_id=1, source_target_pairs={{0,8},{1,9},{8,16},{9,17},{16,24},{17,25},{24,56},{25,57},{56,48},... | collective-permute-start | bytes 98312 | tf_op jit(solution)/shard_map/ppermute | solution.py:47
  149.7 4.0 %collective-permute-start.12 = (bf16[2,16,512]{2,1,0:T(8,128)(2,1)S(1)}, bf16[2,16,512]{2,1,0:T(8,128)(2,1)S(1)}, u32[]{:S(2)}, u32[]{:S(2)}) collective-permute-start(bf16[2,16,512]{2,1,0:T(8,128)(2,1)S(1)} %get-tuple-element.65), channel_id=1, source_target_pairs={{0,6},{1,7},{8,0},{9,1},{16,8},{17,9},{24,16},{25,17},{56,24},{57,... | collective-permute-start | bytes 98312 | tf_op jit(solution)/shard_map/ppermute | solution.py:47
  149.8 5.2 %collective-permute-start.11 = (bf16[2,16,512]{2,1,0:T(8,128)(2,1)S(1)}, bf16[2,16,512]{2,1,0:T(8,128)(2,1)S(1)}, u32[]{:S(2)}, u32[]{:S(2)}) collective-permute-start(bf16[2,16,512]{2,1,0:T(8,128)(2,1)S(1)} %get-tuple-element.65), channel_id=1, source_target_pairs={{0,8},{1,9},{8,16},{9,17},{16,24},{17,25},{24,56},{25,57},{56,48},... | collective-permute-start | bytes 98312 | tf_op jit(solution)/shard_map/ppermute | solution.py:47
  156.4 4.0 %collective-permute-start.15 = (bf16[2,16,512]{2,1,0:T(8,128)(2,1)S(1)}, bf16[2,16,512]{2,1,0:T(8,128)(2,1)S(1)}, u32[]{:S(2)}, u32[]{:S(2)}) collective-permute-start(bf16[2,16,512]{2,1,0:T(8,128)(2,1)S(1)} %get-tuple-element.68), channel_id=1, source_target_pairs={{0,6},{1,7},{8,0},{9,1},{16,8},{17,9},{24,16},{25,17},{56,24},{57,... | collective-permute-start | bytes 98312 | tf_op jit(solution)/shard_map/ppermute | solution.py:47
  156.4 5.2 %collective-permute-start.14 = (bf16[2,16,512]{2,1,0:T(8,128)(2,1)S(1)}, bf16[2,16,512]{2,1,0:T(8,128)(2,1)S(1)}, u32[]{:S(2)}, u32[]{:S(2)}) collective-permute-start(bf16[2,16,512]{2,1,0:T(8,128)(2,1)S(1)} %get-tuple-element.68), channel_id=1, source_target_pairs={{0,8},{1,9},{8,16},{9,17},{16,24},{17,25},{24,56},{25,57},{56,48},... | collective-permute-start | bytes 98312 | tf_op jit(solution)/shard_map/ppermute | solution.py:47
  163.0 4.0 %collective-permute-start.17 = (bf16[2,16,512]{2,1,0:T(8,128)(2,1)S(1)}, bf16[2,16,512]{2,1,0:T(8,128)(2,1)S(1)}, u32[]{:S(2)}, u32[]{:S(2)}) collective-permute-start(bf16[2,16,512]{2,1,0:T(8,128)(2,1)S(1)} %get-tuple-element.71), channel_id=1, source_target_pairs={{0,6},{1,7},{8,0},{9,1},{16,8},{17,9},{24,16},{25,17},{56,24},{57,... | collective-permute-start | bytes 98312 | tf_op jit(solution)/shard_map/ppermute | solution.py:47
  163.0 5.2 %collective-permute-start.16 = (bf16[2,16,512]{2,1,0:T(8,128)(2,1)S(1)}, bf16[2,16,512]{2,1,0:T(8,128)(2,1)S(1)}, u32[]{:S(2)}, u32[]{:S(2)}) collective-permute-start(bf16[2,16,512]{2,1,0:T(8,128)(2,1)S(1)} %get-tuple-element.71), channel_id=1, source_target_pairs={{0,8},{1,9},{8,16},{9,17},{16,24},{17,25},{24,56},{25,57},{56,48},... | collective-permute-start | bytes 98312 | tf_op jit(solution)/shard_map/ppermute | solution.py:47
  169.8 4.0 %collective-permute-start.19 = (bf16[2,16,512]{2,1,0:T(8,128)(2,1)S(1)}, bf16[2,16,512]{2,1,0:T(8,128)(2,1)S(1)}, u32[]{:S(2)}, u32[]{:S(2)}) collective-permute-start(bf16[2,16,512]{2,1,0:T(8,128)(2,1)S(1)} %get-tuple-element.74), channel_id=1, source_target_pairs={{0,6},{1,7},{8,0},{9,1},{16,8},{17,9},{24,16},{25,17},{56,24},{57,... | collective-permute-start | bytes 98312 | tf_op jit(solution)/shard_map/ppermute | solution.py:47
  169.8 5.2 %collective-permute-start.18 = (bf16[2,16,512]{2,1,0:T(8,128)(2,1)S(1)}, bf16[2,16,512]{2,1,0:T(8,128)(2,1)S(1)}, u32[]{:S(2)}, u32[]{:S(2)}) collective-permute-start(bf16[2,16,512]{2,1,0:T(8,128)(2,1)S(1)} %get-tuple-element.74), channel_id=1, source_target_pairs={{0,8},{1,9},{8,16},{9,17},{16,24},{17,25},{24,56},{25,57},{56,48},... | collective-permute-start | bytes 98312 | tf_op jit(solution)/shard_map/ppermute | solution.py:47
  176.4 4.0 %collective-permute-start.21 = (bf16[2,16,512]{2,1,0:T(8,128)(2,1)S(1)}, bf16[2,16,512]{2,1,0:T(8,128)(2,1)S(1)}, u32[]{:S(2)}, u32[]{:S(2)}) collective-permute-start(bf16[2,16,512]{2,1,0:T(8,128)(2,1)S(1)} %get-tuple-element.77), channel_id=1, source_target_pairs={{0,6},{1,7},{8,0},{9,1},{16,8},{17,9},{24,16},{25,17},{56,24},{57,... | collective-permute-start | bytes 98312 | tf_op jit(solution)/shard_map/ppermute | solution.py:47
  176.4 5.2 %collective-permute-start.20 = (bf16[2,16,512]{2,1,0:T(8,128)(2,1)S(1)}, bf16[2,16,512]{2,1,0:T(8,128)(2,1)S(1)}, u32[]{:S(2)}, u32[]{:S(2)}) collective-permute-start(bf16[2,16,512]{2,1,0:T(8,128)(2,1)S(1)} %get-tuple-element.77), channel_id=1, source_target_pairs={{0,8},{1,9},{8,16},{9,17},{16,24},{17,25},{24,56},{25,57},{56,48},... | collective-permute-start | bytes 98312 | tf_op jit(solution)/shard_map/ppermute | solution.py:47
  183.0 4.0 %collective-permute-start.23 = (bf16[2,16,512]{2,1,0:T(8,128)(2,1)S(1)}, bf16[2,16,512]{2,1,0:T(8,128)(2,1)S(1)}, u32[]{:S(2)}, u32[]{:S(2)}) collective-permute-start(bf16[2,16,512]{2,1,0:T(8,128)(2,1)S(1)} %get-tuple-element.80), channel_id=1, source_target_pairs={{0,6},{1,7},{8,0},{9,1},{16,8},{17,9},{24,16},{25,17},{56,24},{57,... | collective-permute-start | bytes 98312 | tf_op jit(solution)/shard_map/ppermute | solution.py:47
  183.1 5.1 %collective-permute-start.22 = (bf16[2,16,512]{2,1,0:T(8,128)(2,1)S(1)}, bf16[2,16,512]{2,1,0:T(8,128)(2,1)S(1)}, u32[]{:S(2)}, u32[]{:S(2)}) collective-permute-start(bf16[2,16,512]{2,1,0:T(8,128)(2,1)S(1)} %get-tuple-element.80), channel_id=1, source_target_pairs={{0,8},{1,9},{8,16},{9,17},{16,24},{17,25},{24,56},{25,57},{56,48},... | collective-permute-start | bytes 98312 | tf_op jit(solution)/shard_map/ppermute | solution.py:47
  189.7 4.0 %collective-permute-start.25 = (bf16[2,16,512]{2,1,0:T(8,128)(2,1)S(1)}, bf16[2,16,512]{2,1,0:T(8,128)(2,1)S(1)}, u32[]{:S(2)}, u32[]{:S(2)}) collective-permute-start(bf16[2,16,512]{2,1,0:T(8,128)(2,1)S(1)} %get-tuple-element.83), channel_id=1, source_target_pairs={{0,6},{1,7},{8,0},{9,1},{16,8},{17,9},{24,16},{25,17},{56,24},{57,... | collective-permute-start | bytes 98312 | tf_op jit(solution)/shard_map/ppermute | solution.py:47
  189.7 5.2 %collective-permute-start.24 = (bf16[2,16,512]{2,1,0:T(8,128)(2,1)S(1)}, bf16[2,16,512]{2,1,0:T(8,128)(2,1)S(1)}, u32[]{:S(2)}, u32[]{:S(2)}) collective-permute-start(bf16[2,16,512]{2,1,0:T(8,128)(2,1)S(1)} %get-tuple-element.83), channel_id=1, source_target_pairs={{0,8},{1,9},{8,16},{9,17},{16,24},{17,25},{24,56},{25,57},{56,48},... | collective-permute-start | bytes 98312 | tf_op jit(solution)/shard_map/ppermute | solution.py:47
  196.3 4.0 %collective-permute-start.27 = (bf16[2,16,512]{2,1,0:T(8,128)(2,1)S(1)}, bf16[2,16,512]{2,1,0:T(8,128)(2,1)S(1)}, u32[]{:S(2)}, u32[]{:S(2)}) collective-permute-start(bf16[2,16,512]{2,1,0:T(8,128)(2,1)S(1)} %get-tuple-element.86), channel_id=1, source_target_pairs={{0,6},{1,7},{8,0},{9,1},{16,8},{17,9},{24,16},{25,17},{56,24},{57,... | collective-permute-start | bytes 98312 | tf_op jit(solution)/shard_map/ppermute | solution.py:47
  196.3 5.2 %collective-permute-start.26 = (bf16[2,16,512]{2,1,0:T(8,128)(2,1)S(1)}, bf16[2,16,512]{2,1,0:T(8,128)(2,1)S(1)}, u32[]{:S(2)}, u32[]{:S(2)}) collective-permute-start(bf16[2,16,512]{2,1,0:T(8,128)(2,1)S(1)} %get-tuple-element.86), channel_id=1, source_target_pairs={{0,8},{1,9},{8,16},{9,17},{16,24},{17,25},{24,56},{25,57},{56,48},... | collective-permute-start | bytes 98312 | tf_op jit(solution)/shard_map/ppermute | solution.py:47
  202.9 4.0 %collective-permute-start.29 = (bf16[2,16,512]{2,1,0:T(8,128)(2,1)S(1)}, bf16[2,16,512]{2,1,0:T(8,128)(2,1)S(1)}, u32[]{:S(2)}, u32[]{:S(2)}) collective-permute-start(bf16[2,16,512]{2,1,0:T(8,128)(2,1)S(1)} %get-tuple-element.89), channel_id=1, source_target_pairs={{0,6},{1,7},{8,0},{9,1},{16,8},{17,9},{24,16},{25,17},{56,24},{57,... | collective-permute-start | bytes 98312 | tf_op jit(solution)/shard_map/ppermute | solution.py:47
  203.0 5.2 %collective-permute-start.28 = (bf16[2,16,512]{2,1,0:T(8,128)(2,1)S(1)}, bf16[2,16,512]{2,1,0:T(8,128)(2,1)S(1)}, u32[]{:S(2)}, u32[]{:S(2)}) collective-permute-start(bf16[2,16,512]{2,1,0:T(8,128)(2,1)S(1)} %get-tuple-element.89), channel_id=1, source_target_pairs={{0,8},{1,9},{8,16},{9,17},{16,24},{17,25},{24,56},{25,57},{56,48},... | collective-permute-start | bytes 98312 | tf_op jit(solution)/shard_map/ppermute | solution.py:47
  209.5 4.0 %collective-permute-start.31 = (bf16[2,16,512]{2,1,0:T(8,128)(2,1)S(1)}, bf16[2,16,512]{2,1,0:T(8,128)(2,1)S(1)}, u32[]{:S(2)}, u32[]{:S(2)}) collective-permute-start(bf16[2,16,512]{2,1,0:T(8,128)(2,1)S(1)} %get-tuple-element.92), channel_id=1, source_target_pairs={{0,6},{1,7},{8,0},{9,1},{16,8},{17,9},{24,16},{25,17},{56,24},{57,... | collective-permute-start | bytes 98312 | tf_op jit(solution)/shard_map/ppermute | solution.py:47
  209.6 5.3 %collective-permute-start.30 = (bf16[2,16,512]{2,1,0:T(8,128)(2,1)S(1)}, bf16[2,16,512]{2,1,0:T(8,128)(2,1)S(1)}, u32[]{:S(2)}, u32[]{:S(2)}) collective-permute-start(bf16[2,16,512]{2,1,0:T(8,128)(2,1)S(1)} %get-tuple-element.92), channel_id=1, source_target_pairs={{0,8},{1,9},{8,16},{9,17},{16,24},{17,25},{24,56},{25,57},{56,48},... | collective-permute-start | bytes 98312 | tf_op jit(solution)/shard_map/ppermute | solution.py:47
  216.3 4.0 %collective-permute-start.33 = (bf16[2,16,512]{2,1,0:T(8,128)(2,1)S(1)}, bf16[2,16,512]{2,1,0:T(8,128)(2,1)S(1)}, u32[]{:S(2)}, u32[]{:S(2)}) collective-permute-start(bf16[2,16,512]{2,1,0:T(8,128)(2,1)S(1)} %get-tuple-element.95), channel_id=1, source_target_pairs={{0,6},{1,7},{8,0},{9,1},{16,8},{17,9},{24,16},{25,17},{56,24},{57,... | collective-permute-start | bytes 98312 | tf_op jit(solution)/shard_map/ppermute | solution.py:47
  216.5 5.1 %collective-permute-start.32 = (bf16[2,16,512]{2,1,0:T(8,128)(2,1)S(1)}, bf16[2,16,512]{2,1,0:T(8,128)(2,1)S(1)}, u32[]{:S(2)}, u32[]{:S(2)}) collective-permute-start(bf16[2,16,512]{2,1,0:T(8,128)(2,1)S(1)} %get-tuple-element.95), channel_id=1, source_target_pairs={{0,8},{1,9},{8,16},{9,17},{16,24},{17,25},{24,56},{25,57},{56,48},... | collective-permute-start | bytes 98312 | tf_op jit(solution)/shard_map/ppermute | solution.py:47
  223.0 4.1 %collective-permute-start.35 = (bf16[2,16,512]{2,1,0:T(8,128)(2,1)S(1)}, bf16[2,16,512]{2,1,0:T(8,128)(2,1)S(1)}, u32[]{:S(2)}, u32[]{:S(2)}) collective-permute-start(bf16[2,16,512]{2,1,0:T(8,128)(2,1)S(1)} %get-tuple-element.98), channel_id=1, source_target_pairs={{0,6},{1,7},{8,0},{9,1},{16,8},{17,9},{24,16},{25,17},{56,24},{57,... | collective-permute-start | bytes 98312 | tf_op jit(solution)/shard_map/ppermute | solution.py:47
  223.3 5.2 %collective-permute-start.34 = (bf16[2,16,512]{2,1,0:T(8,128)(2,1)S(1)}, bf16[2,16,512]{2,1,0:T(8,128)(2,1)S(1)}, u32[]{:S(2)}, u32[]{:S(2)}) collective-permute-start(bf16[2,16,512]{2,1,0:T(8,128)(2,1)S(1)} %get-tuple-element.98), channel_id=1, source_target_pairs={{0,8},{1,9},{8,16},{9,17},{16,24},{17,25},{24,56},{25,57},{56,48},... | collective-permute-start | bytes 98312 | tf_op jit(solution)/shard_map/ppermute | solution.py:47
  230.9 1.6 collective-permute-start.36
  250.0 8.9 %collective-permute-start.41 = (bf16[8,32,512]{2,1,0:T(8,128)(2,1)S(1)}, bf16[8,32,512]{2,1,0:T(8,128)(2,1)S(1)}, u32[]{:S(2)}, u32[]{:S(2)}) collective-permute-start(bf16[8,32,512]{2,1,0:T(8,128)(2,1)S(1)} %get-tuple-element.103), channel_id=1, source_target_pairs={{0,1},{1,0},{8,9},{9,8},{16,17},{17,16},{24,25},{25,24},{56,57},{5... | collective-permute-start | bytes 786440 | tf_op jit(solution)/shard_map/ppermute | solution.py:47
  250.1 1.5 collective-permute-start.37
  251.6 3.7 %collective-permute-start.40 = (f32[32,32]{1,0:T(8,128)S(1)}, f32[32,32]{1,0:T(8,128)S(1)}, u32[]{:S(2)}, u32[]{:S(2)}) collective-permute-start(f32[32,32]{1,0:T(8,128)S(1)} %add.49.gram_0), channel_id=1, source_target_pairs={{0,6},{1,7},{2,0},{3,1},{4,2},{5,3},{6,4},{7,5},{8,14},{9,15},{10,... | collective-permute-start | bytes 12296 | tf_op jit(solution)/shard_map/ppermute | solution.py:47
  251.6 5.0 %collective-permute-start.39 = (f32[32,32]{1,0:T(8,128)S(1)}, f32[32,32]{1,0:T(8,128)S(1)}, u32[]{:S(2)}, u32[]{:S(2)}) collective-permute-start(f32[32,32]{1,0:T(8,128)S(1)} %add.49.gram_0), channel_id=1, source_target_pairs={{0,2},{1,3},{2,4},{3,5},{4,6},{5,7},{6,0},{7,1},{8,10},{9,11},{10,... | collective-permute-start | bytes 12296 | tf_op jit(solution)/shard_map/ppermute | solution.py:47
  253.6 5.2 %collective-permute-start.38 = (f32[32,32]{1,0:T(8,128)S(1)}, f32[32,32]{1,0:T(8,128)S(1)}, u32[]{:S(2)}, u32[]{:S(2)}) collective-permute-start(f32[32,32]{1,0:T(8,128)S(1)} %add.49.gram_0), channel_id=1, source_target_pairs={{0,4},{1,5},{2,6},{3,7},{4,0},{5,1},{6,2},{7,3},{8,12},{9,13},{10,... | collective-permute-start | bytes 12296 | tf_op jit(solution)/shard_map/ppermute | solution.py:47

commit v5 on v4

--- a/solution.py
+++ b/solution.py
@@ -15,6 +15,8 @@
 W = 512
 NJ = 32
 HALF = NJ // 2
+LATE = 2
+SENT = 4
 BOUNDS = (0, 2, 4, 8, 16)
 EXTRA = 16
 BLOCK = W + EXTRA
@@ -63,15 +65,15 @@
         copy.wait()
 
 
-def pack_send(blocks, send, held, sems):
+def pack_send(first, blocks, send, held, sems):
     other = 1 - lax.axis_index("tile") % 2
     entering = start_all([
-        pltpu.make_async_copy(blocks.at[0, other, i], held.at[i], sems.at[i]) for i in range(8)
+        pltpu.make_async_copy(blocks.at[0, other, first + i], held.at[i], sems.at[i]) for i in range(SENT)
     ])
     leaving = []
-    for i in range(8):
+    for i in range(SENT):
         entering[i].wait()
-        leaving += start_all([pltpu.make_async_copy(held.at[i], send.at[i], sems.at[8 + i])])
+        leaving += start_all([pltpu.make_async_copy(held.at[i], send.at[i], sems.at[SENT + i])])
     wait_all(leaving)
 
 
@@ -86,11 +88,12 @@
     wait_all(copies)
 
 
-def pack_other(place, received, more, phases, taper, part, out, phases_out, taper_out, sems):
+def pack_other(place, received_0, received_1, more, phases, taper, part, out, phases_out, taper_out, sems):
     core, y = place[0], place[1]
     to = [spot(8 * (1 - core) + i, y) for i in range(8)]
     copies = start_all([
-        pltpu.make_async_copy(received.at[i], out.at[to[i], pl.ds(0, W)], sems.at[i]) for i in range(8)
+        pltpu.make_async_copy(received.at[i], out.at[to[at + i], pl.ds(0, W)], sems.at[at + i])
+        for at, received in ((0, received_0), (SENT, received_1)) for i in range(SENT)
     ] + [
         pltpu.make_async_copy(more.at[i], out.at[to[i], pl.ds(W, EXTRA)], sems.at[8 + i]) for i in range(8)
     ])
@@ -205,16 +208,17 @@
     return out
 
 
-def share_kernel(place, up, send):
-    for layer in range(NL):
-        send[layer] = up[1 - place[0], layer].astype(BF16)
-
-
-def gram_kernel(place, up, received, send):
+def share_kernel(start, place, up, send):
+    for at in range(send.shape[0]):
+        send[at] = up[1 - place[0], start + at].astype(BF16)
+
+
+def gram_kernel(place, up, late, early, send):
     core = place[0]
     total = jnp.zeros((NJ, NJ), F32)
     for layer in range(NL):
-        own, other = up[core, layer], received[layer].astype(F32)
+        own = up[core, layer]
+        other = (late[layer] if layer < LATE else early[layer - LATE]).astype(F32)
         low, high = jnp.where(core == 0, own, other), jnp.where(core == 0, other, own)
         rows = jnp.concatenate([low, high], axis=0).astype(BF16)
         total += lax.dot_general(
@@ -294,15 +298,20 @@
     port_taper = 1.0 / (1.0 + offsets * offsets)
     angle = frequencies[None, :] * (jnp.arange(NL, dtype=F32)[:, None] + 1.0)
     phases = jnp.stack([jnp.cos(angle), jnp.sin(angle)], axis=2).reshape(NL, 4)
-    to_send = pl.pallas_call(
-        pack_send,
-        out_shape=jax.ShapeDtypeStruct((8, W, W), BF16),
-        in_specs=[ANY],
-        out_specs=ANY,
-        scratch_shapes=[pltpu.VMEM((8, W, W), BF16), pltpu.SemaphoreType.DMA((16,))],
-        compiler_params=ALONE,
-    )(layer_inverse)
-    received = swap(to_send, CORE)
+    received = [
+        swap(
+            pl.pallas_call(
+                functools.partial(pack_send, first),
+                out_shape=jax.ShapeDtypeStruct((SENT, W, W), BF16),
+                in_specs=[ANY],
+                out_specs=ANY,
+                scratch_shapes=[pltpu.VMEM((SENT, W, W), BF16), pltpu.SemaphoreType.DMA((2 * SENT,))],
+                compiler_params=ALONE,
+            )(layer_inverse),
+            CORE,
+        )
+        for first in (0, SENT)
+    ]
     more = swap(lax.dynamic_index_in_dim(extras, 1 - core, 0, keepdims=False), CORE)
     part = pl.pallas_call(
         pack_own,
@@ -319,12 +328,12 @@
             jax.ShapeDtypeStruct(phases.shape, F32),
             jax.ShapeDtypeStruct(port_taper.shape, F32),
         ),
-        in_specs=[SMEM, VMEM, VMEM, VMEM, VMEM, ANY],
+        in_specs=[SMEM] + [VMEM] * 5 + [ANY],
         out_specs=(ANY, VMEM, VMEM),
-        input_output_aliases={5: 0},
+        input_output_aliases={6: 0},
         scratch_shapes=[pltpu.SemaphoreType.DMA((16,))],
         compiler_params=PARAMS,
-    )(place, received, more, phases, port_taper, part)
+    )(place, *received, more, phases, port_taper, part)
     arrived = lax.all_to_all(packed, "layer", 0, 0, tiled=True)
 
     parts, others = [], []
@@ -345,6 +354,15 @@
     run = lambda x_steps, y_steps, near, state: sweep(
         x_steps, y_steps, place, phases, port_taper, near, parts, others, state
     )
+    def share(up, start, end):
+        return pl.pallas_call(
+            functools.partial(share_kernel, start),
+            out_shape=jax.ShapeDtypeStruct((end - start, HALF, W), BF16),
+            in_specs=[SMEM, VMEM],
+            out_specs=VMEM,
+            compiler_params=PARAMS,
+        )(place, up)
+
     trade(port_taper)
     down, up, pair = run(range(1), range(2), (), ())
     last = len(STEPS)
@@ -352,24 +370,20 @@
         near = (swap(pair, RAISE), swap(pair, LOWER))
         if len(parts) < len(BOUNDS) - 1:
             trade(pair)
+        if at + 2 == last:
+            early = swap(share(up, LATE, NL), CORE)
         down, up, pair = run(
             range(at, min(at + 2, last)), range(at + 1, min(at + 3, last)), near, (down, up)
         )
 
-    shared = pl.pallas_call(
-        share_kernel,
-        out_shape=jax.ShapeDtypeStruct((NL, HALF, W), BF16),
-        in_specs=[SMEM, VMEM],
-        out_specs=VMEM,
-        compiler_params=PARAMS,
-    )(place, up)
+    late = swap(share(up, 0, LATE), CORE)
     basis = pl.pallas_call(
         gram_kernel,
         out_shape=jax.ShapeDtypeStruct((NL, NJ, W + TAIL), BF16),
-        in_specs=[SMEM, VMEM, VMEM],
+        in_specs=[SMEM, VMEM, VMEM, VMEM],
         out_specs=VMEM,
         compiler_params=PARAMS,
-    )(place, up, swap(shared, CORE))
+    )(place, up, late, early)
     rows = lax.all_to_all(basis, "layer", 0, 0, tiled=True)
     gram, back = pl.pallas_call(
         collect_kernel,

time: 264 us -> 264 us (level)
    pallas_call x2 -> x4, Pallas kernels: 4.25 us -> 6.08 us  [the longest x2 4.96 us: per_device(): pl.pallas_call(functools.partial(pack_send, first), out_shape=jax.ShapeDt...]
    ppermute x42 -> x44, waiting for transfers between devices: 61.6 us -> 59.8 us  [swap(): return lax.ppermute(value, AXES, pairs)]
    ppermute x42 -> x44, starting transfers between devices: 35.8 us -> 35.9 us  [swap(): return lax.ppermute(value, AXES, pairs)]
  transfers between devices with their start and end apart: 42 -> 44, of which waited for: 38 -> 36; matrix products, arithmetic and copies ran while one was open for 0% -> 0% of each run, Pallas kernels for 1% -> 3%
where the time goes in v5:
time: 264 us
  blocking collectives  123 us (47%)
  waiting for transfers between devices  59.8 us (23%)
  Pallas kernels  40.1 us (15%)
  starting transfers between devices  35.9 us (14%)
  local copies, waits for them, and re-layouts  3.96 us (2%)
    all_to_all x1, blocking collectives, per_device(): arrived = lax.all_to_all(packed, 'layer', 0, 0, tiled=True)  107 us
    ppermute x44, waiting for transfers between devices, swap(): return lax.ppermute(value, AXES, pairs)  59.8 us
    ppermute x44, starting transfers between devices, swap(): return lax.ppermute(value, AXES, pairs)  35.9 us
    pallas_call x16, Pallas kernels, sweep(): pl.pallas_call(functools.partial(sweep_kernel, x_steps, y_steps, chunks),...  22.8 us
    all_to_all x1, blocking collectives, per_device(): rows = lax.all_to_all(basis, 'layer', 0, 0, tiled=True)  15.9 us
  transfers between devices with their start and end apart: 44, of which 36 were waited for; matrix products, arithmetic and copies ran while one was open for 0% of the time, Pallas kernels for 3%

profile of v5, /device:TPU:0, one launch (start us, length us, event | category | flops | bytes accessed | tf_op | source)
XLA Modules:
  0.0 264.0 jit_solution(17625800702253827520)
XLA Ops:
  0.6 2.5 shard_map.78
  3.3 2.5 shard_map.77
  7.5 3.4 %copy-done = bf16[1,2,8,512,512]{4,3,2,1,0:T(8,128)(2,1)S(1)} copy-done((bf16[1,2,8,512,512]{4,3,2,1,0:T(8,128)(2,1)S(1)}, bf16[1,2,8,512,512]{4,3,2,1,0:T(8,128)(2,1)}, u32[]{:S(2)}) %copy-start) | copy-done | bytes 8388632
  12.0 2.3 shard_map.80
  14.4 106.7 %all_to_all.10.arrived = bf16[16,528,512]{2,1,0:T(8,128)(2,1)S(1)} all-to-all(bf16[16,528,512]{2,1,0:T(8,128)(2,1)S(1)} %get-tuple-element.55), channel_id=1, replica_groups=mesh['layer'=16,'tile'=8] {'layer'}, dimensions={0} | all-to-all | bytes 17301504 | tf_op jit(solution)/shard_map/all_to_all | solution.py:337
  121.3 2.7 %collective-permute-done.3.refs_1_.refs_4_.refs_3_ = bf16[2,528,512]{2,1,0:T(8,128)(2,1)S(1)} collective-permute-done((bf16[2,528,512]{2,1,0:T(8,128)(2,1)S(1)}, bf16[2,528,512]{2,1,0:T(8,128)(2,1)S(1)}, u32[]{:S(2)}, u32[]{:S(2)}) %collective-permute-start.3) | collective-permute-done | bytes 1081376 | tf_op jit(solution)/shard_map/ppermute | solution.py:49
  125.6 3.0 %collective-permute-start.5 = (bf16[2,16,512]{2,1,0:T(8,128)(2,1)S(1)}, bf16[2,16,512]{2,1,0:T(8,128)(2,1)S(1)}, u32[]{:S(2)}, u32[]{:S(2)}) collective-permute-start(bf16[2,16,512]{2,1,0:T(8,128)(2,1)S(1)} %get-tuple-element.56.after), channel_id=1, source_target_pairs={{0,6},{1,7},{8,0},{9,1},{16,8},{17,9},{24,16},{25,17},{56,24},{57,... | collective-permute-start | bytes 98312 | tf_op jit(solution)/shard_map/ppermute | solution.py:49
  128.7 1.6 collective-permute-done.5.refs_1_
  130.3 3.5 %collective-permute-done.4.refs_0_ = bf16[2,16,512]{2,1,0:T(8,128)(2,1)S(1)} collective-permute-done((bf16[2,16,512]{2,1,0:T(8,128)(2,1)S(1)}, bf16[2,16,512]{2,1,0:T(8,128)(2,1)S(1)}, u32[]{:S(2)}, u32[]{:S(2)}) %collective-permute-start.4) | collective-permute-done | bytes 32800 | tf_op jit(solution)/shard_map/ppermute | solution.py:49
  133.8 1.4 shard_map.84
  135.6 2.0 collective-permute-start.7
  137.7 1.9 collective-permute-done.8.refs_1_
  140.8 1.4 shard_map.86
  142.9 2.0 collective-permute-start.10
  144.9 1.9 collective-permute-done.11.refs_1_
  149.6 2.0 collective-permute-start.12
  151.6 1.9 collective-permute-done.13.refs_1_
  156.2 2.1 collective-permute-start.15
  158.2 1.9 collective-permute-done.16.refs_1_
  162.8 2.1 collective-permute-start.17
  164.8 1.9 collective-permute-done.18.refs_1_
  166.7 1.4 collective-permute-done.17.refs_0_
  169.6 2.1 collective-permute-start.19
  171.6 1.9 collective-permute-done.20.refs_1_
  174.8 1.4 shard_map.92
  176.2 2.0 collective-permute-start.21
  178.2 1.9 collective-permute-done.22.refs_1_
  182.9 2.0 collective-permute-start.23
  184.9 1.9 collective-permute-done.24.refs_1_
  189.5 2.0 collective-permute-start.25
  191.5 1.9 collective-permute-done.26.refs_1_
  196.1 2.0 collective-permute-start.27
  198.1 1.9 collective-permute-done.28.refs_1_
  202.7 2.0 collective-permute-start.29
  204.8 1.9 collective-permute-done.30.refs_1_
  209.4 2.0 collective-permute-start.31
  211.4 1.9 collective-permute-done.32.refs_1_
  216.0 2.0 collective-permute-start.33
  218.0 1.9 collective-permute-done.34.refs_1_
  221.2 1.5 shard_map.99
  223.5 2.0 collective-permute-start.35
  225.5 1.9 collective-permute-done.36.refs_1_
  228.7 1.9 shard_map.100
  233.3 15.9 %all_to_all.11.rows = bf16[16,32,640]{2,1,0:T(8,128)(2,1)S(1)} all-to-all(bf16[16,32,640]{2,1,0:T(8,128)(2,1)S(1)} %shard_map.103), channel_id=1, replica_groups=mesh['layer'=16,'tile'=8] {'layer'}, dimensions={0} | all-to-all | bytes 1310720 | tf_op jit(solution)/shard_map/all_to_all | solution.py:387
  251.5 2.0 collective-permute-start.41
  253.6 1.7 collective-permute-done.42.gram_3
  256.5 2.2 collective-permute-done.40.gram_2
  258.8 5.2 %shard_map.105 = (f32[1,32,2,8,512]{4,3,2,1,0:T(8,128)}, f32[32,32]{1,0:T(8,128)}) custom-call(s32[4]{0:T(128)S(1)} %pad_add_fusion.place, f32[32,32]{1,0:T(8,128)S(1)} %add.49.gram_0, f32[32,32]{1,0:T(8,128)S(1)} %collective-permute-done.40.gram_2, f32[32,32]{1,0:T(8,128)S(1)} %collective-permute-done.41.gram_1, ...), custom_call_target="tpu_custom_call" | custom-call | tf_op jit(solution)/shard_map/pallas_call | solution.py:398
  (96 shorter events, 43.6 us)
Async XLA Ops:
  3.1 3.3 %copy-start.2 = (f32[1,2,8,512]{3,2,1,0:T(8,128)S(1)}, f32[1,2,8,512]{3,2,1,0:T(8,128)}, u32[]{:S(2)}) copy-start(f32[1,2,8,512]{3,2,1,0:T(8,128)} %param.10) | copy-start | bytes 98308
  3.2 4.0 %copy-start.5 = (s32[8]{0:T(128)S(1)}, s32[8]{0:T(128)}, u32[]{:S(2)}) copy-start(s32[8]{0:T(128)} %param.7) | copy-start | bytes 100
  3.2 4.0 %copy-start.4 = (f32[2]{0:T(128)S(1)}, f32[2]{0:T(128)}, u32[]{:S(2)}) copy-start(f32[2]{0:T(128)} %param.8) | copy-start | bytes 28
  3.2 8.8 %collective-permute-start.1 = (bf16[4,512,512]{2,1,0:T(8,128)(2,1)}, bf16[4,512,512]{2,1,0:T(8,128)(2,1)S(1)}, u32[]{:S(2)}, u32[]{:S(2)}) collective-permute-start(bf16[4,512,512]{2,1,0:T(8,128)(2,1)} %shard_map.78), channel_id=1, source_target_pairs={{0,1},{1,0},{8,9},{9,8},{16,17},{17,16},{24,25},{25,24},{56,57},{5... | collective-permute-start | bytes 6291464 | tf_op jit(solution)/shard_map/ppermute | solution.py:49
  5.8 6.3 %collective-permute-start = (bf16[4,512,512]{2,1,0:T(8,128)(2,1)}, bf16[4,512,512]{2,1,0:T(8,128)(2,1)}, u32[]{:S(2)}, u32[]{:S(2)}) collective-permute-start(bf16[4,512,512]{2,1,0:T(8,128)(2,1)} %shard_map.77), channel_id=1, source_target_pairs={{0,1},{1,0},{8,9},{9,8},{16,17},{17,16},{24,25},{25,24},{56,57},{5... | collective-permute-start | bytes 6291464 | tf_op jit(solution)/shard_map/ppermute | solution.py:49
  7.0 5.0 %collective-permute-start.2 = (bf16[8,16,512]{2,1,0:T(8,128)(2,1)S(1)}, bf16[8,16,512]{2,1,0:T(8,128)(2,1)S(1)}, u32[]{:S(2)}, u32[]{:S(2)}) collective-permute-start(bf16[8,16,512]{2,1,0:T(8,128)(2,1)S(1)} %dynamic-slice_bitcast_fusion), channel_id=1, source_target_pairs={{0,1},{1,0},{8,9},{9,8},{16,17},{17,16},{24,25},{25,24},{56,57},{5... | collective-permute-start | bytes 393224 | tf_op jit(solution)/shard_map/ppermute | solution.py:49
  7.5 3.4 %copy-start = (bf16[1,2,8,512,512]{4,3,2,1,0:T(8,128)(2,1)S(1)}, bf16[1,2,8,512,512]{4,3,2,1,0:T(8,128)(2,1)}, u32[]{:S(2)}) copy-start(bf16[1,2,8,512,512]{4,3,2,1,0:T(8,128)(2,1)} %blocks.5) | copy-start | bytes 25165828
  121.2 2.8 %collective-permute-start.3 = (bf16[2,528,512]{2,1,0:T(8,128)(2,1)S(1)}, bf16[2,528,512]{2,1,0:T(8,128)(2,1)S(1)}, u32[]{:S(2)}, u32[]{:S(2)}) collective-permute-start(bf16[2,528,512]{2,1,0:T(8,128)(2,1)S(1)} %shard_map.81.refs_0_.refs_2_), channel_id=1, source_target_pairs={{0,1},{1,0},{8,9},{9,8},{16,17},{17,16},{24,25},{25,24},{56,57},{5... | collective-permute-start | bytes 3244040 | tf_op jit(solution)/shard_map/ppermute | solution.py:49
  125.4 8.4 %collective-permute-start.6 = (bf16[2,528,512]{2,1,0:T(8,128)(2,1)S(1)}, bf16[2,528,512]{2,1,0:T(8,128)(2,1)S(1)}, u32[]{:S(2)}, u32[]{:S(2)}) collective-permute-start(bf16[2,528,512]{2,1,0:T(8,128)(2,1)S(1)} %shard_map.83.refs_3_.refs_2_), channel_id=1, source_target_pairs={{0,1},{1,0},{8,9},{9,8},{16,17},{17,16},{24,25},{25,24},{56,57},{5... | collective-permute-start | bytes 3244040 | tf_op jit(solution)/shard_map/ppermute | solution.py:49
  125.6 4.6 %collective-permute-start.5 = (bf16[2,16,512]{2,1,0:T(8,128)(2,1)S(1)}, bf16[2,16,512]{2,1,0:T(8,128)(2,1)S(1)}, u32[]{:S(2)}, u32[]{:S(2)}) collective-permute-start(bf16[2,16,512]{2,1,0:T(8,128)(2,1)S(1)} %get-tuple-element.56.after), channel_id=1, source_target_pairs={{0,6},{1,7},{8,0},{9,1},{16,8},{17,9},{24,16},{25,17},{56,24},{57,... | collective-permute-start | bytes 98312 | tf_op jit(solution)/shard_map/ppermute | solution.py:49
  128.7 5.1 %collective-permute-start.4 = (bf16[2,16,512]{2,1,0:T(8,128)(2,1)S(1)}, bf16[2,16,512]{2,1,0:T(8,128)(2,1)S(1)}, u32[]{:S(2)}, u32[]{:S(2)}) collective-permute-start(bf16[2,16,512]{2,1,0:T(8,128)(2,1)S(1)} %get-tuple-element.56.after), channel_id=1, source_target_pairs={{0,8},{1,9},{8,16},{9,17},{16,24},{17,25},{24,56},{25,57},{56,48},... | collective-permute-start | bytes 98312 | tf_op jit(solution)/shard_map/ppermute | solution.py:49
  135.5 5.4 %collective-permute-start.9 = (bf16[4,528,512]{2,1,0:T(8,128)(2,1)S(1)}, bf16[4,528,512]{2,1,0:T(8,128)(2,1)S(1)}, u32[]{:S(2)}, u32[]{:S(2)}) collective-permute-start(bf16[4,528,512]{2,1,0:T(8,128)(2,1)S(1)} %shard_map.85.refs_3_.refs_2_), channel_id=1, source_target_pairs={{0,1},{1,0},{8,9},{9,8},{16,17},{17,16},{24,25},{25,24},{56,57},{5... | collective-permute-start | bytes 6488072 | tf_op jit(solution)/shard_map/ppermute | solution.py:49
  135.6 4.0 %collective-permute-start.8 = (bf16[2,16,512]{2,1,0:T(8,128)(2,1)S(1)}, bf16[2,16,512]{2,1,0:T(8,128)(2,1)S(1)}, u32[]{:S(2)}, u32[]{:S(2)}) collective-permute-start(bf16[2,16,512]{2,1,0:T(8,128)(2,1)S(1)} %get-tuple-element.59.after), channel_id=1, source_target_pairs={{0,6},{1,7},{8,0},{9,1},{16,8},{17,9},{24,16},{25,17},{56,24},{57,... | collective-permute-start | bytes 98312 | tf_op jit(solution)/shard_map/ppermute | solution.py:49
  135.6 5.2 %collective-permute-start.7 = (bf16[2,16,512]{2,1,0:T(8,128)(2,1)S(1)}, bf16[2,16,512]{2,1,0:T(8,128)(2,1)S(1)}, u32[]{:S(2)}, u32[]{:S(2)}) collective-permute-start(bf16[2,16,512]{2,1,0:T(8,128)(2,1)S(1)} %get-tuple-element.59.after), channel_id=1, source_target_pairs={{0,8},{1,9},{8,16},{9,17},{16,24},{17,25},{24,56},{25,57},{56,48},... | collective-permute-start | bytes 98312 | tf_op jit(solution)/shard_map/ppermute | solution.py:49
  142.8 12.0 %collective-permute-start.14 = (bf16[8,528,512]{2,1,0:T(8,128)(2,1)S(1)}, bf16[8,528,512]{2,1,0:T(8,128)(2,1)S(1)}, u32[]{:S(2)}, u32[]{:S(2)}) collective-permute-start(bf16[8,528,512]{2,1,0:T(8,128)(2,1)S(1)} %shard_map.88.refs_3_.refs_2_), channel_id=1, source_target_pairs={{0,1},{1,0},{8,9},{9,8},{16,17},{17,16},{24,25},{25,24},{56,57},{5... | collective-permute-start | bytes 12976136 | tf_op jit(solution)/shard_map/ppermute | solution.py:49
  142.8 4.0 %collective-permute-start.11 = (bf16[2,16,512]{2,1,0:T(8,128)(2,1)S(1)}, bf16[2,16,512]{2,1,0:T(8,128)(2,1)S(1)}, u32[]{:S(2)}, u32[]{:S(2)}) collective-permute-start(bf16[2,16,512]{2,1,0:T(8,128)(2,1)S(1)} %get-tuple-element.62.after), channel_id=1, source_target_pairs={{0,6},{1,7},{8,0},{9,1},{16,8},{17,9},{24,16},{25,17},{56,24},{57,... | collective-permute-start | bytes 98312 | tf_op jit(solution)/shard_map/ppermute | solution.py:49
  142.9 5.2 %collective-permute-start.10 = (bf16[2,16,512]{2,1,0:T(8,128)(2,1)S(1)}, bf16[2,16,512]{2,1,0:T(8,128)(2,1)S(1)}, u32[]{:S(2)}, u32[]{:S(2)}) collective-permute-start(bf16[2,16,512]{2,1,0:T(8,128)(2,1)S(1)} %get-tuple-element.62.after), channel_id=1, source_target_pairs={{0,8},{1,9},{8,16},{9,17},{16,24},{17,25},{24,56},{25,57},{56,48},... | collective-permute-start | bytes 98312 | tf_op jit(solution)/shard_map/ppermute | solution.py:49
  149.5 4.0 %collective-permute-start.13 = (bf16[2,16,512]{2,1,0:T(8,128)(2,1)S(1)}, bf16[2,16,512]{2,1,0:T(8,128)(2,1)S(1)}, u32[]{:S(2)}, u32[]{:S(2)}) collective-permute-start(bf16[2,16,512]{2,1,0:T(8,128)(2,1)S(1)} %get-tuple-element.65), channel_id=1, source_target_pairs={{0,6},{1,7},{8,0},{9,1},{16,8},{17,9},{24,16},{25,17},{56,24},{57,... | collective-permute-start | bytes 98312 | tf_op jit(solution)/shard_map/ppermute | solution.py:49
  149.6 5.2 %collective-permute-start.12 = (bf16[2,16,512]{2,1,0:T(8,128)(2,1)S(1)}, bf16[2,16,512]{2,1,0:T(8,128)(2,1)S(1)}, u32[]{:S(2)}, u32[]{:S(2)}) collective-permute-start(bf16[2,16,512]{2,1,0:T(8,128)(2,1)S(1)} %get-tuple-element.65), channel_id=1, source_target_pairs={{0,8},{1,9},{8,16},{9,17},{16,24},{17,25},{24,56},{25,57},{56,48},... | collective-permute-start | bytes 98312 | tf_op jit(solution)/shard_map/ppermute | solution.py:49
  156.1 4.0 %collective-permute-start.16 = (bf16[2,16,512]{2,1,0:T(8,128)(2,1)S(1)}, bf16[2,16,512]{2,1,0:T(8,128)(2,1)S(1)}, u32[]{:S(2)}, u32[]{:S(2)}) collective-permute-start(bf16[2,16,512]{2,1,0:T(8,128)(2,1)S(1)} %get-tuple-element.68), channel_id=1, source_target_pairs={{0,6},{1,7},{8,0},{9,1},{16,8},{17,9},{24,16},{25,17},{56,24},{57,... | collective-permute-start | bytes 98312 | tf_op jit(solution)/shard_map/ppermute | solution.py:49
  156.2 5.2 %collective-permute-start.15 = (bf16[2,16,512]{2,1,0:T(8,128)(2,1)S(1)}, bf16[2,16,512]{2,1,0:T(8,128)(2,1)S(1)}, u32[]{:S(2)}, u32[]{:S(2)}) collective-permute-start(bf16[2,16,512]{2,1,0:T(8,128)(2,1)S(1)} %get-tuple-element.68), channel_id=1, source_target_pairs={{0,8},{1,9},{8,16},{9,17},{16,24},{17,25},{24,56},{25,57},{56,48},... | collective-permute-start | bytes 98312 | tf_op jit(solution)/shard_map/ppermute | solution.py:49
  162.8 4.0 %collective-permute-start.18 = (bf16[2,16,512]{2,1,0:T(8,128)(2,1)S(1)}, bf16[2,16,512]{2,1,0:T(8,128)(2,1)S(1)}, u32[]{:S(2)}, u32[]{:S(2)}) collective-permute-start(bf16[2,16,512]{2,1,0:T(8,128)(2,1)S(1)} %get-tuple-element.71), channel_id=1, source_target_pairs={{0,6},{1,7},{8,0},{9,1},{16,8},{17,9},{24,16},{25,17},{56,24},{57,... | collective-permute-start | bytes 98312 | tf_op jit(solution)/shard_map/ppermute | solution.py:49
  162.8 5.4 %collective-permute-start.17 = (bf16[2,16,512]{2,1,0:T(8,128)(2,1)S(1)}, bf16[2,16,512]{2,1,0:T(8,128)(2,1)S(1)}, u32[]{:S(2)}, u32[]{:S(2)}) collective-permute-start(bf16[2,16,512]{2,1,0:T(8,128)(2,1)S(1)} %get-tuple-element.71), channel_id=1, source_target_pairs={{0,8},{1,9},{8,16},{9,17},{16,24},{17,25},{24,56},{25,57},{56,48},... | collective-permute-start | bytes 98312 | tf_op jit(solution)/shard_map/ppermute | solution.py:49
  169.6 4.0 %collective-permute-start.20 = (bf16[2,16,512]{2,1,0:T(8,128)(2,1)S(1)}, bf16[2,16,512]{2,1,0:T(8,128)(2,1)S(1)}, u32[]{:S(2)}, u32[]{:S(2)}) collective-permute-start(bf16[2,16,512]{2,1,0:T(8,128)(2,1)S(1)} %get-tuple-element.74), channel_id=1, source_target_pairs={{0,6},{1,7},{8,0},{9,1},{16,8},{17,9},{24,16},{25,17},{56,24},{57,... | collective-permute-start | bytes 98312 | tf_op jit(solution)/shard_map/ppermute | solution.py:49
  169.6 5.2 %collective-permute-start.19 = (bf16[2,16,512]{2,1,0:T(8,128)(2,1)S(1)}, bf16[2,16,512]{2,1,0:T(8,128)(2,1)S(1)}, u32[]{:S(2)}, u32[]{:S(2)}) collective-permute-start(bf16[2,16,512]{2,1,0:T(8,128)(2,1)S(1)} %get-tuple-element.74), channel_id=1, source_target_pairs={{0,8},{1,9},{8,16},{9,17},{16,24},{17,25},{24,56},{25,57},{56,48},... | collective-permute-start | bytes 98312 | tf_op jit(solution)/shard_map/ppermute | solution.py:49
  176.2 4.0 %collective-permute-start.22 = (bf16[2,16,512]{2,1,0:T(8,128)(2,1)S(1)}, bf16[2,16,512]{2,1,0:T(8,128)(2,1)S(1)}, u32[]{:S(2)}, u32[]{:S(2)}) collective-permute-start(bf16[2,16,512]{2,1,0:T(8,128)(2,1)S(1)} %get-tuple-element.77), channel_id=1, source_target_pairs={{0,6},{1,7},{8,0},{9,1},{16,8},{17,9},{24,16},{25,17},{56,24},{57,... | collective-permute-start | bytes 98312 | tf_op jit(solution)/shard_map/ppermute | solution.py:49
  176.2 5.2 %collective-permute-start.21 = (bf16[2,16,512]{2,1,0:T(8,128)(2,1)S(1)}, bf16[2,16,512]{2,1,0:T(8,128)(2,1)S(1)}, u32[]{:S(2)}, u32[]{:S(2)}) collective-permute-start(bf16[2,16,512]{2,1,0:T(8,128)(2,1)S(1)} %get-tuple-element.77), channel_id=1, source_target_pairs={{0,8},{1,9},{8,16},{9,17},{16,24},{17,25},{24,56},{25,57},{56,48},... | collective-permute-start | bytes 98312 | tf_op jit(solution)/shard_map/ppermute | solution.py:49
  182.8 4.0 %collective-permute-start.24 = (bf16[2,16,512]{2,1,0:T(8,128)(2,1)S(1)}, bf16[2,16,512]{2,1,0:T(8,128)(2,1)S(1)}, u32[]{:S(2)}, u32[]{:S(2)}) collective-permute-start(bf16[2,16,512]{2,1,0:T(8,128)(2,1)S(1)} %get-tuple-element.80), channel_id=1, source_target_pairs={{0,6},{1,7},{8,0},{9,1},{16,8},{17,9},{24,16},{25,17},{56,24},{57,... | collective-permute-start | bytes 98312 | tf_op jit(solution)/shard_map/ppermute | solution.py:49
  182.9 5.1 %collective-permute-start.23 = (bf16[2,16,512]{2,1,0:T(8,128)(2,1)S(1)}, bf16[2,16,512]{2,1,0:T(8,128)(2,1)S(1)}, u32[]{:S(2)}, u32[]{:S(2)}) collective-permute-start(bf16[2,16,512]{2,1,0:T(8,128)(2,1)S(1)} %get-tuple-element.80), channel_id=1, source_target_pairs={{0,8},{1,9},{8,16},{9,17},{16,24},{17,25},{24,56},{25,57},{56,48},... | collective-permute-start | bytes 98312 | tf_op jit(solution)/shard_map/ppermute | solution.py:49
  189.4 4.0 %collective-permute-start.26 = (bf16[2,16,512]{2,1,0:T(8,128)(2,1)S(1)}, bf16[2,16,512]{2,1,0:T(8,128)(2,1)S(1)}, u32[]{:S(2)}, u32[]{:S(2)}) collective-permute-start(bf16[2,16,512]{2,1,0:T(8,128)(2,1)S(1)} %get-tuple-element.83), channel_id=1, source_target_pairs={{0,6},{1,7},{8,0},{9,1},{16,8},{17,9},{24,16},{25,17},{56,24},{57,... | collective-permute-start | bytes 98312 | tf_op jit(solution)/shard_map/ppermute | solution.py:49
  189.5 5.2 %collective-permute-start.25 = (bf16[2,16,512]{2,1,0:T(8,128)(2,1)S(1)}, bf16[2,16,512]{2,1,0:T(8,128)(2,1)S(1)}, u32[]{:S(2)}, u32[]{:S(2)}) collective-permute-start(bf16[2,16,512]{2,1,0:T(8,128)(2,1)S(1)} %get-tuple-element.83), channel_id=1, source_target_pairs={{0,8},{1,9},{8,16},{9,17},{16,24},{17,25},{24,56},{25,57},{56,48},... | collective-permute-start | bytes 98312 | tf_op jit(solution)/shard_map/ppermute | solution.py:49
  196.1 4.0 %collective-permute-start.28 = (bf16[2,16,512]{2,1,0:T(8,128)(2,1)S(1)}, bf16[2,16,512]{2,1,0:T(8,128)(2,1)S(1)}, u32[]{:S(2)}, u32[]{:S(2)}) collective-permute-start(bf16[2,16,512]{2,1,0:T(8,128)(2,1)S(1)} %get-tuple-element.86), channel_id=1, source_target_pairs={{0,6},{1,7},{8,0},{9,1},{16,8},{17,9},{24,16},{25,17},{56,24},{57,... | collective-permute-start | bytes 98312 | tf_op jit(solution)/shard_map/ppermute | solution.py:49
  196.1 5.2 %collective-permute-start.27 = (bf16[2,16,512]{2,1,0:T(8,128)(2,1)S(1)}, bf16[2,16,512]{2,1,0:T(8,128)(2,1)S(1)}, u32[]{:S(2)}, u32[]{:S(2)}) collective-permute-start(bf16[2,16,512]{2,1,0:T(8,128)(2,1)S(1)} %get-tuple-element.86), channel_id=1, source_target_pairs={{0,8},{1,9},{8,16},{9,17},{16,24},{17,25},{24,56},{25,57},{56,48},... | collective-permute-start | bytes 98312 | tf_op jit(solution)/shard_map/ppermute | solution.py:49
  202.7 4.0 %collective-permute-start.30 = (bf16[2,16,512]{2,1,0:T(8,128)(2,1)S(1)}, bf16[2,16,512]{2,1,0:T(8,128)(2,1)S(1)}, u32[]{:S(2)}, u32[]{:S(2)}) collective-permute-start(bf16[2,16,512]{2,1,0:T(8,128)(2,1)S(1)} %get-tuple-element.89), channel_id=1, source_target_pairs={{0,6},{1,7},{8,0},{9,1},{16,8},{17,9},{24,16},{25,17},{56,24},{57,... | collective-permute-start | bytes 98312 | tf_op jit(solution)/shard_map/ppermute | solution.py:49
  202.7 5.2 %collective-permute-start.29 = (bf16[2,16,512]{2,1,0:T(8,128)(2,1)S(1)}, bf16[2,16,512]{2,1,0:T(8,128)(2,1)S(1)}, u32[]{:S(2)}, u32[]{:S(2)}) collective-permute-start(bf16[2,16,512]{2,1,0:T(8,128)(2,1)S(1)} %get-tuple-element.89), channel_id=1, source_target_pairs={{0,8},{1,9},{8,16},{9,17},{16,24},{17,25},{24,56},{25,57},{56,48},... | collective-permute-start | bytes 98312 | tf_op jit(solution)/shard_map/ppermute | solution.py:49
  209.3 4.0 %collective-permute-start.32 = (bf16[2,16,512]{2,1,0:T(8,128)(2,1)S(1)}, bf16[2,16,512]{2,1,0:T(8,128)(2,1)S(1)}, u32[]{:S(2)}, u32[]{:S(2)}) collective-permute-start(bf16[2,16,512]{2,1,0:T(8,128)(2,1)S(1)} %get-tuple-element.92), channel_id=1, source_target_pairs={{0,6},{1,7},{8,0},{9,1},{16,8},{17,9},{24,16},{25,17},{56,24},{57,... | collective-permute-start | bytes 98312 | tf_op jit(solution)/shard_map/ppermute | solution.py:49
  209.4 5.2 %collective-permute-start.31 = (bf16[2,16,512]{2,1,0:T(8,128)(2,1)S(1)}, bf16[2,16,512]{2,1,0:T(8,128)(2,1)S(1)}, u32[]{:S(2)}, u32[]{:S(2)}) collective-permute-start(bf16[2,16,512]{2,1,0:T(8,128)(2,1)S(1)} %get-tuple-element.92), channel_id=1, source_target_pairs={{0,8},{1,9},{8,16},{9,17},{16,24},{17,25},{24,56},{25,57},{56,48},... | collective-permute-start | bytes 98312 | tf_op jit(solution)/shard_map/ppermute | solution.py:49
  216.0 4.0 %collective-permute-start.34 = (bf16[2,16,512]{2,1,0:T(8,128)(2,1)S(1)}, bf16[2,16,512]{2,1,0:T(8,128)(2,1)S(1)}, u32[]{:S(2)}, u32[]{:S(2)}) collective-permute-start(bf16[2,16,512]{2,1,0:T(8,128)(2,1)S(1)} %get-tuple-element.95), channel_id=1, source_target_pairs={{0,6},{1,7},{8,0},{9,1},{16,8},{17,9},{24,16},{25,17},{56,24},{57,... | collective-permute-start | bytes 98312 | tf_op jit(solution)/shard_map/ppermute | solution.py:49
  216.0 5.2 %collective-permute-start.33 = (bf16[2,16,512]{2,1,0:T(8,128)(2,1)S(1)}, bf16[2,16,512]{2,1,0:T(8,128)(2,1)S(1)}, u32[]{:S(2)}, u32[]{:S(2)}) collective-permute-start(bf16[2,16,512]{2,1,0:T(8,128)(2,1)S(1)} %get-tuple-element.95), channel_id=1, source_target_pairs={{0,8},{1,9},{8,16},{9,17},{16,24},{17,25},{24,56},{25,57},{56,48},... | collective-permute-start | bytes 98312 | tf_op jit(solution)/shard_map/ppermute | solution.py:49
  223.3 9.1 %collective-permute-start.38 = (bf16[14,16,512]{2,1,0:T(8,128)(2,1)S(1)}, bf16[14,16,512]{2,1,0:T(8,128)(2,1)S(1)}, u32[]{:S(2)}, u32[]{:S(2)}) collective-permute-start(bf16[14,16,512]{2,1,0:T(8,128)(2,1)S(1)} %shard_map.102), channel_id=1, source_target_pairs={{0,1},{1,0},{8,9},{9,8},{16,17},{17,16},{24,25},{25,24},{56,57},{5... | collective-permute-start | bytes 688136 | tf_op jit(solution)/shard_map/ppermute | solution.py:49
  223.4 4.0 %collective-permute-start.36 = (bf16[2,16,512]{2,1,0:T(8,128)(2,1)S(1)}, bf16[2,16,512]{2,1,0:T(8,128)(2,1)S(1)}, u32[]{:S(2)}, u32[]{:S(2)}) collective-permute-start(bf16[2,16,512]{2,1,0:T(8,128)(2,1)S(1)} %get-tuple-element.98), channel_id=1, source_target_pairs={{0,6},{1,7},{8,0},{9,1},{16,8},{17,9},{24,16},{25,17},{56,24},{57,... | collective-permute-start | bytes 98312 | tf_op jit(solution)/shard_map/ppermute | solution.py:49
  223.5 5.2 %collective-permute-start.35 = (bf16[2,16,512]{2,1,0:T(8,128)(2,1)S(1)}, bf16[2,16,512]{2,1,0:T(8,128)(2,1)S(1)}, u32[]{:S(2)}, u32[]{:S(2)}) collective-permute-start(bf16[2,16,512]{2,1,0:T(8,128)(2,1)S(1)} %get-tuple-element.98), channel_id=1, source_target_pairs={{0,8},{1,9},{8,16},{9,17},{16,24},{17,25},{24,56},{25,57},{56,48},... | collective-permute-start | bytes 98312 | tf_op jit(solution)/shard_map/ppermute | solution.py:49
  231.1 1.3 collective-permute-start.37
  249.9 8.9 %collective-permute-start.43 = (bf16[8,32,512]{2,1,0:T(8,128)(2,1)S(1)}, bf16[8,32,512]{2,1,0:T(8,128)(2,1)S(1)}, u32[]{:S(2)}, u32[]{:S(2)}) collective-permute-start(bf16[8,32,512]{2,1,0:T(8,128)(2,1)S(1)} %get-tuple-element.103), channel_id=1, source_target_pairs={{0,1},{1,0},{8,9},{9,8},{16,17},{17,16},{24,25},{25,24},{56,57},{5... | collective-permute-start | bytes 786440 | tf_op jit(solution)/shard_map/ppermute | solution.py:49
  250.0 1.5 collective-permute-start.39
  251.5 3.7 %collective-permute-start.42 = (f32[32,32]{1,0:T(8,128)S(1)}, f32[32,32]{1,0:T(8,128)S(1)}, u32[]{:S(2)}, u32[]{:S(2)}) collective-permute-start(f32[32,32]{1,0:T(8,128)S(1)} %add.49.gram_0), channel_id=1, source_target_pairs={{0,6},{1,7},{2,0},{3,1},{4,2},{5,3},{6,4},{7,5},{8,14},{9,15},{10,... | collective-permute-start | bytes 12296 | tf_op jit(solution)/shard_map/ppermute | solution.py:49
  251.5 5.0 %collective-permute-start.41 = (f32[32,32]{1,0:T(8,128)S(1)}, f32[32,32]{1,0:T(8,128)S(1)}, u32[]{:S(2)}, u32[]{:S(2)}) collective-permute-start(f32[32,32]{1,0:T(8,128)S(1)} %add.49.gram_0), channel_id=1, source_target_pairs={{0,2},{1,3},{2,4},{3,5},{4,6},{5,7},{6,0},{7,1},{8,10},{9,11},{10,... | collective-permute-start | bytes 12296 | tf_op jit(solution)/shard_map/ppermute | solution.py:49
  253.5 5.2 %collective-permute-start.40 = (f32[32,32]{1,0:T(8,128)S(1)}, f32[32,32]{1,0:T(8,128)S(1)}, u32[]{:S(2)}, u32[]{:S(2)}) collective-permute-start(f32[32,32]{1,0:T(8,128)S(1)} %add.49.gram_0), channel_id=1, source_target_pairs={{0,4},{1,5},{2,6},{3,7},{4,0},{5,1},{6,2},{7,3},{8,12},{9,13},{10,... | collective-permute-start | bytes 12296 | tf_op jit(solution)/shard_map/ppermute | solution.py:49
  (2 other events, 6.5 us)
